TPU v7x, 256 devices: a whole 4x4x8 slice. The times are simulated.
256 devices in a mesh: sec: 32 (over x, z), tile: 8 (over y, core).
Axes of the slice: x: 4, y: 4, z: 8, core: 2. Of those that a mesh axis runs over, the one named last changes fastest.
Arguments:
- right_side: float32 [32, 8, 64, 128], P('sec', 'tile'), may hold values from -6 to 6
- anchor_diag: float32 [32, 8, 64, 128], P('sec', 'tile'), may hold values from 0.5 to 2
- intra_own: int32 [32, 8, 96], P('sec', 'tile'), may hold values from 0 to 63
- intra_far: int32 [32, 8, 96], P('sec', 'tile'), may hold values from 0 to 511
- intra_count: int32 [32, 8], P('sec', 'tile'), may hold values from 12 to 96, as said below
- inter_own: int32 [32, 8, 48], P('sec', 'tile'), may hold values from 0 to 63
- inter_prev: int32 [32, 8, 48], P('sec', 'tile'), may hold values from 0 to 63
- inter_count: int32 [32, 8], P('sec', 'tile'), may hold values from 6 to 48, as said below
- intra_stiff: bfloat16 [32, 8, 96, 128, 128], P('sec', 'tile'), as said below
- inter_stiff: bfloat16 [32, 8, 48, 128, 128], P('sec', 'tile'), as said below
Outputs:
- solution_field: float32 [32, 8, 64, 128], P('sec', 'tile')
- residual: float32 [32, 8, 64, 128], P('sec', 'tile')
Inputs may be any that keep to these rules, and one draw needn't show every extreme that they name: `intra_count`: slots at or beyond the count are ignored; some tile of some section uses all 96 slots. `inter_count`: slots at or beyond the count are ignored; some tile of some section uses all 48 slots. `intra_stiff`: every block is symmetric, and each diagonal entry exceeds the sum of magnitudes of the other entries of its row. `inter_stiff`: every block is symmetric, and each diagonal entry exceeds the sum of magnitudes of the other entries of its row.
All inputs are finite; a program needn't handle non-finite values.
Results may differ from a plain program's by a relative error of at most 0.04.
Values may be sent and summed in bfloat16 or wider, within the bound.
No kernel may reach another device: no remote copies, remote signals or barrier semaphores. Data moves between devices by JAX's collectives and lax.ppermute only.
A program may use at most 64 MiB of HBM per device.

v0:
```python
import jax
import jax.numpy as jnp
from jax import lax
from jax.sharding import PartitionSpec as P

ITERS = 3


def shifted(x, axis, by):
    peers = lax.axis_size(axis)
    pairs = [(i, i + by) for i in range(peers) if 0 <= i + by < peers]
    return lax.ppermute(x, axis, pairs)


def spread_rows(onehot, values):
    return jnp.einsum("skb,skn->sbn", onehot, values, precision=lax.Precision.HIGHEST)


def residual_norm(vector):
    return lax.psum(jnp.sum(vector * vector), ("sec", "tile"))


def per_device(
    right_side,
    anchor_diag,
    intra_own,
    intra_far,
    intra_count,
    inter_own,
    inter_prev,
    inter_count,
    intra_stiff,
    inter_stiff,
):
    n_sec, n_tile_one, n_blk, n_node = right_side.shape
    tiles = lax.axis_size("tile")
    slots_in = intra_own.shape[2]
    slots_ex = inter_own.shape[2]
    own_in = intra_own[:, 0]
    far_in = intra_far[:, 0]
    stiff_in = intra_stiff[:, 0]
    own_ex = inter_own[:, 0]
    prev_ex = inter_prev[:, 0]
    stiff_ex = inter_stiff[:, 0]
    live_in = (jnp.arange(slots_in)[None, :] < intra_count).astype(jnp.float32)
    live_ex = (jnp.arange(slots_ex)[None, :] < inter_count).astype(jnp.float32)
    blocks = jnp.arange(n_blk)
    own_hot = (own_in[:, :, None] == blocks).astype(jnp.float32)
    near_hot = (own_ex[:, :, None] == blocks).astype(jnp.float32)
    back_hot = (prev_ex[:, :, None] == blocks).astype(jnp.float32)
    target_hot = (far_in[:, :, None] == jnp.arange(tiles * n_blk)).astype(jnp.float32)
    solution_field = jnp.zeros_like(right_side)
    residual = right_side
    direction = right_side
    norm_now = residual_norm(residual)
    for step in range(ITERS):
        rounded = direction.astype(jnp.bfloat16)
        whole = lax.all_gather(rounded, "tile", axis=1, tiled=True).reshape(
            n_sec, tiles * n_blk, n_node
        )
        mine = rounded[:, 0]
        near = jnp.take_along_axis(mine, own_in[:, :, None], 1)
        far = jnp.take_along_axis(whole, far_in[:, :, None], 1)
        diff_in = (near.astype(jnp.float32) - far.astype(jnp.float32)).astype(jnp.bfloat16)
        u_in = (
            jnp.einsum("skij,skj->ski", stiff_in, diff_in, preferred_element_type=jnp.float32)
            * live_in[:, :, None]
        )
        local = spread_rows(own_hot, u_in)
        spread = spread_rows(target_hot, -u_in).reshape(n_sec, tiles, n_blk, n_node)
        local = (
            local
            + lax.psum_scatter(
                spread.astype(jnp.bfloat16), "tile", scatter_dimension=1, tiled=True
            ).astype(jnp.float32)[:, 0]
        )
        edge = shifted(mine, "sec", 1)
        before = jnp.concatenate([edge, mine[:-1]], 0)
        near_ex = jnp.take_along_axis(mine, own_ex[:, :, None], 1)
        back_ex = jnp.take_along_axis(before, prev_ex[:, :, None], 1)
        diff_ex = (near_ex.astype(jnp.float32) - back_ex.astype(jnp.float32)).astype(jnp.bfloat16)
        u_ex = (
            jnp.einsum("skij,skj->ski", stiff_ex, diff_ex, preferred_element_type=jnp.float32)
            * live_ex[:, :, None]
        )
        local = local + spread_rows(near_hot, u_ex)
        backward = -spread_rows(back_hot, u_ex)
        incoming = shifted(backward.astype(jnp.bfloat16), "sec", -1).astype(backward.dtype)
        local = local + jnp.concatenate([backward[1:], incoming], 0)
        image = anchor_diag * direction + local[:, None]
        alpha = norm_now / lax.psum(jnp.sum(direction * image), ("sec", "tile"))
        solution_field = solution_field + alpha * direction
        residual = residual - alpha * image
        norm_next = residual_norm(residual)
        direction = residual + norm_next / norm_now * direction
        norm_now = norm_next
    return (solution_field, residual)


def solution(mesh):
    return jax.shard_map(
        per_device,
        mesh=mesh,
        in_specs=(
            P("sec", "tile", None, None),
            P("sec", "tile", None, None),
            P("sec", "tile", None),
            P("sec", "tile", None),
            P("sec", "tile"),
            P("sec", "tile", None),
            P("sec", "tile", None),
            P("sec", "tile"),
            P("sec", "tile", None, None, None),
            P("sec", "tile", None, None, None),
        ),
        out_specs=(P("sec", "tile", None, None), P("sec", "tile", None, None)),
        check_vma=False,
    )
```

profile of v0, /device:TPU:32, one launch (start us, length us, event | category | flops | bytes accessed | tf_op | source)
XLA Modules:
  0.0 566.1 jit_solution(6081867425183190698)
XLA Ops:
  7.3 0.9 convert_bitcast_fusion.7
  8.2 3.9 collective-permute-start
  13.4 0.7 and_bitcast_fusion.2
  14.9 13.3 %all_gather.9 = bf16[1,8,64,128]{3,2,0,1:T(8,128)(2,1)S(1)} all-gather(bf16[1,1,64,128]{3,2,0,1:T(8,128)(2,1)S(1)} %get-tuple-element.19), channel_id=1, replica_groups=mesh['sec'=32,'tile'=8] {'tile'}, dimensions={1}, use_global_device_ids=true | all-gather | bytes 147456 | tf_op jit(solution)/shard_map/all_gather | solution.py:58
  28.8 0.7 gather_fusion.1
  29.6 1.7 fusion.4
  31.3 1.0 fusion.12
  34.5 2.3 fusion.10
  37.1 2.0 collective-permute-start.1
  39.2 27.2 %reduce-scatter.4.cloned.1.call-done = bf16[1,1,64,128]{3,2,1,0:T(8,128)(2,1)} async-done(((bf16[1,8,64,128]{3,2,1,0:T(8,128)(2,1)}), bf16[1,1,64,128]{3,2,1,0:T(8,128)(2,1)}) %reduce-scatter.4.cloned.1.call-update) | async-done | bytes 16400 | tf_op jit(solution)/shard_map/reduce_scatter | solution.py:73
  66.3 1.0 convolution_add_fusion.5
  67.4 1.0 multiply_reduce_fusion.4
  68.3 76.3 %all-reduce = (f32[]{:T(128)}, f32[]{:T(128)}) all-reduce(f32[]{:T(128)} %get-tuple-element.6, f32[]{:T(128)} %get-tuple-element.4), channel_id=1, replica_groups=mesh['sec'=32,'tile'=8] {'sec','tile'}, use_global_device_ids=true, to_apply=%region_1.0 | all-reduce | flops 2 | bytes 16 | tf_op jit(solution)/shard_map/psum | solution.py:20
  146.6 72.7 %psum.44 = f32[]{:T(128)} all-reduce(f32[]{:T(128)} %multiply_reduce_fusion.3), channel_id=1, replica_groups=mesh['sec'=32,'tile'=8] {'sec','tile'}, use_global_device_ids=true, to_apply=%region_6.0 | all-reduce | flops 1 | bytes 8 | tf_op jit(solution)/shard_map/psum | solution.py:20
  220.8 0.7 gather_fusion.4
  221.4 1.9 collective-permute-start.2
  223.4 12.8 %all_gather.10 = bf16[1,8,64,128]{3,2,0,1:T(8,128)(2,1)S(1)} all-gather(bf16[1,1,64,128]{3,2,0,1:T(8,128)(2,1)S(1)} %get-tuple-element.13), channel_id=1, replica_groups=mesh['sec'=32,'tile'=8] {'tile'}, dimensions={1}, use_global_device_ids=true | all-gather | bytes 147456 | tf_op jit(solution)/shard_map/all_gather | solution.py:58
  236.1 0.8 gather_fusion.5
  236.9 0.7 fusion.49
  237.6 1.7 fusion.2
  239.3 1.0 fusion.13
  240.4 0.7 gather_fusion.6
  241.2 0.7 gather_fusion.7
  242.0 2.3 fusion.8
  244.3 1.0 fusion.22
  245.3 3.9 collective-permute-start.3
  249.2 22.9 %reduce-scatter.6.cloned.1.call-done = bf16[1,1,64,128]{3,2,1,0:T(8,128)(2,1)} async-done(((bf16[1,8,64,128]{3,2,1,0:T(8,128)(2,1)}), bf16[1,1,64,128]{3,2,1,0:T(8,128)(2,1)}) %reduce-scatter.6.cloned.1.call-update) | async-done | bytes 16400 | tf_op jit(solution)/shard_map/reduce_scatter | solution.py:73
  272.1 1.0 convolution_add_fusion.3
  273.1 0.9 multiply_reduce_fusion.2
  274.0 76.0 %psum.45 = f32[]{:T(128)} all-reduce(f32[]{:T(128)} %get-tuple-element.23), channel_id=1, replica_groups=mesh['sec'=32,'tile'=8] {'sec','tile'}, use_global_device_ids=true, to_apply=%region_9.0 | all-reduce | flops 1 | bytes 8 | tf_op jit(solution)/shard_map/psum | solution.py:91
  351.9 72.9 %psum.46 = f32[]{:T(128)} all-reduce(f32[]{:T(128)} %get-tuple-element.11), channel_id=1, replica_groups=mesh['sec'=32,'tile'=8] {'sec','tile'}, use_global_device_ids=true, to_apply=%region_11.0 | all-reduce | flops 1 | bytes 8 | tf_op jit(solution)/shard_map/psum | solution.py:20
  426.1 0.8 gather_fusion.8
  426.9 1.9 collective-permute-start.4
  428.9 12.9 %all_gather.11 = bf16[1,8,64,128]{3,2,0,1:T(8,128)(2,1)S(1)} all-gather(bf16[1,1,64,128]{3,2,0,1:T(8,128)(2,1)S(1)} %get-tuple-element.9), channel_id=1, replica_groups=mesh['sec'=32,'tile'=8] {'tile'}, dimensions={1}, use_global_device_ids=true | all-gather | bytes 147456 | tf_op jit(solution)/shard_map/all_gather | solution.py:58
  441.8 0.8 gather_fusion.9
  442.6 0.7 fusion.50
  443.3 1.7 fusion
  445.0 1.6 fusion.14
  446.6 0.7 gather_fusion.10
  447.4 0.7 gather_fusion.11
  448.1 0.7 fusion.71
  448.9 2.3 fusion.6
  451.2 1.0 fusion.21
  452.2 3.9 collective-permute-start.5
  456.1 22.2 %reduce-scatter.8.cloned.1.call-done = bf16[1,1,64,128]{3,2,1,0:T(8,128)(2,1)} async-done(((bf16[1,8,64,128]{3,2,1,0:T(8,128)(2,1)}), bf16[1,1,64,128]{3,2,1,0:T(8,128)(2,1)}) %reduce-scatter.8.cloned.1.call-update) | async-done | bytes 16400 | tf_op jit(solution)/shard_map/reduce_scatter | solution.py:73
  478.4 1.0 convolution_add_fusion.1
  479.4 1.6 multiply_reduce_fusion
  481.0 76.0 %psum.47 = f32[]{:T(128)} all-reduce(f32[]{:T(128)} %get-tuple-element.25), channel_id=1, replica_groups=mesh['sec'=32,'tile'=8] {'sec','tile'}, use_global_device_ids=true, to_apply=%region_14.0 | all-reduce | flops 1 | bytes 8 | tf_op jit(solution)/shard_map/psum | solution.py:91
  (77 shorter events, 6.7 us)
Async XLA Ops:
  7.2 22.4 %copy-start = (bf16[1,1,96,128,128]{4,3,2,1,0:T(8,128)(2,1)S(1)}, bf16[1,1,96,128,128]{4,3,2,1,0:T(8,128)(2,1)}, u32[]{:S(2)}) copy-start(bf16[1,1,96,128,128]{4,3,2,1,0:T(8,128)(2,1)} %param.24) | copy-start | bytes 9437188
  7.2 24.1 %copy-start.3 = (s32[1,1,96]{2,1,0:T(1,128)S(1)}, s32[1,1,96]{2,1,0:T(1,128)}, u32[]{:S(2)}) copy-start(s32[1,1,96]{2,1,0:T(1,128)} %param.19) | copy-start | bytes 1156
  7.2 25.2 %copy-start.4 = (s32[1,1,48]{2,1,0:T(1,128)S(1)}, s32[1,1,48]{2,1,0:T(1,128)}, u32[]{:S(2)}) copy-start(s32[1,1,48]{2,1,0:T(1,128)} %param.21) | copy-start | bytes 580
  7.2 25.2 %copy-start.18 = (s32[1,1,48]{2,1,0:T(1,128)S(1)}, s32[1,1,48]{2,1,0:T(1,128)}, u32[]{:S(2)}) copy-start(s32[1,1,48]{2,1,0:T(1,128)} %param.22) | copy-start | bytes 580
  7.2 59.1 %reduce-scatter.4.cloned.1.call-start = ((), (), s32[]{:S(2)}) async-start(), calls=%async_computation.3 | async-start | bytes 147456 | tf_op jit(solution)/shard_map/reduce_scatter | solution.py:73
  8.2 25.6 %collective-permute-start = (bf16[1,64,128]{2,1,0:T(8,128)(2,1)S(1)}, bf16[1,64,128]{2,1,0:T(8,128)(2,1)S(1)}, u32[]{:S(2)}, u32[]{:S(2)}) collective-permute-start(bf16[1,64,128]{2,1,0:T(8,128)(2,1)S(1)} %get-tuple-element.21), channel_id=1, source_target_pairs={{0,8},{8,16},{16,24},{24,32},{32,40},{40,48},{48,56},{56,64},{64,7... | collective-permute-start | bytes 49160 | tf_op jit(solution)/shard_map/ppermute | solution.py:12
  14.1 206.6 %copy-start.5 = (pred[96]{0:T(512)(128)(4,1)}, pred[96]{0:T(512)(128)(4,1)S(1)}, u32[]{:S(2)}) copy-start(pred[96]{0:T(512)(128)(4,1)S(1)} %get-tuple-element.30) | copy-start | bytes 292
  14.8 51.5 %copy-start.14 = (f32[96]{0:T(128)}, f32[96]{0:T(128)S(1)}, u32[]{:S(2)}) copy-start(f32[96]{0:T(128)S(1)} %compare_convert_fusion.1) | copy-start | bytes 1156
  14.8 17.6 %copy-start.10 = (s32[1024]{0:T(1024)}, s32[1024]{0:T(1024)S(1)}, u32[]{:S(2)}) copy-start(s32[1024]{0:T(1024)S(1)} %pad_clamp_fusion.2) | copy-start | bytes 12292
  14.8 205.9 %copy-start.12 = (s32[1024]{0:T(1024)}, s32[1024]{0:T(1024)S(1)}, u32[]{:S(2)}) copy-start(s32[1024]{0:T(1024)S(1)} %pad_clamp_fusion.3) | copy-start | bytes 12292
  28.1 39.2 %copy-start.1 = (f32[1,1,64,128]{3,2,1,0:T(8,128)S(1)}, f32[1,1,64,128]{3,2,1,0:T(8,128)}, u32[]{:S(2)}) copy-start(f32[1,1,64,128]{3,2,1,0:T(8,128)} %param.16) | copy-start | bytes 98308
  28.1 39.3 %copy-start.2 = (f32[1,1,64,128]{3,2,1,0:T(8,128)S(1)}, f32[1,1,64,128]{3,2,1,0:T(8,128)}, u32[]{:S(2)}) copy-start(f32[1,1,64,128]{3,2,1,0:T(8,128)} %param.17) | copy-start | bytes 98308
  32.3 239.8 %reduce-scatter.6.cloned.1.call-start = ((), (), s32[]{:S(2)}) async-start(), calls=%async_computation.4 | async-start | bytes 147456 | tf_op jit(solution)/shard_map/reduce_scatter | solution.py:73
  32.5 188.2 %copy-start.6 = (pred[48]{0:T(512)(128)(4,1)}, pred[48]{0:T(512)(128)(4,1)S(1)}, u32[]{:S(2)}) copy-start(pred[48]{0:T(512)(128)(4,1)S(1)} %get-tuple-element.27) | copy-start | bytes 148
  32.5 188.2 %copy-start.8 = (pred[48]{0:T(512)(128)(4,1)}, pred[48]{0:T(512)(128)(4,1)S(1)}, u32[]{:S(2)}) copy-start(pred[48]{0:T(512)(128)(4,1)S(1)} %get-tuple-element.28) | copy-start | bytes 148
  33.1 187.6 %copy-start.11 = (s32[1024]{0:T(1024)}, s32[1024]{0:T(1024)S(1)}, u32[]{:S(2)}) copy-start(s32[1024]{0:T(1024)S(1)} %pad_clamp_fusion) | copy-start | bytes 12292
  33.2 1.3 copy-start.13
  33.2 202.9 %copy-start.16 = (f32[48]{0:T(128)}, f32[48]{0:T(128)S(1)}, u32[]{:S(2)}) copy-start(f32[48]{0:T(128)S(1)} %compare_convert_fusion) | copy-start | bytes 580
  37.1 30.2 %collective-permute-start.1 = (bf16[1,64,128]{2,1,0:T(8,128)(2,1)S(1)}, bf16[1,64,128]{2,1,0:T(8,128)(2,1)S(1)}, u32[]{:S(2)}, u32[]{:S(2)}) collective-permute-start(bf16[1,64,128]{2,1,0:T(8,128)(2,1)S(1)} %fusion.23), channel_id=1, source_target_pairs={{8,0},{16,8},{24,16},{32,24},{40,32},{48,40},{56,48},{64,56},{72,6... | collective-permute-start | bytes 49160 | tf_op jit(solution)/shard_map/ppermute | solution.py:12
  220.7 21.2 %copy-start.7 = (pred[48]{0:T(512)(128)(4,1)S(1)}, pred[48]{0:T(512)(128)(4,1)}, u32[]{:S(2)}) copy-start(pred[48]{0:T(512)(128)(4,1)} %copy-done.6) | copy-start | bytes 148
  220.7 21.2 %copy-start.9 = (pred[48]{0:T(512)(128)(4,1)S(1)}, pred[48]{0:T(512)(128)(4,1)}, u32[]{:S(2)}) copy-start(pred[48]{0:T(512)(128)(4,1)} %copy-done.8) | copy-start | bytes 148
  221.4 19.7 %collective-permute-start.2 = (bf16[1,64,128]{2,1,0:T(8,128)(2,1)S(1)}, bf16[1,64,128]{2,1,0:T(8,128)(2,1)S(1)}, u32[]{:S(2)}, u32[]{:S(2)}) collective-permute-start(bf16[1,64,128]{2,1,0:T(8,128)(2,1)S(1)} %get-tuple-element.18), channel_id=1, source_target_pairs={{0,8},{8,16},{16,24},{24,32},{32,40},{40,48},{48,56},{56,64},{64,7... | collective-permute-start | bytes 49160 | tf_op jit(solution)/shard_map/ppermute | solution.py:12
  236.9 2.4 copy-start.15
  236.9 7.4 %copy-start.17 = (f32[48]{0:T(128)S(1)}, f32[48]{0:T(128)}, u32[]{:S(2)}) copy-start(f32[48]{0:T(128)} %copy-done.16) | copy-start | bytes 580
  241.1 237.2 %reduce-scatter.8.cloned.1.call-start = ((), (), s32[]{:S(2)}) async-start(), calls=%async_computation.5 | async-start | bytes 147456 | tf_op jit(solution)/shard_map/reduce_scatter | solution.py:73
  245.3 27.8 %collective-permute-start.3 = (bf16[1,64,128]{2,1,0:T(8,128)(2,1)S(1)}, bf16[1,64,128]{2,1,0:T(8,128)(2,1)S(1)}, u32[]{:S(2)}, u32[]{:S(2)}) collective-permute-start(bf16[1,64,128]{2,1,0:T(8,128)(2,1)S(1)} %fusion.22), channel_id=1, source_target_pairs={{8,0},{16,8},{24,16},{32,24},{40,32},{48,40},{56,48},{64,56},{72,6... | collective-permute-start | bytes 49160 | tf_op jit(solution)/shard_map/ppermute | solution.py:12
  426.9 20.4 %collective-permute-start.4 = (bf16[1,64,128]{2,1,0:T(8,128)(2,1)S(1)}, bf16[1,64,128]{2,1,0:T(8,128)(2,1)S(1)}, u32[]{:S(2)}, u32[]{:S(2)}) collective-permute-start(bf16[1,64,128]{2,1,0:T(8,128)(2,1)S(1)} %get-tuple-element.16), channel_id=1, source_target_pairs={{0,8},{8,16},{16,24},{24,32},{32,40},{40,48},{48,56},{56,64},{64,7... | collective-permute-start | bytes 49160 | tf_op jit(solution)/shard_map/ppermute | solution.py:12
  452.2 27.2 %collective-permute-start.5 = (bf16[1,64,128]{2,1,0:T(8,128)(2,1)S(1)}, bf16[1,64,128]{2,1,0:T(8,128)(2,1)S(1)}, u32[]{:S(2)}, u32[]{:S(2)}) collective-permute-start(bf16[1,64,128]{2,1,0:T(8,128)(2,1)S(1)} %fusion.21), channel_id=1, source_target_pairs={{8,0},{16,8},{24,16},{32,24},{40,32},{48,40},{56,48},{64,56},{72,6... | collective-permute-start | bytes 49160 | tf_op jit(solution)/shard_map/ppermute | solution.py:12
Sparse Core Ops, SparseCore 0:
  32.5 33.8 reduce-scatter.3
  241.2 30.8 reduce-scatter.5
  447.5 30.8 reduce-scatter.7
where the time goes:
time: 569 us; the launch traced here: 566 us
  blocking collectives  413 us (73%)
  waiting for transfers between devices  72.3 us (13%)
  matrix products  24.5 us (4%)
  between operations  22 us (4%)
  starting transfers between devices  17.7 us (3%)
  local copies, waits for them, and re-layouts  8.68 us (2%)
  other arithmetic  7.92 us (1%)
    psum x3, blocking collectives, residual_norm(): return lax.psum(jnp.sum(vector * vector), ('sec', 'tile'))  222 us
    psum x2, blocking collectives, per_device(): alpha = norm_now / lax.psum(jnp.sum(direction * image), ('sec', 'tile'))  152 us
    reduce_scatter x3, waiting for transfers between devices, per_device(): lax.psum_scatter(spread.astype(jnp.bfloat16), 'tile', scatter_dimension=1...  72.2 us
    all_gather x3, blocking collectives, per_device(): lax.all_gather(rounded, 'tile', axis=1, tiled=True)  39 us
    ppermute x6, starting transfers between devices, shifted(): return lax.ppermute(x, axis, pairs)  17.6 us
    dot_general x12, matrix products, spread_rows(): jnp.einsum('skb,skn->sbn', onehot, values, precision=lax.Precision.HIGHEST)  12.5 us
  transfers between devices with their start and end apart: 9, of which 3 were waited for; matrix products, arithmetic and copies ran while one was open for 6% of the time, Pallas kernels for 0%

commit v1 on v0

v1 whole, which is shorter than its diff:
```python
import functools

import jax
import jax.numpy as jnp
from jax import lax
from jax.experimental import pallas as pl
from jax.experimental.pallas import tpu as pltpu
from jax.sharding import PartitionSpec as P

ITERS = 3
F32, BF16 = jnp.float32, jnp.bfloat16
VMEM = pl.BlockSpec(memory_space=pltpu.VMEM)
CONTRACT_ROWS = (((0,), (0,)), ((), ()))
GROUP = 8


def split(x):
    high = x.astype(BF16)
    return jnp.concatenate([high, (x - high.astype(F32)).astype(BF16)], 1)


def fold(x):
    half = x.shape[1] // 2
    return x[:, :half] + x[:, half:]


def springs(hot, field, stiff_ref, u_ref):
    slots, node = u_ref.shape
    diff = fold(lax.dot_general(hot, split(field), CONTRACT_ROWS, preferred_element_type=F32))
    rows = lax.broadcasted_iota(jnp.int32, (2 * GROUP, GROUP * node), 0) % GROUP
    cols = lax.broadcasted_iota(jnp.int32, (2 * GROUP, GROUP * node), 1) // node
    own = rows == cols
    for start in range(0, slots, GROUP):
        part = diff[start : start + GROUP]
        high = part.astype(BF16).astype(F32)
        both = jnp.concatenate([high, part - high], 0)
        wide = jnp.where(own, jnp.concatenate([both] * GROUP, 1), 0.0).astype(BF16)
        block = stiff_ref[start : start + GROUP].reshape(GROUP * node, node)
        got = jnp.dot(wide, block, preferred_element_type=F32)
        u_ref[start : start + GROUP, :] = got[:GROUP] + got[GROUP:]
    u = u_ref[...]
    spread = fold(jnp.dot(hot, split(u), preferred_element_type=F32))
    return spread, jnp.sum(diff * u, axis=0, keepdims=True)


def one_hot(near, far, count, blocks):
    slots = near.shape[1]
    live = lax.broadcasted_iota(jnp.int32, (1, slots), 1) < count
    place = lax.broadcasted_iota(jnp.int32, (blocks, slots), 0)
    plus = jnp.where(live & (place == near), 1.0, 0.0)
    minus = jnp.where(live & (place == far), 1.0, 0.0)
    return (plus - minus).astype(BF16)


def intra_kernel(tile, *refs):
    own_ref, far_ref, count_ref, stiff_ref = refs[:4]
    fields = refs[4:12]
    mine_ref, other_ref, energy_ref, u_ref = refs[12:]
    blk = fields[0].shape[0]
    me = tile[0]
    far = far_ref[0]
    far_tile, far_blk = far // blk, far % blk
    there = me ^ far_tile
    place = ((there % 2) * 4 + there // 2) * blk + far_blk
    hot = one_hot(own_ref[0], place, count_ref[0, 0], 8 * blk)
    field = jnp.concatenate([f[...] for f in fields], 0)
    spread, energy = springs(hot, field, stiff_ref.at[0, 0], u_ref)
    mine_ref[...] = spread[: 4 * blk]
    other_ref[...] = spread[4 * blk :]
    energy_ref[...] = energy


def inter_kernel(own_ref, prev_ref, count_ref, stiff_ref, mine_ref, before_ref, near_ref, back_ref, energy_ref, u_ref):
    blk = mine_ref.shape[0]
    hot = one_hot(own_ref[0], prev_ref[0] + blk, count_ref[0, 0], 2 * blk)
    field = jnp.concatenate([mine_ref[...], before_ref[...]], 0)
    spread, energy = springs(hot, field, stiff_ref.at[0, 0], u_ref)
    near_ref[...] = spread[:blk]
    back_ref[...] = spread[blk:]
    energy_ref[...] = energy


def pair_kernel(mine_ref, got_ref, *outs):
    blk = outs[0].shape[0]
    for j, out in enumerate(outs):
        out[...] = mine_ref[j * blk : (j + 1) * blk] + got_ref[j * blk : (j + 1) * blk]


def image_of(anchor_ref, v_ref, parts):
    total = anchor_ref[...] * v_ref[...]
    for part in parts:
        total = total + part[...]
    return total


def sum_kernel(anchor_ref, v_ref, *refs):
    *parts, out_ref = refs
    out_ref[...] = image_of(anchor_ref, v_ref, parts)


def lane(x, index):
    total = jnp.sum(jnp.sum(x, axis=0, keepdims=True), axis=1, keepdims=True)
    return jnp.where(lax.broadcasted_iota(jnp.int32, (1, 128), 1) == index, total, 0.0)


def moment_kernel(anchor_ref, v0, v1, v2, e1, e2, e3, f1, f2, f3, out_ref):
    row = jnp.zeros((1, 128), F32)
    for k, (v, e, f) in enumerate(((v0, e1, f1), (v1, e2, f2), (v2, e3, f3))):
        square = v[...] * v[...]
        row = row + lane(square, 2 * k)
        row = row + lane(jnp.sum(anchor_ref[...] * square, axis=0, keepdims=True) + e[...] + f[...], 2 * k + 1)
    out_ref[...] = jnp.broadcast_to(row, out_ref.shape)


def quadratic(coef, moments, shift):
    total = 0.0
    for i, a in enumerate(coef):
        for j, b in enumerate(coef):
            total = total + a * b * moments[i + j + shift]
    return total


def final_kernel(sums_ref, *refs):
    *vs, x_ref, r_ref = refs
    row = jnp.sum(sums_ref[...], axis=0, keepdims=True)
    lanes = lax.broadcasted_iota(jnp.int32, row.shape, 1)
    raw = [jnp.sum(jnp.where(lanes == j, row, 0.0), axis=1, keepdims=True) for j in range(2 * ITERS)]
    sigma = raw[1] / raw[0]
    inverse = 1.0 / sigma
    moments, scale = [], 1.0 / raw[0]
    for m in raw:
        moments.append(m * scale)
        scale = scale * inverse
    zero, one = jnp.zeros_like(sigma), jnp.ones_like(sigma)
    r, p, x = [one], [one], [zero]
    rr = one
    for step in range(ITERS):
        alpha = rr / quadratic(p, moments, 1)
        x = [a + alpha * b for a, b in zip(x + [zero] * (len(p) - len(x)), p)]
        q = [zero] + p
        r = [a - alpha * b for a, b in zip(r + [zero], q)]
        if step < ITERS - 1:
            new = quadratic(r, moments, 0)
            p = [a + (new / rr) * b for a, b in zip(r, p + [zero])]
            rr = new
    power = one
    x_sum, r_sum = 0.0, 0.0
    for k in range(ITERS + 1):
        v = vs[k][...]
        r_sum = r_sum + (r[k] * power) * v
        power = power * inverse
        if k < ITERS:
            x_sum = x_sum + (x[k] * power) * v
    x_ref[...] = x_sum
    r_ref[...] = r_sum


def call(kernel, outs, *args, scratch=(), scalars=0):
    specs = [pl.BlockSpec(memory_space=pltpu.SMEM)] * scalars + [VMEM] * (len(args) - scalars)
    return pl.pallas_call(
        kernel,
        out_shape=[jax.ShapeDtypeStruct(o, F32) for o in outs],
        in_specs=specs,
        out_specs=[VMEM] * len(outs),
        scratch_shapes=[pltpu.VMEM(s, F32) for s in scratch],
        compiler_params=pltpu.CompilerParams(vmem_limit_bytes=16 * 2**20),
    )(*args)


def swap(x, by):
    return lax.ppermute(x, "tile", [(i, i ^ by) for i in range(lax.axis_size("tile"))])


def shifted(x, by):
    peers = lax.axis_size("sec")
    return lax.ppermute(x, "sec", [(i, i + by) for i in range(peers) if 0 <= i + by < peers])


def per_device(
    right_side,
    anchor_diag,
    intra_own,
    intra_far,
    intra_count,
    inter_own,
    inter_prev,
    inter_count,
    intra_stiff,
    inter_stiff,
):
    blk, node = right_side.shape[2:]
    anchor = anchor_diag[0, 0]
    tile = lax.axis_index("tile").astype(jnp.int32).reshape(1)
    field, row = (blk, node), (1, node)
    vs, energies, energies_ex = [right_side[0, 0]], [], []
    for step in range(ITERS):
        v = vs[-1]
        before = shifted(v, 1)
        here = [v] + [swap(v, 2 * j) for j in (1, 2, 3)]
        there = [swap(h, 1) for h in here]
        near, back, energy_ex = call(
            inter_kernel, (field, field, row), inter_own, inter_prev, inter_count, inter_stiff, v, before,
            scratch=((inter_own.shape[2], node),),
        )
        incoming = shifted(back, -1)
        mine, other, energy = call(
            intra_kernel, ((4 * blk, node), (4 * blk, node), row),
            tile, intra_own, intra_far, intra_count, intra_stiff, *here, *there,
            scratch=((intra_own.shape[2], node),), scalars=1,
        )
        energies.append(energy)
        energies_ex.append(energy_ex)
        if step == ITERS - 1:
            (moments,) = call(moment_kernel, ((8, node),), anchor, *vs, *energies, *energies_ex)
            mine = jnp.concatenate([mine.reshape(4, blk, node), jnp.broadcast_to(moments, (4, 8, node))], 1).reshape(-1, node)
            other = jnp.concatenate([other.reshape(4, blk, node), jnp.broadcast_to(moments, (4, 8, node))], 1).reshape(-1, node)
            got = swap(other, 1)
            parts = call(pair_kernel, ((blk + 8, node),) * 4, mine, got)
            parts = [parts[0]] + [swap(parts[j], 2 * j) for j in (1, 2, 3)]
            sums = (parts[0][blk:] + parts[1][blk:]) + (parts[2][blk:] + parts[3][blk:])
            parts = [p[:blk] for p in parts]
        else:
            got = swap(other, 1)
            parts = call(pair_kernel, (field,) * 4, mine, got)
            parts = [parts[0]] + [swap(parts[j], 2 * j) for j in (1, 2, 3)]
        (nxt,) = call(sum_kernel, (field,), anchor, v, *parts, near, incoming)
        vs.append(nxt)
    sections = lax.axis_size("sec")
    sums = lax.all_to_all(jnp.broadcast_to(sums[:1], (sections, node)), "sec", 0, 0, tiled=True)
    x, r = call(final_kernel, (field, field), sums, *vs)
    return x[None, None], r[None, None]


def solution(mesh):
    return jax.shard_map(
        per_device,
        mesh=mesh,
        in_specs=(
            P("sec", "tile", None, None),
            P("sec", "tile", None, None),
            P("sec", "tile", None),
            P("sec", "tile", None),
            P("sec", "tile"),
            P("sec", "tile", None),
            P("sec", "tile", None),
            P("sec", "tile"),
            P("sec", "tile", None, None, None),
            P("sec", "tile", None, None, None),
        ),
        out_specs=(P("sec", "tile", None, None), P("sec", "tile", None, None)),
        check_vma=False,
    )
```

time: 569 us -> 109 us (0.19)
  blocking collectives: 413 us -> 0 us
  starting transfers between devices: 17.7 us -> 62.7 us
  waiting for transfers between devices: 72.3 us -> 30.6 us
  matrix products: 24.5 us -> 0 us
  between operations: 22 us -> 2.29 us
  other arithmetic: 7.92 us -> 0.03 us
  Pallas kernels: 0 us -> 6.07 us
    psum x5 -> x0, blocking collectives: 374 us -> none  [the longest x3 222 us: residual_norm(): return lax.psum(jnp.sum(vector * vector), ('sec', 'tile'))]
    reduce_scatter x3 -> x0, waiting for transfers between devices: 72.2 us -> none  [per_device(): lax.psum_scatter(spread.astype(jnp.bfloat16), 'tile', scatter_dimension=1...]
    all_gather x3 -> x0, blocking collectives: 39 us -> none  [per_device(): lax.all_gather(rounded, 'tile', axis=1, tiled=True)]
    ppermute x6 -> x39, starting transfers between devices: 17.6 us -> 47.9 us  [the longest x33 30.2 us: swap(): lax.ppermute(x, 'tile', [(i, i ^ by) for i in range(lax.axis_size('tile'))])]
    dot_general x18 -> x0, matrix products: 24.5 us -> none  [the longest x12 12.5 us: spread_rows(): jnp.einsum('skb,skn->sbn', onehot, values, precision=lax.Precision.HIGHEST)]
    ppermute x6 -> x39, waiting for transfers between devices: 0.02 us -> 22.2 us  [the longest x33 18.5 us: swap(): lax.ppermute(x, 'tile', [(i, i ^ by) for i in range(lax.axis_size('tile'))])]
    all_to_all x0 -> x1, starting transfers between devices: none -> 14.8 us  [per_device(): lax.all_to_all(jnp.broadcast_to(sums[:1], (sections, node)), 'sec', 0, 0,...]
    gather x12 -> x0, local copies, waits for them, and re-layouts: 8.59 us -> none  [the longest x3 2.27 us: per_device(): far = jnp.take_along_axis(whole, far_in[:, :, None], 1)]
  transfers between devices with their start and end apart: 9 -> 40, of which waited for: 3 -> 17; matrix products, arithmetic and copies ran while one was open for 6% -> 1% of each run, Pallas kernels for 0% -> 2%
where the time goes in v1:
time: 109 us; the launch traced here: 108 us
  starting transfers between devices  62.7 us (58%)
  waiting for transfers between devices  30.6 us (28%)
  Pallas kernels  6.07 us (6%)
  local copies, waits for them, and re-layouts  6.04 us (6%)
  between operations  2.29 us (2%)
    ppermute x33, starting transfers between devices, swap(): lax.ppermute(x, 'tile', [(i, i ^ by) for i in range(lax.axis_size('tile'))])  30.2 us
    ppermute x33, waiting for transfers between devices, swap(): lax.ppermute(x, 'tile', [(i, i ^ by) for i in range(lax.axis_size('tile'))])  18.5 us
    ppermute x6, starting transfers between devices, shifted(): lax.ppermute(x, 'sec', [(i, i + by) for i in range(peers) if 0 <= i + by...  17.7 us
    all_to_all x1, starting transfers between devices, per_device(): lax.all_to_all(jnp.broadcast_to(sums[:1], (sections, node)), 'sec', 0, 0,...  14.8 us
    all_to_all x1, waiting for transfers between devices, per_device(): lax.all_to_all(jnp.broadcast_to(sums[:1], (sections, node)), 'sec', 0, 0,...  8.45 us
    pallas_call x14, Pallas kernels, call(): pl.pallas_call(kernel, out_shape=[jax.ShapeDtypeStruct(o, F32) for o in o...  6.07 us
    unnamed x26, local copies, waits for them, and re-layouts  5.4 us
    ppermute x6, waiting for transfers between devices, shifted(): lax.ppermute(x, 'sec', [(i, i + by) for i in range(peers) if 0 <= i + by...  3.67 us
  transfers between devices with their start and end apart: 40, of which 17 were waited for; matrix products, arithmetic and copies ran while one was open for 1% of the time, Pallas kernels for 2%

profile of v1, /device:TPU:32, one launch (start us, length us, event | category | flops | bytes accessed | tf_op | source)
XLA Modules:
  0.0 107.8 jit_solution(17973117545669170976)
XLA Ops:
  0.7 3.1 %collective-permute-start.2 = (f32[64,128]{1,0:T(8,128)}, f32[64,128]{1,0:T(8,128)S(1)}, u32[]{:S(2)}, u32[]{:S(2)}) collective-permute-start(f32[64,128]{1,0:T(8,128)} %bitcast.12), channel_id=1, source_target_pairs={{0,6},{1,7},{2,4},{3,5},{4,2},{5,3},{6,0},{7,1},{8,14},{9,15},{10,... | collective-permute-start | bytes 98312 | tf_op jit(solution)/shard_map/ppermute | solution.py:171
  3.8 0.6 collective-permute-start.1
  4.9 1.2 %collective-permute-done.2.refs_7_ = f32[64,128]{1,0:T(8,128)S(1)} collective-permute-done((f32[64,128]{1,0:T(8,128)}, f32[64,128]{1,0:T(8,128)S(1)}, u32[]{:S(2)}, u32[]{:S(2)}) %collective-permute-start.2) | collective-permute-done | bytes 32800 | tf_op jit(solution)/shard_map/ppermute | solution.py:171
  6.1 3.3 %collective-permute-done.1.refs_6_ = f32[64,128]{1,0:T(8,128)S(1)} collective-permute-done((f32[64,128]{1,0:T(8,128)}, f32[64,128]{1,0:T(8,128)S(1)}, u32[]{:S(2)}, u32[]{:S(2)}) %collective-permute-start.1) | collective-permute-done | bytes 32800 | tf_op jit(solution)/shard_map/ppermute | solution.py:171
  9.4 0.5 collective-permute-start.4
  10.8 1.9 %copy-done = bf16[1,1,96,128,128]{4,3,2,1,0:T(8,128)(2,1)S(1)} copy-done((bf16[1,1,96,128,128]{4,3,2,1,0:T(8,128)(2,1)S(1)}, bf16[1,1,96,128,128]{4,3,2,1,0:T(8,128)(2,1)}, u32[]{:S(2)}) %copy-start) | copy-done | bytes 3145752
  12.7 0.8 copy-done.4
  13.4 0.7 copy-done.9
  14.1 0.7 copy-done.11
  14.7 1.0 shard_map.113
  16.2 3.8 %collective-permute-start.11 = (f32[64,128]{1,0:T(8,128)S(1)}, f32[64,128]{1,0:T(8,128)S(1)}, u32[]{:S(2)}, u32[]{:S(2)}) collective-permute-start(f32[64,128]{1,0:T(8,128)S(1)} %bitcast.17), channel_id=1, source_target_pairs={{0,8},{8,16},{16,24},{24,32},{32,40},{40,48},{48,56},{56,64},{64,7... | collective-permute-start | bytes 98312 | tf_op jit(solution)/shard_map/ppermute | solution.py:176
  20.7 1.3 %collective-permute-done.11.before_ref = f32[64,128]{1,0:T(8,128)S(1)} collective-permute-done((f32[64,128]{1,0:T(8,128)S(1)}, f32[64,128]{1,0:T(8,128)S(1)}, u32[]{:S(2)}, u32[]{:S(2)}) %collective-permute-start.11) | collective-permute-done | bytes 32800 | tf_op jit(solution)/shard_map/ppermute | solution.py:176
  22.0 1.4 %copy-done.2 = bf16[1,1,48,128,128]{4,3,2,1,0:T(8,128)(2,1)S(1)} copy-done((bf16[1,1,48,128,128]{4,3,2,1,0:T(8,128)(2,1)S(1)}, bf16[1,1,48,128,128]{4,3,2,1,0:T(8,128)(2,1)}, u32[]{:S(2)}) %copy-start.2) | copy-done | bytes 1572888
  23.4 0.7 shard_map.115
  24.1 1.9 %collective-permute-start.12 = (f32[64,128]{1,0:T(8,128)S(1)}, f32[64,128]{1,0:T(8,128)S(1)}, u32[]{:S(2)}, u32[]{:S(2)}) collective-permute-start(f32[64,128]{1,0:T(8,128)S(1)} %get-tuple-element.41), channel_id=1, source_target_pairs={{8,0},{16,8},{24,16},{32,24},{40,32},{48,40},{56,48},{64,56},{72,6... | collective-permute-start | bytes 98312 | tf_op jit(solution)/shard_map/ppermute | solution.py:176
  26.3 2.3 %collective-permute-start.9 = (f32[64,128]{1,0:T(8,128)S(1)}, f32[64,128]{1,0:T(8,128)S(1)}, u32[]{:S(2)}, u32[]{:S(2)}) collective-permute-start(f32[64,128]{1,0:T(8,128)S(1)} %get-tuple-element.38), channel_id=1, source_target_pairs={{0,4},{1,5},{2,6},{3,7},{4,0},{5,1},{6,2},{7,3},{8,12},{9,13},{10,... | collective-permute-start | bytes 98312 | tf_op jit(solution)/shard_map/ppermute | solution.py:171
  28.6 2.3 %collective-permute-start.10 = (f32[64,128]{1,0:T(8,128)S(1)}, f32[64,128]{1,0:T(8,128)S(1)}, u32[]{:S(2)}, u32[]{:S(2)}) collective-permute-start(f32[64,128]{1,0:T(8,128)S(1)} %get-tuple-element.39), channel_id=1, source_target_pairs={{0,6},{1,7},{2,4},{3,5},{4,2},{5,3},{6,0},{7,1},{8,14},{9,15},{10,... | collective-permute-start | bytes 98312 | tf_op jit(solution)/shard_map/ppermute | solution.py:171
  30.8 0.9 collective-permute-done.9.refs_2_
  31.7 2.0 %collective-permute-done.10.refs_3_ = f32[64,128]{1,0:T(8,128)S(1)} collective-permute-done((f32[64,128]{1,0:T(8,128)S(1)}, f32[64,128]{1,0:T(8,128)S(1)}, u32[]{:S(2)}, u32[]{:S(2)}) %collective-permute-start.10) | collective-permute-done | bytes 32800 | tf_op jit(solution)/shard_map/ppermute | solution.py:171
  33.7 2.4 %collective-permute-start.15 = (f32[64,128]{1,0:T(8,128)S(1)}, f32[64,128]{1,0:T(8,128)S(1)}, u32[]{:S(2)}, u32[]{:S(2)}) collective-permute-start(f32[64,128]{1,0:T(8,128)S(1)} %shard_map.116.refs_4_.mine_ref.v_ref.v1.refs_1_), channel_id=1, source_target_pairs={{0,6},{1,7},{2,4},{3,5},{4,2},{5,3},{6,0},{7,1},{8,14},{9,15},{10,... | collective-permute-start | bytes 98312 | tf_op jit(solution)/shard_map/ppermute | solution.py:171
  36.1 1.8 %collective-permute-start.13 = (f32[64,128]{1,0:T(8,128)S(1)}, f32[64,128]{1,0:T(8,128)S(1)}, u32[]{:S(2)}, u32[]{:S(2)}) collective-permute-start(f32[64,128]{1,0:T(8,128)S(1)} %shard_map.116.refs_4_.mine_ref.v_ref.v1.refs_1_), channel_id=1, source_target_pairs={{0,2},{1,3},{2,0},{3,1},{4,6},{5,7},{6,4},{7,5},{8,10},{9,11},{10,... | collective-permute-start | bytes 98312 | tf_op jit(solution)/shard_map/ppermute | solution.py:171
  37.9 1.0 collective-permute-done.15.refs_7_
  38.9 2.6 %collective-permute-done.14.refs_6_ = f32[64,128]{1,0:T(8,128)S(1)} collective-permute-done((f32[64,128]{1,0:T(8,128)S(1)}, f32[64,128]{1,0:T(8,128)S(1)}, u32[]{:S(2)}, u32[]{:S(2)}) %collective-permute-start.14) | collective-permute-done | bytes 32800 | tf_op jit(solution)/shard_map/ppermute | solution.py:171
  42.0 0.7 collective-permute-done.18.refs_10_
  42.9 1.0 shard_map.117
  43.9 0.6 collective-permute-start.20
  44.5 3.9 %collective-permute-start.24 = (f32[64,128]{1,0:T(8,128)S(1)}, f32[64,128]{1,0:T(8,128)S(1)}, u32[]{:S(2)}, u32[]{:S(2)}) collective-permute-start(f32[64,128]{1,0:T(8,128)S(1)} %shard_map.116.refs_4_.mine_ref.v_ref.v1.refs_1_), channel_id=1, source_target_pairs={{0,8},{8,16},{16,24},{24,32},{32,40},{40,48},{48,56},{56,64},{64,7... | collective-permute-start | bytes 98312 | tf_op jit(solution)/shard_map/ppermute | solution.py:176
  48.5 1.9 %collective-permute-done.24.before_ref = f32[64,128]{1,0:T(8,128)S(1)} collective-permute-done((f32[64,128]{1,0:T(8,128)S(1)}, f32[64,128]{1,0:T(8,128)S(1)}, u32[]{:S(2)}, u32[]{:S(2)}) %collective-permute-start.24) | collective-permute-done | bytes 32800 | tf_op jit(solution)/shard_map/ppermute | solution.py:176
  50.3 0.7 shard_map.119
  51.0 1.9 %collective-permute-start.25 = (f32[64,128]{1,0:T(8,128)S(1)}, f32[64,128]{1,0:T(8,128)S(1)}, u32[]{:S(2)}, u32[]{:S(2)}) collective-permute-start(f32[64,128]{1,0:T(8,128)S(1)} %get-tuple-element.49), channel_id=1, source_target_pairs={{8,0},{16,8},{24,16},{32,24},{40,32},{48,40},{56,48},{64,56},{72,6... | collective-permute-start | bytes 98312 | tf_op jit(solution)/shard_map/ppermute | solution.py:176
  53.1 2.4 %collective-permute-start.22 = (f32[64,128]{1,0:T(8,128)S(1)}, f32[64,128]{1,0:T(8,128)S(1)}, u32[]{:S(2)}, u32[]{:S(2)}) collective-permute-start(f32[64,128]{1,0:T(8,128)S(1)} %get-tuple-element.46), channel_id=1, source_target_pairs={{0,4},{1,5},{2,6},{3,7},{4,0},{5,1},{6,2},{7,3},{8,12},{9,13},{10,... | collective-permute-start | bytes 98312 | tf_op jit(solution)/shard_map/ppermute | solution.py:171
  55.5 2.3 %collective-permute-start.23 = (f32[64,128]{1,0:T(8,128)S(1)}, f32[64,128]{1,0:T(8,128)S(1)}, u32[]{:S(2)}, u32[]{:S(2)}) collective-permute-start(f32[64,128]{1,0:T(8,128)S(1)} %get-tuple-element.47), channel_id=1, source_target_pairs={{0,6},{1,7},{2,4},{3,5},{4,2},{5,3},{6,0},{7,1},{8,14},{9,15},{10,... | collective-permute-start | bytes 98312 | tf_op jit(solution)/shard_map/ppermute | solution.py:171
  57.8 0.8 collective-permute-done.22.refs_2_
  58.6 2.0 %collective-permute-done.23.refs_3_ = f32[64,128]{1,0:T(8,128)S(1)} collective-permute-done((f32[64,128]{1,0:T(8,128)S(1)}, f32[64,128]{1,0:T(8,128)S(1)}, u32[]{:S(2)}, u32[]{:S(2)}) %collective-permute-start.23) | collective-permute-done | bytes 32800 | tf_op jit(solution)/shard_map/ppermute | solution.py:171
  60.6 2.4 %collective-permute-start.28 = (f32[64,128]{1,0:T(8,128)S(1)}, f32[64,128]{1,0:T(8,128)S(1)}, u32[]{:S(2)}, u32[]{:S(2)}) collective-permute-start(f32[64,128]{1,0:T(8,128)S(1)} %shard_map.120.refs_4_.mine_ref.v2.v_ref.refs_2_), channel_id=1, source_target_pairs={{0,6},{1,7},{2,4},{3,5},{4,2},{5,3},{6,0},{7,1},{8,14},{9,15},{10,... | collective-permute-start | bytes 98312 | tf_op jit(solution)/shard_map/ppermute | solution.py:171
  63.0 1.8 %collective-permute-start.26 = (f32[64,128]{1,0:T(8,128)S(1)}, f32[64,128]{1,0:T(8,128)S(1)}, u32[]{:S(2)}, u32[]{:S(2)}) collective-permute-start(f32[64,128]{1,0:T(8,128)S(1)} %shard_map.120.refs_4_.mine_ref.v2.v_ref.refs_2_), channel_id=1, source_target_pairs={{0,2},{1,3},{2,0},{3,1},{4,6},{5,7},{6,4},{7,5},{8,10},{9,11},{10,... | collective-permute-start | bytes 98312 | tf_op jit(solution)/shard_map/ppermute | solution.py:171
  64.8 4.2 %collective-permute-start.33 = (f32[64,128]{1,0:T(8,128)S(1)}, f32[64,128]{1,0:T(8,128)S(1)}, u32[]{:S(2)}, u32[]{:S(2)}) collective-permute-start(f32[64,128]{1,0:T(8,128)S(1)} %shard_map.120.refs_4_.mine_ref.v2.v_ref.refs_2_), channel_id=1, source_target_pairs={{0,8},{8,16},{16,24},{24,32},{32,40},{40,48},{48,56},{56,64},{64,7... | collective-permute-start | bytes 98312 | tf_op jit(solution)/shard_map/ppermute | solution.py:176
  70.6 0.7 shard_map.122
  71.3 1.0 shard_map.121
  72.6 1.3 %collective-permute-done.34.got_ref = f32[288,128]{1,0:T(8,128)S(1)} collective-permute-done((f32[288,128]{1,0:T(8,128)S(1)}, f32[288,128]{1,0:T(8,128)S(1)}, u32[]{:S(2)}, u32[]{:S(2)}) %collective-permute-start.34) | collective-permute-done | bytes 147488 | tf_op jit(solution)/shard_map/ppermute | solution.py:171
  74.3 3.5 %collective-permute-start.36 = (f32[72,128]{1,0:T(8,128)S(1)}, f32[72,128]{1,0:T(8,128)S(1)}, u32[]{:S(2)}, u32[]{:S(2)}) collective-permute-start(f32[72,128]{1,0:T(8,128)S(1)} %get-tuple-element.60), channel_id=1, source_target_pairs={{0,4},{1,5},{2,6},{3,7},{4,0},{5,1},{6,2},{7,3},{8,12},{9,13},{10,... | collective-permute-start | bytes 110600 | tf_op jit(solution)/shard_map/ppermute | solution.py:171
  77.8 1.0 collective-permute-start.37
  78.8 1.9 %collective-permute-start.38 = (f32[64,128]{1,0:T(8,128)S(1)}, f32[64,128]{1,0:T(8,128)S(1)}, u32[]{:S(2)}, u32[]{:S(2)}) collective-permute-start(f32[64,128]{1,0:T(8,128)S(1)} %get-tuple-element.63), channel_id=1, source_target_pairs={{8,0},{16,8},{24,16},{32,24},{40,32},{48,40},{56,48},{64,56},{72,6... | collective-permute-start | bytes 98312 | tf_op jit(solution)/shard_map/ppermute | solution.py:176
  80.7 2.3 %collective-permute-done.37 = f32[72,128]{1,0:T(8,128)S(1)} collective-permute-done((f32[72,128]{1,0:T(8,128)S(1)}, f32[72,128]{1,0:T(8,128)S(1)}, u32[]{:S(2)}, u32[]{:S(2)}) %collective-permute-start.37) | collective-permute-done | bytes 36896 | tf_op jit(solution)/shard_map/ppermute | solution.py:171
  83.0 0.6 broadcast_in_dim.16
  83.6 14.8 %all-to-all-start = ((f32[32,1,128]{2,1,0:T(1,128)}), f32[32,1,128]{2,1,0:T(1,128)S(1)}, u32[]{:S(2)}, u32[]{:S(2)}) async-start(f32[32,1,128]{2,1,0:T(1,128)} %broadcast_in_dim.16), calls=%async_computation | async-start | bytes 32768 | tf_op jit(solution)/shard_map/all_to_all | solution.py:229
  98.5 8.5 %all-to-all-done = f32[32,1,128]{2,1,0:T(1,128)S(1)} async-done(((f32[32,1,128]{2,1,0:T(1,128)}), f32[32,1,128]{2,1,0:T(1,128)S(1)}, u32[]{:S(2)}, u32[]{:S(2)}) %all-to-all-start) | async-done | bytes 16416 | tf_op jit(solution)/shard_map/all_to_all | solution.py:229
  107.0 0.8 shard_map.126
  (81 shorter events, 4.4 us)
Async XLA Ops:
  0.6 42.2 %copy-start.12 = (s32[1,1,96]{2,1,0:T(1,128)S(1)}, s32[1,1,96]{2,1,0:T(1,128)}, u32[]{:S(2)}) copy-start(s32[1,1,96]{2,1,0:T(1,128)} %refs_1_.5) | copy-start | bytes 1156
  0.6 42.2 %copy-start.10 = (s32[1,1,96]{2,1,0:T(1,128)S(1)}, s32[1,1,96]{2,1,0:T(1,128)}, u32[]{:S(2)}) copy-start(s32[1,1,96]{2,1,0:T(1,128)} %refs_0_.5) | copy-start | bytes 1156
  0.7 21.4 %copy-start.8 = (s32[1,1,48]{2,1,0:T(1,128)S(1)}, s32[1,1,48]{2,1,0:T(1,128)}, u32[]{:S(2)}) copy-start(s32[1,1,48]{2,1,0:T(1,128)} %prev_ref.5) | copy-start | bytes 580
  0.7 21.3 %copy-start.7 = (s32[1,1,48]{2,1,0:T(1,128)S(1)}, s32[1,1,48]{2,1,0:T(1,128)}, u32[]{:S(2)}) copy-start(s32[1,1,48]{2,1,0:T(1,128)} %own_ref.5) | copy-start | bytes 580
  0.7 5.4 %collective-permute-start.2 = (f32[64,128]{1,0:T(8,128)}, f32[64,128]{1,0:T(8,128)S(1)}, u32[]{:S(2)}, u32[]{:S(2)}) collective-permute-start(f32[64,128]{1,0:T(8,128)} %bitcast.12), channel_id=1, source_target_pairs={{0,6},{1,7},{2,4},{3,5},{4,2},{5,3},{6,0},{7,1},{8,14},{9,15},{10,... | collective-permute-start | bytes 98312 | tf_op jit(solution)/shard_map/ppermute | solution.py:171
  3.8 5.6 %collective-permute-start.1 = (f32[64,128]{1,0:T(8,128)}, f32[64,128]{1,0:T(8,128)S(1)}, u32[]{:S(2)}, u32[]{:S(2)}) collective-permute-start(f32[64,128]{1,0:T(8,128)} %bitcast.13), channel_id=1, source_target_pairs={{0,4},{1,5},{2,6},{3,7},{4,0},{5,1},{6,2},{7,3},{8,12},{9,13},{10,... | collective-permute-start | bytes 98312 | tf_op jit(solution)/shard_map/ppermute | solution.py:171
  4.4 5.0 %collective-permute-start = (f32[64,128]{1,0:T(8,128)}, f32[64,128]{1,0:T(8,128)S(1)}, u32[]{:S(2)}, u32[]{:S(2)}) collective-permute-start(f32[64,128]{1,0:T(8,128)} %bitcast.14), channel_id=1, source_target_pairs={{0,2},{1,3},{2,0},{3,1},{4,6},{5,7},{6,4},{7,5},{8,10},{9,11},{10,... | collective-permute-start | bytes 98312 | tf_op jit(solution)/shard_map/ppermute | solution.py:171
  4.9 5.7 %collective-permute-start.3 = (f32[64,128]{1,0:T(8,128)}, f32[64,128]{1,0:T(8,128)S(1)}, u32[]{:S(2)}, u32[]{:S(2)}) collective-permute-start(f32[64,128]{1,0:T(8,128)} %bitcast.15), channel_id=1, source_target_pairs={{0,1},{1,0},{2,3},{3,2},{4,5},{5,4},{6,7},{7,6},{8,9},{9,8},{10,11... | collective-permute-start | bytes 98312 | tf_op jit(solution)/shard_map/ppermute | solution.py:171
  6.1 4.5 %collective-permute-start.6 = (f32[64,128]{1,0:T(8,128)S(1)}, f32[64,128]{1,0:T(8,128)S(1)}, u32[]{:S(2)}, u32[]{:S(2)}) collective-permute-start(f32[64,128]{1,0:T(8,128)S(1)} %collective-permute-done.2.refs_7_), channel_id=1, source_target_pairs={{0,1},{1,0},{2,3},{3,2},{4,5},{5,4},{6,7},{7,6},{8,9},{9,8},{10,11... | collective-permute-start | bytes 98312 | tf_op jit(solution)/shard_map/ppermute | solution.py:171
  9.4 1.2 %collective-permute-start.5 = (f32[64,128]{1,0:T(8,128)S(1)}, f32[64,128]{1,0:T(8,128)S(1)}, u32[]{:S(2)}, u32[]{:S(2)}) collective-permute-start(f32[64,128]{1,0:T(8,128)S(1)} %collective-permute-done.1.refs_6_), channel_id=1, source_target_pairs={{0,1},{1,0},{2,3},{3,2},{4,5},{5,4},{6,7},{7,6},{8,9},{9,8},{10,11... | collective-permute-start | bytes 98312 | tf_op jit(solution)/shard_map/ppermute | solution.py:171
  9.4 1.4 %collective-permute-start.4 = (f32[64,128]{1,0:T(8,128)S(1)}, f32[64,128]{1,0:T(8,128)S(1)}, u32[]{:S(2)}, u32[]{:S(2)}) collective-permute-start(f32[64,128]{1,0:T(8,128)S(1)} %collective-permute-done.refs_5_), channel_id=1, source_target_pairs={{0,1},{1,0},{2,3},{3,2},{4,5},{5,4},{6,7},{7,6},{8,9},{9,8},{10,11... | collective-permute-start | bytes 98312 | tf_op jit(solution)/shard_map/ppermute | solution.py:171
  14.7 18.9 %copy-start.6 = (f32[1,1,64,128]{3,2,1,0:T(8,128)S(1)}, f32[1,1,64,128]{3,2,1,0:T(8,128)}, u32[]{:S(2)}) copy-start(f32[1,1,64,128]{3,2,1,0:T(8,128)} %param.11) | copy-start | bytes 98308
  14.7 28.1 %copy-start.1 = (bf16[1,1,96,128,128]{4,3,2,1,0:T(8,128)(2,1)S(1)}, bf16[1,1,96,128,128]{4,3,2,1,0:T(8,128)(2,1)}, u32[]{:S(2)}) copy-start(bf16[1,1,96,128,128]{4,3,2,1,0:T(8,128)(2,1)} %refs_3_.5) | copy-start | bytes 9437188
  15.8 10.3 %collective-permute-start.7 = (f32[256,128]{1,0:T(8,128)S(1)}, f32[256,128]{1,0:T(8,128)S(1)}, u32[]{:S(2)}, u32[]{:S(2)}) collective-permute-start(f32[256,128]{1,0:T(8,128)S(1)} %get-tuple-element.35), channel_id=1, source_target_pairs={{0,1},{1,0},{2,3},{3,2},{4,5},{5,4},{6,7},{7,6},{8,9},{9,8},{10,11... | collective-permute-start | bytes 393224 | tf_op jit(solution)/shard_map/ppermute | solution.py:171
  16.2 5.8 %collective-permute-start.11 = (f32[64,128]{1,0:T(8,128)S(1)}, f32[64,128]{1,0:T(8,128)S(1)}, u32[]{:S(2)}, u32[]{:S(2)}) collective-permute-start(f32[64,128]{1,0:T(8,128)S(1)} %bitcast.17), channel_id=1, source_target_pairs={{0,8},{8,16},{16,24},{24,32},{32,40},{40,48},{48,56},{56,64},{64,7... | collective-permute-start | bytes 98312 | tf_op jit(solution)/shard_map/ppermute | solution.py:176
  23.4 26.9 %copy-start.3 = (bf16[1,1,48,128,128]{4,3,2,1,0:T(8,128)(2,1)S(1)}, bf16[1,1,48,128,128]{4,3,2,1,0:T(8,128)(2,1)}, u32[]{:S(2)}) copy-start(bf16[1,1,48,128,128]{4,3,2,1,0:T(8,128)(2,1)} %stiff_ref.5) | copy-start | bytes 4718596
  24.1 6.8 %collective-permute-start.12 = (f32[64,128]{1,0:T(8,128)S(1)}, f32[64,128]{1,0:T(8,128)S(1)}, u32[]{:S(2)}, u32[]{:S(2)}) collective-permute-start(f32[64,128]{1,0:T(8,128)S(1)} %get-tuple-element.41), channel_id=1, source_target_pairs={{8,0},{16,8},{24,16},{32,24},{40,32},{48,40},{56,48},{64,56},{72,6... | collective-permute-start | bytes 98312 | tf_op jit(solution)/shard_map/ppermute | solution.py:176
  26.1 4.8 %collective-permute-start.8 = (f32[64,128]{1,0:T(8,128)S(1)}, f32[64,128]{1,0:T(8,128)S(1)}, u32[]{:S(2)}, u32[]{:S(2)}) collective-permute-start(f32[64,128]{1,0:T(8,128)S(1)} %get-tuple-element.37), channel_id=1, source_target_pairs={{0,2},{1,3},{2,0},{3,1},{4,6},{5,7},{6,4},{7,5},{8,10},{9,11},{10,... | collective-permute-start | bytes 98312 | tf_op jit(solution)/shard_map/ppermute | solution.py:171
  26.3 5.4 %collective-permute-start.9 = (f32[64,128]{1,0:T(8,128)S(1)}, f32[64,128]{1,0:T(8,128)S(1)}, u32[]{:S(2)}, u32[]{:S(2)}) collective-permute-start(f32[64,128]{1,0:T(8,128)S(1)} %get-tuple-element.38), channel_id=1, source_target_pairs={{0,4},{1,5},{2,6},{3,7},{4,0},{5,1},{6,2},{7,3},{8,12},{9,13},{10,... | collective-permute-start | bytes 98312 | tf_op jit(solution)/shard_map/ppermute | solution.py:171
  28.6 5.1 %collective-permute-start.10 = (f32[64,128]{1,0:T(8,128)S(1)}, f32[64,128]{1,0:T(8,128)S(1)}, u32[]{:S(2)}, u32[]{:S(2)}) collective-permute-start(f32[64,128]{1,0:T(8,128)S(1)} %get-tuple-element.39), channel_id=1, source_target_pairs={{0,6},{1,7},{2,4},{3,5},{4,2},{5,3},{6,0},{7,1},{8,14},{9,15},{10,... | collective-permute-start | bytes 98312 | tf_op jit(solution)/shard_map/ppermute | solution.py:171
  33.7 5.2 %collective-permute-start.15 = (f32[64,128]{1,0:T(8,128)S(1)}, f32[64,128]{1,0:T(8,128)S(1)}, u32[]{:S(2)}, u32[]{:S(2)}) collective-permute-start(f32[64,128]{1,0:T(8,128)S(1)} %shard_map.116.refs_4_.mine_ref.v_ref.v1.refs_1_), channel_id=1, source_target_pairs={{0,6},{1,7},{2,4},{3,5},{4,2},{5,3},{6,0},{7,1},{8,14},{9,15},{10,... | collective-permute-start | bytes 98312 | tf_op jit(solution)/shard_map/ppermute | solution.py:171
  36.1 5.4 %collective-permute-start.14 = (f32[64,128]{1,0:T(8,128)S(1)}, f32[64,128]{1,0:T(8,128)S(1)}, u32[]{:S(2)}, u32[]{:S(2)}) collective-permute-start(f32[64,128]{1,0:T(8,128)S(1)} %shard_map.116.refs_4_.mine_ref.v_ref.v1.refs_1_), channel_id=1, source_target_pairs={{0,4},{1,5},{2,6},{3,7},{4,0},{5,1},{6,2},{7,3},{8,12},{9,13},{10,... | collective-permute-start | bytes 98312 | tf_op jit(solution)/shard_map/ppermute | solution.py:171
  36.1 5.4 %collective-permute-start.13 = (f32[64,128]{1,0:T(8,128)S(1)}, f32[64,128]{1,0:T(8,128)S(1)}, u32[]{:S(2)}, u32[]{:S(2)}) collective-permute-start(f32[64,128]{1,0:T(8,128)S(1)} %shard_map.116.refs_4_.mine_ref.v_ref.v1.refs_1_), channel_id=1, source_target_pairs={{0,2},{1,3},{2,0},{3,1},{4,6},{5,7},{6,4},{7,5},{8,10},{9,11},{10,... | collective-permute-start | bytes 98312 | tf_op jit(solution)/shard_map/ppermute | solution.py:171
  37.9 4.1 %collective-permute-start.16 = (f32[64,128]{1,0:T(8,128)S(1)}, f32[64,128]{1,0:T(8,128)S(1)}, u32[]{:S(2)}, u32[]{:S(2)}) collective-permute-start(f32[64,128]{1,0:T(8,128)S(1)} %shard_map.116.refs_4_.mine_ref.v_ref.v1.refs_1_), channel_id=1, source_target_pairs={{0,1},{1,0},{2,3},{3,2},{4,5},{5,4},{6,7},{7,6},{8,9},{9,8},{10,11... | collective-permute-start | bytes 98312 | tf_op jit(solution)/shard_map/ppermute | solution.py:171
  38.9 3.1 %collective-permute-start.19 = (f32[64,128]{1,0:T(8,128)S(1)}, f32[64,128]{1,0:T(8,128)S(1)}, u32[]{:S(2)}, u32[]{:S(2)}) collective-permute-start(f32[64,128]{1,0:T(8,128)S(1)} %collective-permute-done.15.refs_7_), channel_id=1, source_target_pairs={{0,1},{1,0},{2,3},{3,2},{4,5},{5,4},{6,7},{7,6},{8,9},{9,8},{10,11... | collective-permute-start | bytes 98312 | tf_op jit(solution)/shard_map/ppermute | solution.py:171
  41.5 1.2 %collective-permute-start.18 = (f32[64,128]{1,0:T(8,128)S(1)}, f32[64,128]{1,0:T(8,128)S(1)}, u32[]{:S(2)}, u32[]{:S(2)}) collective-permute-start(f32[64,128]{1,0:T(8,128)S(1)} %collective-permute-done.14.refs_6_), channel_id=1, source_target_pairs={{0,1},{1,0},{2,3},{3,2},{4,5},{5,4},{6,7},{7,6},{8,9},{9,8},{10,11... | collective-permute-start | bytes 98312 | tf_op jit(solution)/shard_map/ppermute | solution.py:171
  41.5 1.4 %collective-permute-start.17 = (f32[64,128]{1,0:T(8,128)S(1)}, f32[64,128]{1,0:T(8,128)S(1)}, u32[]{:S(2)}, u32[]{:S(2)}) collective-permute-start(f32[64,128]{1,0:T(8,128)S(1)} %collective-permute-done.13.refs_5_), channel_id=1, source_target_pairs={{0,1},{1,0},{2,3},{3,2},{4,5},{5,4},{6,7},{7,6},{8,9},{9,8},{10,11... | collective-permute-start | bytes 98312 | tf_op jit(solution)/shard_map/ppermute | solution.py:171
  43.9 9.0 %collective-permute-start.20 = (f32[256,128]{1,0:T(8,128)S(1)}, f32[256,128]{1,0:T(8,128)S(1)}, u32[]{:S(2)}, u32[]{:S(2)}) collective-permute-start(f32[256,128]{1,0:T(8,128)S(1)} %get-tuple-element.43), channel_id=1, source_target_pairs={{0,1},{1,0},{2,3},{3,2},{4,5},{5,4},{6,7},{7,6},{8,9},{9,8},{10,11... | collective-permute-start | bytes 393224 | tf_op jit(solution)/shard_map/ppermute | solution.py:171
  44.5 5.8 %collective-permute-start.24 = (f32[64,128]{1,0:T(8,128)S(1)}, f32[64,128]{1,0:T(8,128)S(1)}, u32[]{:S(2)}, u32[]{:S(2)}) collective-permute-start(f32[64,128]{1,0:T(8,128)S(1)} %shard_map.116.refs_4_.mine_ref.v_ref.v1.refs_1_), channel_id=1, source_target_pairs={{0,8},{8,16},{16,24},{24,32},{32,40},{40,48},{48,56},{56,64},{64,7... | collective-permute-start | bytes 98312 | tf_op jit(solution)/shard_map/ppermute | solution.py:176
  51.0 6.8 %collective-permute-start.25 = (f32[64,128]{1,0:T(8,128)S(1)}, f32[64,128]{1,0:T(8,128)S(1)}, u32[]{:S(2)}, u32[]{:S(2)}) collective-permute-start(f32[64,128]{1,0:T(8,128)S(1)} %get-tuple-element.49), channel_id=1, source_target_pairs={{8,0},{16,8},{24,16},{32,24},{40,32},{48,40},{56,48},{64,56},{72,6... | collective-permute-start | bytes 98312 | tf_op jit(solution)/shard_map/ppermute | solution.py:176
  53.0 4.8 %collective-permute-start.21 = (f32[64,128]{1,0:T(8,128)S(1)}, f32[64,128]{1,0:T(8,128)S(1)}, u32[]{:S(2)}, u32[]{:S(2)}) collective-permute-start(f32[64,128]{1,0:T(8,128)S(1)} %get-tuple-element.45), channel_id=1, source_target_pairs={{0,2},{1,3},{2,0},{3,1},{4,6},{5,7},{6,4},{7,5},{8,10},{9,11},{10,... | collective-permute-start | bytes 98312 | tf_op jit(solution)/shard_map/ppermute | solution.py:171
  53.1 5.5 %collective-permute-start.22 = (f32[64,128]{1,0:T(8,128)S(1)}, f32[64,128]{1,0:T(8,128)S(1)}, u32[]{:S(2)}, u32[]{:S(2)}) collective-permute-start(f32[64,128]{1,0:T(8,128)S(1)} %get-tuple-element.46), channel_id=1, source_target_pairs={{0,4},{1,5},{2,6},{3,7},{4,0},{5,1},{6,2},{7,3},{8,12},{9,13},{10,... | collective-permute-start | bytes 98312 | tf_op jit(solution)/shard_map/ppermute | solution.py:171
  55.5 5.1 %collective-permute-start.23 = (f32[64,128]{1,0:T(8,128)S(1)}, f32[64,128]{1,0:T(8,128)S(1)}, u32[]{:S(2)}, u32[]{:S(2)}) collective-permute-start(f32[64,128]{1,0:T(8,128)S(1)} %get-tuple-element.47), channel_id=1, source_target_pairs={{0,6},{1,7},{2,4},{3,5},{4,2},{5,3},{6,0},{7,1},{8,14},{9,15},{10,... | collective-permute-start | bytes 98312 | tf_op jit(solution)/shard_map/ppermute | solution.py:171
  60.6 46.4 %copy-start.5 = (f32[1,1,64,128]{3,2,1,0:T(8,128)S(1)}, f32[1,1,64,128]{3,2,1,0:T(8,128)}, u32[]{:S(2)}) copy-start(f32[1,1,64,128]{3,2,1,0:T(8,128)} %param.10) | copy-start | bytes 98308
  60.6 8.5 %collective-permute-start.28 = (f32[64,128]{1,0:T(8,128)S(1)}, f32[64,128]{1,0:T(8,128)S(1)}, u32[]{:S(2)}, u32[]{:S(2)}) collective-permute-start(f32[64,128]{1,0:T(8,128)S(1)} %shard_map.120.refs_4_.mine_ref.v2.v_ref.refs_2_), channel_id=1, source_target_pairs={{0,6},{1,7},{2,4},{3,5},{4,2},{5,3},{6,0},{7,1},{8,14},{9,15},{10,... | collective-permute-start | bytes 98312 | tf_op jit(solution)/shard_map/ppermute | solution.py:171
  63.0 6.6 %collective-permute-start.27 = (f32[64,128]{1,0:T(8,128)S(1)}, f32[64,128]{1,0:T(8,128)S(1)}, u32[]{:S(2)}, u32[]{:S(2)}) collective-permute-start(f32[64,128]{1,0:T(8,128)S(1)} %shard_map.120.refs_4_.mine_ref.v2.v_ref.refs_2_), channel_id=1, source_target_pairs={{0,4},{1,5},{2,6},{3,7},{4,0},{5,1},{6,2},{7,3},{8,12},{9,13},{10,... | collective-permute-start | bytes 98312 | tf_op jit(solution)/shard_map/ppermute | solution.py:171
  63.0 6.8 %collective-permute-start.26 = (f32[64,128]{1,0:T(8,128)S(1)}, f32[64,128]{1,0:T(8,128)S(1)}, u32[]{:S(2)}, u32[]{:S(2)}) collective-permute-start(f32[64,128]{1,0:T(8,128)S(1)} %shard_map.120.refs_4_.mine_ref.v2.v_ref.refs_2_), channel_id=1, source_target_pairs={{0,2},{1,3},{2,0},{3,1},{4,6},{5,7},{6,4},{7,5},{8,10},{9,11},{10,... | collective-permute-start | bytes 98312 | tf_op jit(solution)/shard_map/ppermute | solution.py:171
  64.8 5.8 %collective-permute-start.33 = (f32[64,128]{1,0:T(8,128)S(1)}, f32[64,128]{1,0:T(8,128)S(1)}, u32[]{:S(2)}, u32[]{:S(2)}) collective-permute-start(f32[64,128]{1,0:T(8,128)S(1)} %shard_map.120.refs_4_.mine_ref.v2.v_ref.refs_2_), channel_id=1, source_target_pairs={{0,8},{8,16},{16,24},{24,32},{32,40},{40,48},{48,56},{56,64},{64,7... | collective-permute-start | bytes 98312 | tf_op jit(solution)/shard_map/ppermute | solution.py:176
  69.0 2.2 %collective-permute-start.29 = (f32[64,128]{1,0:T(8,128)S(1)}, f32[64,128]{1,0:T(8,128)S(1)}, u32[]{:S(2)}, u32[]{:S(2)}) collective-permute-start(f32[64,128]{1,0:T(8,128)S(1)} %shard_map.120.refs_4_.mine_ref.v2.v_ref.refs_2_), channel_id=1, source_target_pairs={{0,1},{1,0},{2,3},{3,2},{4,5},{5,4},{6,7},{7,6},{8,9},{9,8},{10,11... | collective-permute-start | bytes 98312 | tf_op jit(solution)/shard_map/ppermute | solution.py:171
  69.1 2.1 %collective-permute-start.32 = (f32[64,128]{1,0:T(8,128)S(1)}, f32[64,128]{1,0:T(8,128)S(1)}, u32[]{:S(2)}, u32[]{:S(2)}) collective-permute-start(f32[64,128]{1,0:T(8,128)S(1)} %collective-permute-done.28.refs_7_), channel_id=1, source_target_pairs={{0,1},{1,0},{2,3},{3,2},{4,5},{5,4},{6,7},{7,6},{8,9},{9,8},{10,11... | collective-permute-start | bytes 98312 | tf_op jit(solution)/shard_map/ppermute | solution.py:171
  69.6 1.7 %collective-permute-start.31 = (f32[64,128]{1,0:T(8,128)S(1)}, f32[64,128]{1,0:T(8,128)S(1)}, u32[]{:S(2)}, u32[]{:S(2)}) collective-permute-start(f32[64,128]{1,0:T(8,128)S(1)} %collective-permute-done.27.refs_6_), channel_id=1, source_target_pairs={{0,1},{1,0},{2,3},{3,2},{4,5},{5,4},{6,7},{7,6},{8,9},{9,8},{10,11... | collective-permute-start | bytes 98312 | tf_op jit(solution)/shard_map/ppermute | solution.py:171
  69.8 1.6 %collective-permute-start.30 = (f32[64,128]{1,0:T(8,128)S(1)}, f32[64,128]{1,0:T(8,128)S(1)}, u32[]{:S(2)}, u32[]{:S(2)}) collective-permute-start(f32[64,128]{1,0:T(8,128)S(1)} %collective-permute-done.26.refs_5_), channel_id=1, source_target_pairs={{0,1},{1,0},{2,3},{3,2},{4,5},{5,4},{6,7},{7,6},{8,9},{9,8},{10,11... | collective-permute-start | bytes 98312 | tf_op jit(solution)/shard_map/ppermute | solution.py:171
  72.5 1.5 %collective-permute-start.34 = (f32[288,128]{1,0:T(8,128)S(1)}, f32[288,128]{1,0:T(8,128)S(1)}, u32[]{:S(2)}, u32[]{:S(2)}) collective-permute-start(f32[288,128]{1,0:T(8,128)S(1)} %bitcast.30), channel_id=1, source_target_pairs={{0,1},{1,0},{2,3},{3,2},{4,5},{5,4},{6,7},{7,6},{8,9},{9,8},{10,11... | collective-permute-start | bytes 442376 | tf_op jit(solution)/shard_map/ppermute | solution.py:171
  74.0 6.7 %collective-permute-start.35 = (f32[72,128]{1,0:T(8,128)S(1)}, f32[72,128]{1,0:T(8,128)S(1)}, u32[]{:S(2)}, u32[]{:S(2)}) collective-permute-start(f32[72,128]{1,0:T(8,128)S(1)} %get-tuple-element.59), channel_id=1, source_target_pairs={{0,2},{1,3},{2,0},{3,1},{4,6},{5,7},{6,4},{7,5},{8,10},{9,11},{10,... | collective-permute-start | bytes 110600 | tf_op jit(solution)/shard_map/ppermute | solution.py:171
  74.3 6.4 %collective-permute-start.36 = (f32[72,128]{1,0:T(8,128)S(1)}, f32[72,128]{1,0:T(8,128)S(1)}, u32[]{:S(2)}, u32[]{:S(2)}) collective-permute-start(f32[72,128]{1,0:T(8,128)S(1)} %get-tuple-element.60), channel_id=1, source_target_pairs={{0,4},{1,5},{2,6},{3,7},{4,0},{5,1},{6,2},{7,3},{8,12},{9,13},{10,... | collective-permute-start | bytes 110600 | tf_op jit(solution)/shard_map/ppermute | solution.py:171
  77.8 5.2 %collective-permute-start.37 = (f32[72,128]{1,0:T(8,128)S(1)}, f32[72,128]{1,0:T(8,128)S(1)}, u32[]{:S(2)}, u32[]{:S(2)}) collective-permute-start(f32[72,128]{1,0:T(8,128)S(1)} %get-tuple-element.61), channel_id=1, source_target_pairs={{0,6},{1,7},{2,4},{3,5},{4,2},{5,3},{6,0},{7,1},{8,14},{9,15},{10,... | collective-permute-start | bytes 110600 | tf_op jit(solution)/shard_map/ppermute | solution.py:171
  78.8 19.7 %collective-permute-start.38 = (f32[64,128]{1,0:T(8,128)S(1)}, f32[64,128]{1,0:T(8,128)S(1)}, u32[]{:S(2)}, u32[]{:S(2)}) collective-permute-start(f32[64,128]{1,0:T(8,128)S(1)} %get-tuple-element.63), channel_id=1, source_target_pairs={{8,0},{16,8},{24,16},{32,24},{40,32},{48,40},{56,48},{64,56},{72,6... | collective-permute-start | bytes 98312 | tf_op jit(solution)/shard_map/ppermute | solution.py:176
  83.6 23.4 %all-to-all-start = ((f32[32,1,128]{2,1,0:T(1,128)}), f32[32,1,128]{2,1,0:T(1,128)S(1)}, u32[]{:S(2)}, u32[]{:S(2)}) async-start(f32[32,1,128]{2,1,0:T(1,128)} %broadcast_in_dim.16), calls=%async_computation | async-start | bytes 32768 | tf_op jit(solution)/shard_map/all_to_all | solution.py:229
  (5 other events, 5.4 us)

commit v2 on v1

v2 whole, which is shorter than its diff:
```python
import functools

import jax
import jax.numpy as jnp
from jax import lax
from jax.experimental import pallas as pl
from jax.experimental.pallas import tpu as pltpu
from jax.sharding import PartitionSpec as P

ITERS = 3
ROWS = 8
HOTFLOPS = 20000000000
OPFLOPS = 0
SCATTER = "three"
F32, BF16 = jnp.float32, jnp.bfloat16
VMEM = pl.BlockSpec(memory_space=pltpu.VMEM)
CONTRACT_ROWS = (((0,), (0,)), ((), ()))
GROUP = 8


def split(x):
    high = x.astype(BF16)
    return jnp.concatenate([high, (x - high.astype(F32)).astype(BF16)], 1)


def fold(x):
    half = x.shape[1] // 2
    return x[:, :half] + x[:, half:]


def springs(hot, field, stiff_ref, u_ref):
    slots, node = u_ref.shape
    diff = fold(lax.dot_general(hot, split(field), CONTRACT_ROWS, preferred_element_type=F32))
    rows = lax.broadcasted_iota(jnp.int32, (2 * GROUP, GROUP * node), 0) % GROUP
    cols = lax.broadcasted_iota(jnp.int32, (2 * GROUP, GROUP * node), 1) // node
    own = rows == cols
    for start in range(0, slots, GROUP):
        part = diff[start : start + GROUP]
        high = part.astype(BF16).astype(F32)
        both = jnp.concatenate([high, part - high], 0)
        wide = jnp.where(own, jnp.concatenate([both] * GROUP, 1), 0.0).astype(BF16)
        block = stiff_ref[0, 0, start : start + GROUP].reshape(GROUP * node, node)
        got = jnp.dot(wide, block, preferred_element_type=F32)
        u_ref[start : start + GROUP, :] = got[:GROUP] + got[GROUP:]
    u = u_ref[...]
    spread = fold(jnp.dot(hot, split(u), preferred_element_type=F32))
    return spread, jnp.sum(diff * u, axis=0, keepdims=True)


def one_hot(near, far, count, blocks, paired=True):
    slots = near.shape[1]
    live = lax.broadcasted_iota(jnp.int32, (1, slots), 1) < count
    place = lax.broadcasted_iota(jnp.int32, (blocks, slots), 0)
    plus = jnp.where(live & (place == near), 1.0, 0.0)
    minus = jnp.where(live & paired & (place == far), 1.0, 0.0)
    return (plus - minus).astype(BF16)


def resident(ref):
    return lambda start: ref[0, 0, start : start + GROUP]


def fetched(ref, held, sems):
    pieces = sems.shape[0]
    chunk = held.shape[0] // pieces
    copies = []
    for piece in range(pieces):
        part = pl.ds(piece * chunk, chunk)
        copies.append(pltpu.make_async_copy(ref.at[0, 0, part], held.at[part], sems.at[piece]))
        copies[-1].start()

    def group(start):
        if start % chunk == 0:
            copies[start // chunk].wait()
        return held[start : start + GROUP]

    return group


def hot_kernel(section, tile, count, count_ex, *refs):
    own, far, near, prev = [r[...] for r in refs[:4]]
    hot_in, hot_ex = refs[4:]
    blk = hot_ex.shape[0] // 2
    far = far[0]
    there = tile[0] ^ (far // blk)
    place = ((there % 2) * 4 + there // 2) * blk + far % blk
    hot_in[...] = one_hot(own[0], place, count[0], 8 * blk)
    hot_ex[...] = one_hot(near[0], prev[0] + blk, count_ex[0], 2 * blk, section[0] > 0)


def pass_kernel(v_ref, out_ref):
    out_ref[...] = v_ref[...]


def operator_kernel(step, n_fields, hot_in, hot_ex, in_ref, ex_ref, anchor_ref, row_ref, before_ref, *refs):
    fields = refs[:n_fields]
    mine_ref, other_ref, back_ref, row_out, u_in, u_ex = refs[n_fields:]
    blk = before_ref.shape[0]
    field = jnp.concatenate([f[...] for f in fields], 0)
    spread, energy = springs(hot_in[...], field, in_ref, u_in)
    v = field[:blk]
    spread_ex, energy_ex = springs(hot_ex[...], jnp.concatenate([v, before_ref[...]], 0), ex_ref, u_ex)
    back_ref[...] = spread_ex[blk:]
    image = anchor_ref[...] * v
    energy = jnp.sum(image * v, axis=0, keepdims=True) + energy + energy_ex
    square = jnp.sum(v * v, axis=0, keepdims=True)
    rows = lax.broadcasted_iota(jnp.int32, row_ref.shape, 0)
    row = row_ref[...] + jnp.where(rows == 2 * step, square, 0.0) + jnp.where(rows == 2 * step + 1, energy, 0.0)
    row_out[...] = row
    mine = spread[: 4 * blk]
    other = spread[4 * blk :]
    tall = mine_ref.shape[0] // 4
    for j in range(4):
        block = mine[j * blk : (j + 1) * blk]
        if j == 0:
            block = block + image + spread_ex[:blk]
        mine_ref[j * tall : j * tall + blk, :] = block
        other_ref[j * tall : j * tall + blk, :] = other[j * blk : (j + 1) * blk]
        if tall > blk:
            mine_ref[j * tall + blk : (j + 1) * tall, :] = row
            other_ref[j * tall + blk : (j + 1) * tall, :] = row


def pair_kernel(mine_ref, got_ref, *outs):
    tall = mine_ref.shape[0] // 4
    per = 4 // len(outs)
    for place, j in enumerate((0, 3, 1, 2)):
        block = mine_ref[j * tall : (j + 1) * tall] + got_ref[j * tall : (j + 1) * tall]
        at = (place % per) * tall
        outs[place // per][at : at + tall, :] = block


def half_kernel(a_ref, b_ref, keep_ref, send_ref):
    tall = keep_ref.shape[0]
    keep_ref[...] = a_ref[:tall] + b_ref[:tall]
    send_ref[...] = a_ref[tall:] + b_ref[tall:]


def tree(values):
    while len(values) > 1:
        values = [a + b for a, b in zip(values[::2], values[1::2])]
    return values[0]


def sum_kernel(n, *refs):
    parts, incoming, out = refs[:n], refs[n], refs[n + 1]
    out[...] = tree([p[...] for p in parts]) + incoming[...]


def row_kernel(n, *refs):
    out = refs[n]
    rows = tree([p[p.shape[0] - out.shape[1] :] for p in refs[:n]])
    out[...] = jnp.broadcast_to(rows[None], out.shape)


def quadratic(coef, moments, shift):
    total = 0.0
    for i, a in enumerate(coef):
        for j, b in enumerate(coef):
            total = total + a * b * moments[i + j + shift]
    return total


def final_kernel(n, sums_ref, *refs):
    parts, incoming = refs[:n], refs[n]
    *vs, x_ref, r_ref = refs[n + 1 :]
    blk = incoming.shape[0]
    vs = [v[...] for v in vs] + [tree([p[:blk] for p in parts]) + incoming[...]]
    rows = jnp.sum(jnp.sum(sums_ref[...], axis=0), axis=1, keepdims=True)
    raw = [rows[j : j + 1] for j in range(2 * ITERS)]
    sigma = raw[1] / raw[0]
    inverse = 1.0 / sigma
    moments, scale = [], 1.0 / raw[0]
    for m in raw:
        moments.append(m * scale)
        scale = scale * inverse
    zero, one = jnp.zeros_like(sigma), jnp.ones_like(sigma)
    r, p, x = [one], [one], [zero]
    rr = one
    for step in range(ITERS):
        alpha = rr / quadratic(p, moments, 1)
        x = [a + alpha * b for a, b in zip(x + [zero] * (len(p) - len(x)), p)]
        q = [zero] + p
        r = [a - alpha * b for a, b in zip(r + [zero], q)]
        if step < ITERS - 1:
            new = quadratic(r, moments, 0)
            p = [a + (new / rr) * b for a, b in zip(r, p + [zero])]
            rr = new
    power = one
    x_sum, r_sum = 0.0, 0.0
    for k in range(ITERS + 1):
        v = vs[k]
        r_sum = r_sum + (r[k] * power) * v
        power = power * inverse
        if k < ITERS:
            x_sum = x_sum + (x[k] * power) * v
    x_ref[...] = x_sum
    r_ref[...] = r_sum


def call(kernel, outs, *args, scratch=(), scalars=0, dtype=F32, flops=0, hbm=False, limit=16):
    specs = [pl.BlockSpec(memory_space=pltpu.SMEM)] * scalars
    specs += [pl.BlockSpec(memory_space=pltpu.HBM) if hbm else VMEM] * (len(args) - scalars)
    dtypes = dtype if isinstance(dtype, tuple) else (dtype,) * len(outs)
    return pl.pallas_call(
        kernel,
        out_shape=[jax.ShapeDtypeStruct(o, d) for o, d in zip(outs, dtypes)],
        in_specs=specs,
        out_specs=[VMEM] * len(outs),
        scratch_shapes=scratch,
        compiler_params=pltpu.CompilerParams(vmem_limit_bytes=limit * 2**20),
        cost_estimate=pl.CostEstimate(flops=flops, bytes_accessed=0, transcendentals=0) if flops else None,
    )(*args)


def swap(x, by):
    return lax.ppermute(x, "tile", [(i, i ^ by) for i in range(lax.axis_size("tile"))])


def shifted(x, by):
    peers = lax.axis_size("sec")
    return lax.ppermute(x, "sec", [(i, (i + by) % peers) for i in range(peers)])


def per_device(
    right_side,
    anchor_diag,
    intra_own,
    intra_far,
    intra_count,
    inter_own,
    inter_prev,
    inter_count,
    intra_stiff,
    inter_stiff,
):
    blk, node = right_side.shape[2:]
    anchor = anchor_diag[0, 0]
    section = lax.axis_index("sec").astype(jnp.int32).reshape(1)
    tile = lax.axis_index("tile").astype(jnp.int32).reshape(1)
    field, row = (blk, node), (ROWS, node)
    vs, moments = [right_side[0, 0]], jnp.zeros(row, F32)
    sections = lax.axis_size("sec")
    hot = call(
        hot_kernel, ((lax.axis_size("tile") * blk, intra_own.shape[2]), (2 * blk, inter_own.shape[2])),
        section, tile, intra_count.reshape(1), inter_count.reshape(1), intra_own, intra_far, inter_own, inter_prev, scalars=4, dtype=BF16,
    )
    (early,) = call(pass_kernel, (field,), vs[0], flops=HOTFLOPS)
    for step in range(ITERS):
        last = step == ITERS - 1
        tall = blk + ROWS if last else blk
        v = vs[-1]
        here = [v] + [swap(v, 2 * j) for j in (1, 2, 3)]
        if step == 0:
            v = early
        fields = here + [swap(h, 1) for h in [v] + here[1:]]
        before = shifted(v, 1)
        mine, other, back, moments = call(
            functools.partial(operator_kernel, step, len(fields)), ((4 * tall, node), (4 * tall, node), field, row),
            *hot, intra_stiff, inter_stiff, anchor, moments, before, *fields,
            scratch=[pltpu.VMEM((intra_own.shape[2], node), F32), pltpu.VMEM((inter_own.shape[2], node), F32)], flops=OPFLOPS,
        )
        incoming = shifted(back, -1)
        got = swap(other, 1)
        if SCATTER == "three":
            p0, p3, p1, p2 = call(pair_kernel, ((tall, node),) * 4, mine, got)
            parts = [p0] + [swap(p, 2 * j) for j, p in ((1, p1), (2, p2), (3, p3))]
        else:
            keep, send = call(pair_kernel, ((2 * tall, node),) * 2, mine, got)
            keep, send = call(half_kernel, ((tall, node),) * 2, keep, swap(send, 2))
            parts = [keep, swap(send, 6)]
        if not last:
            (nxt,) = call(functools.partial(sum_kernel, len(parts)), (field,), *parts, incoming)
            vs.append(nxt)
    (sums,) = call(functools.partial(row_kernel, len(parts)), ((sections, ROWS, node),), *parts)
    sums = lax.all_to_all(sums, "sec", 0, 0, tiled=True)
    x, r = call(functools.partial(final_kernel, len(parts)), (field, field), sums, *parts, incoming, *vs)
    return x[None, None], r[None, None]


def solution(mesh):
    return jax.shard_map(
        per_device,
        mesh=mesh,
        in_specs=(
            P("sec", "tile", None, None),
            P("sec", "tile", None, None),
            P("sec", "tile", None),
            P("sec", "tile", None),
            P("sec", "tile"),
            P("sec", "tile", None),
            P("sec", "tile", None),
            P("sec", "tile"),
            P("sec", "tile", None, None, None),
            P("sec", "tile", None, None, None),
        ),
        out_specs=(P("sec", "tile", None, None), P("sec", "tile", None, None)),
        check_vma=False,
    )
```

time: 109 us -> 91.2 us (0.84)
  starting transfers between devices: 62.7 us -> 48.4 us
  local copies, waits for them, and re-layouts: 6.04 us -> 2.23 us
  waiting for transfers between devices: 30.6 us -> 31.9 us
    all_to_all x1, starting transfers between devices: 14.8 us -> 7.41 us  [per_device(): sums = lax.all_to_all(sums, 'sec', 0, 0, tiled=True)]
    ppermute x6, starting transfers between devices: 17.7 us -> 12.3 us  [shifted(): return lax.ppermute(x, 'sec', [(i, (i + by) % peers) for i in range(peers)])]
    unnamed x26 -> x20, local copies, waits for them, and re-layouts: 5.4 us -> 2.23 us
    all_to_all x1, waiting for transfers between devices: 8.45 us -> 5.66 us  [per_device(): sums = lax.all_to_all(sums, 'sec', 0, 0, tiled=True)]
    ppermute x6, waiting for transfers between devices: 3.67 us -> 6.19 us  [shifted(): return lax.ppermute(x, 'sec', [(i, (i + by) % peers) for i in range(peers)])]
    ppermute x33, waiting for transfers between devices: 18.5 us -> 20.1 us  [swap(): lax.ppermute(x, 'tile', [(i, i ^ by) for i in range(lax.axis_size('tile'))])]
    ppermute x33, starting transfers between devices: 30.2 us -> 28.7 us  [swap(): lax.ppermute(x, 'tile', [(i, i ^ by) for i in range(lax.axis_size('tile'))])]
    pallas_call x14 -> x12, Pallas kernels: 6.07 us -> 6.17 us  [call(): pl.pallas_call(kernel, out_shape=[jax.ShapeDtypeStruct(o, d) for o, d in...]
  transfers between devices with their start and end apart: 40 -> 40, of which waited for: 17 -> 18; matrix products, arithmetic and copies ran while one was open for 1% -> 0% of each run, Pallas kernels for 2% -> 0%
where the time goes in v2:
time: 91.2 us; the launch traced here: 90.9 us
  starting transfers between devices  48.4 us (53%)
  waiting for transfers between devices  31.9 us (35%)
  Pallas kernels  6.17 us (7%)
  local copies, waits for them, and re-layouts  2.23 us (2%)
  between operations  2.21 us (2%)
    ppermute x33, starting transfers between devices, swap(): lax.ppermute(x, 'tile', [(i, i ^ by) for i in range(lax.axis_size('tile'))])  28.7 us
    ppermute x33, waiting for transfers between devices, swap(): lax.ppermute(x, 'tile', [(i, i ^ by) for i in range(lax.axis_size('tile'))])  20.1 us
    ppermute x6, starting transfers between devices, shifted(): return lax.ppermute(x, 'sec', [(i, (i + by) % peers) for i in range(peers)])  12.3 us
    all_to_all x1, starting transfers between devices, per_device(): sums = lax.all_to_all(sums, 'sec', 0, 0, tiled=True)  7.41 us
    ppermute x6, waiting for transfers between devices, shifted(): return lax.ppermute(x, 'sec', [(i, (i + by) % peers) for i in range(peers)])  6.19 us
    pallas_call x12, Pallas kernels, call(): pl.pallas_call(kernel, out_shape=[jax.ShapeDtypeStruct(o, d) for o, d in...  6.17 us
    all_to_all x1, waiting for transfers between devices, per_device(): sums = lax.all_to_all(sums, 'sec', 0, 0, tiled=True)  5.66 us
    unnamed x20, local copies, waits for them, and re-layouts  2.23 us
  transfers between devices with their start and end apart: 40, of which 18 were waited for; matrix products, arithmetic and copies ran while one was open for 0% of the time, Pallas kernels for 0%

profile of v2, /device:TPU:32, one launch (start us, length us, event | category | flops | bytes accessed | tf_op | source)
XLA Modules:
  0.0 90.9 jit_solution(16261306117705088477)
XLA Ops:
  0.7 3.1 %collective-permute-start.3 = (f32[64,128]{1,0:T(8,128)}, f32[64,128]{1,0:T(8,128)S(1)}, u32[]{:S(2)}, u32[]{:S(2)}) collective-permute-start(f32[64,128]{1,0:T(8,128)} %bitcast.13), channel_id=1, source_target_pairs={{0,6},{1,7},{2,4},{3,5},{4,2},{5,3},{6,0},{7,1},{8,14},{9,15},{10,... | collective-permute-start | bytes 98312 | tf_op jit(solution)/shard_map/ppermute | solution.py:217
  3.8 0.6 collective-permute-start.2
  4.4 0.5 collective-permute-start.1
  4.9 0.8 copy-done.4
  5.8 2.0 %collective-permute-start = (f32[64,128]{1,0:T(8,128)S(1)}, f32[64,128]{1,0:T(8,128)S(1)}, u32[]{:S(2)}, u32[]{:S(2)}) collective-permute-start(f32[64,128]{1,0:T(8,128)S(1)} %shard_map.114), channel_id=1, source_target_pairs={{0,8},{8,16},{16,24},{24,32},{32,40},{40,48},{48,56},{56,64},{64,7... | collective-permute-start | bytes 98312 | tf_op jit(solution)/shard_map/ppermute | solution.py:222
  7.9 1.5 %collective-permute-done.2.refs_2_ = f32[64,128]{1,0:T(8,128)S(1)} collective-permute-done((f32[64,128]{1,0:T(8,128)}, f32[64,128]{1,0:T(8,128)S(1)}, u32[]{:S(2)}, u32[]{:S(2)}) %collective-permute-start.2) | collective-permute-done | bytes 32800 | tf_op jit(solution)/shard_map/ppermute | solution.py:217
  9.4 0.5 collective-permute-start.5
  11.5 1.4 %copy-done.1 = bf16[1,1,48,128,128]{4,3,2,1,0:T(8,128)(2,1)S(1)} copy-done((bf16[1,1,48,128,128]{4,3,2,1,0:T(8,128)(2,1)S(1)}, bf16[1,1,48,128,128]{4,3,2,1,0:T(8,128)(2,1)}, u32[]{:S(2)}) %copy-start.1) | copy-done | bytes 1572888
  12.9 1.3 %shard_map.115 = (f32[256,128]{1,0:T(8,128)S(1)}, f32[256,128]{1,0:T(8,128)S(1)}, f32[64,128]{1,0:T(8,128)S(1)}, f32[8,128]{1,0:T(8,128)S(1)}) custom-call(bf16[512,96]{1,0:T(8,128)(2,1)S(1)} %get-tuple-element.29.hot_in, bf16[128,48]{1,0:T(8,128)(2,1)S(1)} %get-tuple-element.30.hot_ex, bf16[1,1,96,128,128]{4,3,2,1,0:T(8,128)(2,1)S(1)} %copy-done, ...), custom_call_target="tpu_custom_call" | custom-call | tf_op jit(solution)/shard_map/pallas_call | solution.py:205
  14.3 4.6 %collective-permute-start.12 = (f32[64,128]{1,0:T(8,128)S(1)}, f32[64,128]{1,0:T(8,128)S(1)}, u32[]{:S(2)}, u32[]{:S(2)}) collective-permute-start(f32[64,128]{1,0:T(8,128)S(1)} %get-tuple-element.38), channel_id=1, source_target_pairs={{0,248},{8,0},{16,8},{24,16},{32,24},{40,32},{48,40},{56,48},{64,5... | collective-permute-start | bytes 98312 | tf_op jit(solution)/shard_map/ppermute | solution.py:222
  19.0 1.7 %collective-permute-start.9 = (f32[64,128]{1,0:T(8,128)S(1)}, f32[64,128]{1,0:T(8,128)S(1)}, u32[]{:S(2)}, u32[]{:S(2)}) collective-permute-start(f32[64,128]{1,0:T(8,128)S(1)} %get-tuple-element.35), channel_id=1, source_target_pairs={{0,2},{1,3},{2,0},{3,1},{4,6},{5,7},{6,4},{7,5},{8,10},{9,11},{10,... | collective-permute-start | bytes 98312 | tf_op jit(solution)/shard_map/ppermute | solution.py:217
  20.6 2.9 %collective-permute-start.10 = (f32[64,128]{1,0:T(8,128)S(1)}, f32[64,128]{1,0:T(8,128)S(1)}, u32[]{:S(2)}, u32[]{:S(2)}) collective-permute-start(f32[64,128]{1,0:T(8,128)S(1)} %get-tuple-element.36), channel_id=1, source_target_pairs={{0,4},{1,5},{2,6},{3,7},{4,0},{5,1},{6,2},{7,3},{8,12},{9,13},{10,... | collective-permute-start | bytes 98312 | tf_op jit(solution)/shard_map/ppermute | solution.py:217
  23.5 0.2 collective-permute-start.11
  23.8 2.3 %collective-permute-done.10.refs_2_ = f32[64,128]{1,0:T(8,128)S(1)} collective-permute-done((f32[64,128]{1,0:T(8,128)S(1)}, f32[64,128]{1,0:T(8,128)S(1)}, u32[]{:S(2)}, u32[]{:S(2)}) %collective-permute-start.10) | collective-permute-done | bytes 32800 | tf_op jit(solution)/shard_map/ppermute | solution.py:217
  26.0 2.6 %collective-permute-done.11.refs_3_ = f32[64,128]{1,0:T(8,128)S(1)} collective-permute-done((f32[64,128]{1,0:T(8,128)S(1)}, f32[64,128]{1,0:T(8,128)S(1)}, u32[]{:S(2)}, u32[]{:S(2)}) %collective-permute-start.11) | collective-permute-done | bytes 32800 | tf_op jit(solution)/shard_map/ppermute | solution.py:217
  28.7 0.3 collective-permute-start.16
  29.0 0.8 collective-permute-start.15
  29.8 3.1 %collective-permute-start.14 = (f32[64,128]{1,0:T(8,128)S(1)}, f32[64,128]{1,0:T(8,128)S(1)}, u32[]{:S(2)}, u32[]{:S(2)}) collective-permute-start(f32[64,128]{1,0:T(8,128)S(1)} %shard_map.117.refs_0_.refs_6_), channel_id=1, source_target_pairs={{0,2},{1,3},{2,0},{3,1},{4,6},{5,7},{6,4},{7,5},{8,10},{9,11},{10,... | collective-permute-start | bytes 98312 | tf_op jit(solution)/shard_map/ppermute | solution.py:217
  32.9 1.0 %collective-permute-done.16.refs_3_ = f32[64,128]{1,0:T(8,128)S(1)} collective-permute-done((f32[64,128]{1,0:T(8,128)S(1)}, f32[64,128]{1,0:T(8,128)S(1)}, u32[]{:S(2)}, u32[]{:S(2)}) %collective-permute-start.16) | collective-permute-done | bytes 32800 | tf_op jit(solution)/shard_map/ppermute | solution.py:217
  33.9 0.5 collective-permute-done.15.refs_2_
  34.4 0.7 collective-permute-done.14.refs_1_
  35.1 1.8 %collective-permute-done.13.before_ref = f32[64,128]{1,0:T(8,128)S(1)} collective-permute-done((f32[64,128]{1,0:T(8,128)S(1)}, f32[64,128]{1,0:T(8,128)S(1)}, u32[]{:S(2)}, u32[]{:S(2)}) %collective-permute-start.13) | collective-permute-done | bytes 32800 | tf_op jit(solution)/shard_map/ppermute | solution.py:222
  36.9 1.3 %shard_map.118 = (f32[256,128]{1,0:T(8,128)S(1)}, f32[256,128]{1,0:T(8,128)S(1)}, f32[64,128]{1,0:T(8,128)S(1)}, f32[8,128]{1,0:T(8,128)S(1)}) custom-call(bf16[512,96]{1,0:T(8,128)(2,1)S(1)} %get-tuple-element.29.hot_in, bf16[128,48]{1,0:T(8,128)(2,1)S(1)} %get-tuple-element.30.hot_ex, bf16[1,1,96,128,128]{4,3,2,1,0:T(8,128)(2,1)S(1)} %copy-done, ...), custom_call_target="tpu_custom_call" | custom-call | tf_op jit(solution)/shard_map/pallas_call | solution.py:205
  38.3 5.3 %collective-permute-start.25 = (f32[64,128]{1,0:T(8,128)S(1)}, f32[64,128]{1,0:T(8,128)S(1)}, u32[]{:S(2)}, u32[]{:S(2)}) collective-permute-start(f32[64,128]{1,0:T(8,128)S(1)} %get-tuple-element.46), channel_id=1, source_target_pairs={{0,248},{8,0},{16,8},{24,16},{32,24},{40,32},{48,40},{56,48},{64,5... | collective-permute-start | bytes 98312 | tf_op jit(solution)/shard_map/ppermute | solution.py:222
  43.7 3.3 %collective-permute-start.23 = (f32[64,128]{1,0:T(8,128)S(1)}, f32[64,128]{1,0:T(8,128)S(1)}, u32[]{:S(2)}, u32[]{:S(2)}) collective-permute-start(f32[64,128]{1,0:T(8,128)S(1)} %get-tuple-element.44), channel_id=1, source_target_pairs={{0,4},{1,5},{2,6},{3,7},{4,0},{5,1},{6,2},{7,3},{8,12},{9,13},{10,... | collective-permute-start | bytes 98312 | tf_op jit(solution)/shard_map/ppermute | solution.py:217
  47.0 1.3 %collective-permute-start.24 = (f32[64,128]{1,0:T(8,128)S(1)}, f32[64,128]{1,0:T(8,128)S(1)}, u32[]{:S(2)}, u32[]{:S(2)}) collective-permute-start(f32[64,128]{1,0:T(8,128)S(1)} %get-tuple-element.45), channel_id=1, source_target_pairs={{0,6},{1,7},{2,4},{3,5},{4,2},{5,3},{6,0},{7,1},{8,14},{9,15},{10,... | collective-permute-start | bytes 98312 | tf_op jit(solution)/shard_map/ppermute | solution.py:217
  48.4 0.9 collective-permute-done.23.refs_2_
  49.3 2.9 %collective-permute-done.24.refs_3_ = f32[64,128]{1,0:T(8,128)S(1)} collective-permute-done((f32[64,128]{1,0:T(8,128)S(1)}, f32[64,128]{1,0:T(8,128)S(1)}, u32[]{:S(2)}, u32[]{:S(2)}) %collective-permute-start.24) | collective-permute-done | bytes 32800 | tf_op jit(solution)/shard_map/ppermute | solution.py:217
  52.2 1.4 %collective-permute-start.29 = (f32[64,128]{1,0:T(8,128)S(1)}, f32[64,128]{1,0:T(8,128)S(1)}, u32[]{:S(2)}, u32[]{:S(2)}) collective-permute-start(f32[64,128]{1,0:T(8,128)S(1)} %shard_map.120.refs_0_.refs_7_), channel_id=1, source_target_pairs={{0,6},{1,7},{2,4},{3,5},{4,2},{5,3},{6,0},{7,1},{8,14},{9,15},{10,... | collective-permute-start | bytes 98312 | tf_op jit(solution)/shard_map/ppermute | solution.py:217
  53.6 2.8 %collective-permute-start.27 = (f32[64,128]{1,0:T(8,128)S(1)}, f32[64,128]{1,0:T(8,128)S(1)}, u32[]{:S(2)}, u32[]{:S(2)}) collective-permute-start(f32[64,128]{1,0:T(8,128)S(1)} %shard_map.120.refs_0_.refs_7_), channel_id=1, source_target_pairs={{0,2},{1,3},{2,0},{3,1},{4,6},{5,7},{6,4},{7,5},{8,10},{9,11},{10,... | collective-permute-start | bytes 98312 | tf_op jit(solution)/shard_map/ppermute | solution.py:217
  56.4 1.0 %collective-permute-done.29.refs_3_ = f32[64,128]{1,0:T(8,128)S(1)} collective-permute-done((f32[64,128]{1,0:T(8,128)S(1)}, f32[64,128]{1,0:T(8,128)S(1)}, u32[]{:S(2)}, u32[]{:S(2)}) %collective-permute-start.29) | collective-permute-done | bytes 32800 | tf_op jit(solution)/shard_map/ppermute | solution.py:217
  57.4 1.6 %collective-permute-done.28.refs_2_ = f32[64,128]{1,0:T(8,128)S(1)} collective-permute-done((f32[64,128]{1,0:T(8,128)S(1)}, f32[64,128]{1,0:T(8,128)S(1)}, u32[]{:S(2)}, u32[]{:S(2)}) %collective-permute-start.28) | collective-permute-done | bytes 32800 | tf_op jit(solution)/shard_map/ppermute | solution.py:217
  59.0 0.5 collective-permute-start.31
  59.5 0.7 collective-permute-done.26.before_ref
  60.4 1.8 %shard_map.121 = (f32[288,128]{1,0:T(8,128)S(1)}, f32[288,128]{1,0:T(8,128)S(1)}, f32[64,128]{1,0:T(8,128)S(1)}, f32[8,128]{1,0:T(8,128)}) custom-call(bf16[512,96]{1,0:T(8,128)(2,1)S(1)} %get-tuple-element.29.hot_in, bf16[128,48]{1,0:T(8,128)(2,1)S(1)} %get-tuple-element.30.hot_ex, bf16[1,1,96,128,128]{4,3,2,1,0:T(8,128)(2,1)S(1)} %copy-done, ...), custom_call_target="tpu_custom_call" | custom-call | tf_op jit(solution)/shard_map/pallas_call | solution.py:205
  62.2 0.3 collective-permute-start.34
  62.5 1.0 %collective-permute-done.34.got_ref = f32[288,128]{1,0:T(8,128)S(1)} collective-permute-done((f32[288,128]{1,0:T(8,128)S(1)}, f32[288,128]{1,0:T(8,128)S(1)}, u32[]{:S(2)}, u32[]{:S(2)}) %collective-permute-start.34) | collective-permute-done | bytes 147488 | tf_op jit(solution)/shard_map/ppermute | solution.py:217
  63.6 1.2 %collective-permute-start.35 = (f32[72,128]{1,0:T(8,128)S(1)}, f32[72,128]{1,0:T(8,128)S(1)}, u32[]{:S(2)}, u32[]{:S(2)}) collective-permute-start(f32[72,128]{1,0:T(8,128)S(1)} %get-tuple-element.50), channel_id=1, source_target_pairs={{0,2},{1,3},{2,0},{3,1},{4,6},{5,7},{6,4},{7,5},{8,10},{9,11},{10,... | collective-permute-start | bytes 110600 | tf_op jit(solution)/shard_map/ppermute | solution.py:217
  64.8 2.3 %collective-permute-start.36 = (f32[72,128]{1,0:T(8,128)S(1)}, f32[72,128]{1,0:T(8,128)S(1)}, u32[]{:S(2)}, u32[]{:S(2)}) collective-permute-start(f32[72,128]{1,0:T(8,128)S(1)} %get-tuple-element.51), channel_id=1, source_target_pairs={{0,4},{1,5},{2,6},{3,7},{4,0},{5,1},{6,2},{7,3},{8,12},{9,13},{10,... | collective-permute-start | bytes 110600 | tf_op jit(solution)/shard_map/ppermute | solution.py:217
  67.0 1.3 %collective-permute-start.37 = (f32[72,128]{1,0:T(8,128)S(1)}, f32[72,128]{1,0:T(8,128)S(1)}, u32[]{:S(2)}, u32[]{:S(2)}) collective-permute-start(f32[72,128]{1,0:T(8,128)S(1)} %get-tuple-element.52), channel_id=1, source_target_pairs={{0,6},{1,7},{2,4},{3,5},{4,2},{5,3},{6,0},{7,1},{8,14},{9,15},{10,... | collective-permute-start | bytes 110600 | tf_op jit(solution)/shard_map/ppermute | solution.py:217
  68.4 1.8 %collective-permute-done.36.refs_2_ = f32[72,128]{1,0:T(8,128)S(1)} collective-permute-done((f32[72,128]{1,0:T(8,128)S(1)}, f32[72,128]{1,0:T(8,128)S(1)}, u32[]{:S(2)}, u32[]{:S(2)}) %collective-permute-start.36) | collective-permute-done | bytes 36896 | tf_op jit(solution)/shard_map/ppermute | solution.py:217
  70.2 2.0 %collective-permute-done.37.refs_3_ = f32[72,128]{1,0:T(8,128)S(1)} collective-permute-done((f32[72,128]{1,0:T(8,128)S(1)}, f32[72,128]{1,0:T(8,128)S(1)}, u32[]{:S(2)}, u32[]{:S(2)}) %collective-permute-start.37) | collective-permute-done | bytes 36896 | tf_op jit(solution)/shard_map/ppermute | solution.py:217
  72.2 0.7 shard_map.123
  72.9 7.4 %all-to-all-start = ((f32[32,8,128]{2,1,0:T(8,128)}), f32[32,8,128]{2,1,0:T(8,128)S(1)}, u32[]{:S(2)}, u32[]{:S(2)}) async-start(f32[32,8,128]{2,1,0:T(8,128)} %shard_map.123), calls=%async_computation | async-start | bytes 262144 | tf_op jit(solution)/shard_map/all_to_all | solution.py:276
  80.3 0.4 collective-permute-start.38
  80.7 3.7 %collective-permute-done.38.refs_4_ = f32[64,128]{1,0:T(8,128)S(1)} collective-permute-done((f32[64,128]{1,0:T(8,128)S(1)}, f32[64,128]{1,0:T(8,128)S(1)}, u32[]{:S(2)}, u32[]{:S(2)}) %collective-permute-start.38) | collective-permute-done | bytes 32800 | tf_op jit(solution)/shard_map/ppermute | solution.py:222
  84.4 5.7 %all-to-all-done.sums_ref = f32[32,8,128]{2,1,0:T(8,128)S(1)} async-done(((f32[32,8,128]{2,1,0:T(8,128)}), f32[32,8,128]{2,1,0:T(8,128)S(1)}, u32[]{:S(2)}, u32[]{:S(2)}) %all-to-all-start) | async-done | bytes 131104 | tf_op jit(solution)/shard_map/all_to_all | solution.py:276
  90.1 0.9 shard_map.124
  (65 shorter events, 1.0 us)
Async XLA Ops:
  0.6 10.6 %copy-start.6 = (s32[1,1,96]{2,1,0:T(1,128)S(1)}, s32[1,1,96]{2,1,0:T(1,128)}, u32[]{:S(2)}) copy-start(s32[1,1,96]{2,1,0:T(1,128)} %refs_0_.1) | copy-start | bytes 1156
  0.6 10.6 %copy-start.7 = (s32[1,1,96]{2,1,0:T(1,128)S(1)}, s32[1,1,96]{2,1,0:T(1,128)}, u32[]{:S(2)}) copy-start(s32[1,1,96]{2,1,0:T(1,128)} %refs_1_.1) | copy-start | bytes 1156
  0.7 10.6 %copy-start.8 = (s32[1,1,48]{2,1,0:T(1,128)S(1)}, s32[1,1,48]{2,1,0:T(1,128)}, u32[]{:S(2)}) copy-start(s32[1,1,48]{2,1,0:T(1,128)} %refs_2_.1) | copy-start | bytes 580
  0.7 10.8 %copy-start = (bf16[1,1,96,128,128]{4,3,2,1,0:T(8,128)(2,1)S(1)}, bf16[1,1,96,128,128]{4,3,2,1,0:T(8,128)(2,1)}, u32[]{:S(2)}) copy-start(bf16[1,1,96,128,128]{4,3,2,1,0:T(8,128)(2,1)} %in_ref.5) | copy-start | bytes 9437188
  0.7 10.8 %copy-start.3 = (f32[1,1,64,128]{3,2,1,0:T(8,128)S(1)}, f32[1,1,64,128]{3,2,1,0:T(8,128)}, u32[]{:S(2)}) copy-start(f32[1,1,64,128]{3,2,1,0:T(8,128)} %param.11) | copy-start | bytes 98308
  0.7 7.1 %collective-permute-start.3 = (f32[64,128]{1,0:T(8,128)}, f32[64,128]{1,0:T(8,128)S(1)}, u32[]{:S(2)}, u32[]{:S(2)}) collective-permute-start(f32[64,128]{1,0:T(8,128)} %bitcast.13), channel_id=1, source_target_pairs={{0,6},{1,7},{2,4},{3,5},{4,2},{5,3},{6,0},{7,1},{8,14},{9,15},{10,... | collective-permute-start | bytes 98312 | tf_op jit(solution)/shard_map/ppermute | solution.py:217
  3.8 5.6 %collective-permute-start.2 = (f32[64,128]{1,0:T(8,128)}, f32[64,128]{1,0:T(8,128)S(1)}, u32[]{:S(2)}, u32[]{:S(2)}) collective-permute-start(f32[64,128]{1,0:T(8,128)} %bitcast.14), channel_id=1, source_target_pairs={{0,4},{1,5},{2,6},{3,7},{4,0},{5,1},{6,2},{7,3},{8,12},{9,13},{10,... | collective-permute-start | bytes 98312 | tf_op jit(solution)/shard_map/ppermute | solution.py:217
  4.4 5.0 %collective-permute-start.1 = (f32[64,128]{1,0:T(8,128)}, f32[64,128]{1,0:T(8,128)S(1)}, u32[]{:S(2)}, u32[]{:S(2)}) collective-permute-start(f32[64,128]{1,0:T(8,128)} %bitcast.15), channel_id=1, source_target_pairs={{0,2},{1,3},{2,0},{3,1},{4,6},{5,7},{6,4},{7,5},{8,10},{9,11},{10,... | collective-permute-start | bytes 98312 | tf_op jit(solution)/shard_map/ppermute | solution.py:217
  5.7 5.6 %copy-start.9 = (s32[1,1,48]{2,1,0:T(1,128)S(1)}, s32[1,1,48]{2,1,0:T(1,128)}, u32[]{:S(2)}) copy-start(s32[1,1,48]{2,1,0:T(1,128)} %refs_3_.1) | copy-start | bytes 580
  5.7 5.8 %copy-start.5 = (f32[1,1,64,128]{3,2,1,0:T(8,128)S(1)}, f32[1,1,64,128]{3,2,1,0:T(8,128)}, u32[]{:S(2)}) copy-start(f32[1,1,64,128]{3,2,1,0:T(8,128)} %param.10) | copy-start | bytes 98308
  5.7 5.7 %collective-permute-start.4 = (f32[64,128]{1,0:T(8,128)S(1)}, f32[64,128]{1,0:T(8,128)S(1)}, u32[]{:S(2)}, u32[]{:S(2)}) collective-permute-start(f32[64,128]{1,0:T(8,128)S(1)} %shard_map.114), channel_id=1, source_target_pairs={{0,1},{1,0},{2,3},{3,2},{4,5},{5,4},{6,7},{7,6},{8,9},{9,8},{10,11... | collective-permute-start | bytes 98312 | tf_op jit(solution)/shard_map/ppermute | solution.py:217
  5.8 5.6 %collective-permute-start = (f32[64,128]{1,0:T(8,128)S(1)}, f32[64,128]{1,0:T(8,128)S(1)}, u32[]{:S(2)}, u32[]{:S(2)}) collective-permute-start(f32[64,128]{1,0:T(8,128)S(1)} %shard_map.114), channel_id=1, source_target_pairs={{0,8},{8,16},{16,24},{24,32},{32,40},{40,48},{48,56},{56,64},{64,7... | collective-permute-start | bytes 98312 | tf_op jit(solution)/shard_map/ppermute | solution.py:222
  7.8 3.7 %collective-permute-start.7 = (f32[64,128]{1,0:T(8,128)S(1)}, f32[64,128]{1,0:T(8,128)S(1)}, u32[]{:S(2)}, u32[]{:S(2)}) collective-permute-start(f32[64,128]{1,0:T(8,128)S(1)} %collective-permute-done.3.refs_3_), channel_id=1, source_target_pairs={{0,1},{1,0},{2,3},{3,2},{4,5},{5,4},{6,7},{7,6},{8,9},{9,8},{10,11... | collective-permute-start | bytes 98312 | tf_op jit(solution)/shard_map/ppermute | solution.py:217
  9.4 2.0 %collective-permute-start.6 = (f32[64,128]{1,0:T(8,128)S(1)}, f32[64,128]{1,0:T(8,128)S(1)}, u32[]{:S(2)}, u32[]{:S(2)}) collective-permute-start(f32[64,128]{1,0:T(8,128)S(1)} %collective-permute-done.2.refs_2_), channel_id=1, source_target_pairs={{0,1},{1,0},{2,3},{3,2},{4,5},{5,4},{6,7},{7,6},{8,9},{9,8},{10,11... | collective-permute-start | bytes 98312 | tf_op jit(solution)/shard_map/ppermute | solution.py:217
  9.4 2.0 %collective-permute-start.5 = (f32[64,128]{1,0:T(8,128)S(1)}, f32[64,128]{1,0:T(8,128)S(1)}, u32[]{:S(2)}, u32[]{:S(2)}) collective-permute-start(f32[64,128]{1,0:T(8,128)S(1)} %collective-permute-done.1.refs_1_), channel_id=1, source_target_pairs={{0,1},{1,0},{2,3},{3,2},{4,5},{5,4},{6,7},{7,6},{8,9},{9,8},{10,11... | collective-permute-start | bytes 98312 | tf_op jit(solution)/shard_map/ppermute | solution.py:217
  12.9 24.0 %copy-start.2 = (bf16[1,1,48,128,128]{4,3,2,1,0:T(8,128)(2,1)S(1)}, bf16[1,1,48,128,128]{4,3,2,1,0:T(8,128)(2,1)}, u32[]{:S(2)}) copy-start(bf16[1,1,48,128,128]{4,3,2,1,0:T(8,128)(2,1)} %ex_ref.5) | copy-start | bytes 4718596
  14.2 4.7 %collective-permute-start.8 = (f32[256,128]{1,0:T(8,128)S(1)}, f32[256,128]{1,0:T(8,128)S(1)}, u32[]{:S(2)}, u32[]{:S(2)}) collective-permute-start(f32[256,128]{1,0:T(8,128)S(1)} %get-tuple-element.33), channel_id=1, source_target_pairs={{0,1},{1,0},{2,3},{3,2},{4,5},{5,4},{6,7},{7,6},{8,9},{9,8},{10,11... | collective-permute-start | bytes 393224 | tf_op jit(solution)/shard_map/ppermute | solution.py:217
  14.3 9.4 %collective-permute-start.12 = (f32[64,128]{1,0:T(8,128)S(1)}, f32[64,128]{1,0:T(8,128)S(1)}, u32[]{:S(2)}, u32[]{:S(2)}) collective-permute-start(f32[64,128]{1,0:T(8,128)S(1)} %get-tuple-element.38), channel_id=1, source_target_pairs={{0,248},{8,0},{16,8},{24,16},{32,24},{40,32},{48,40},{56,48},{64,5... | collective-permute-start | bytes 98312 | tf_op jit(solution)/shard_map/ppermute | solution.py:222
  19.0 4.8 %collective-permute-start.9 = (f32[64,128]{1,0:T(8,128)S(1)}, f32[64,128]{1,0:T(8,128)S(1)}, u32[]{:S(2)}, u32[]{:S(2)}) collective-permute-start(f32[64,128]{1,0:T(8,128)S(1)} %get-tuple-element.35), channel_id=1, source_target_pairs={{0,2},{1,3},{2,0},{3,1},{4,6},{5,7},{6,4},{7,5},{8,10},{9,11},{10,... | collective-permute-start | bytes 98312 | tf_op jit(solution)/shard_map/ppermute | solution.py:217
  20.6 5.4 %collective-permute-start.10 = (f32[64,128]{1,0:T(8,128)S(1)}, f32[64,128]{1,0:T(8,128)S(1)}, u32[]{:S(2)}, u32[]{:S(2)}) collective-permute-start(f32[64,128]{1,0:T(8,128)S(1)} %get-tuple-element.36), channel_id=1, source_target_pairs={{0,4},{1,5},{2,6},{3,7},{4,0},{5,1},{6,2},{7,3},{8,12},{9,13},{10,... | collective-permute-start | bytes 98312 | tf_op jit(solution)/shard_map/ppermute | solution.py:217
  23.5 5.1 %collective-permute-start.11 = (f32[64,128]{1,0:T(8,128)S(1)}, f32[64,128]{1,0:T(8,128)S(1)}, u32[]{:S(2)}, u32[]{:S(2)}) collective-permute-start(f32[64,128]{1,0:T(8,128)S(1)} %get-tuple-element.37), channel_id=1, source_target_pairs={{0,6},{1,7},{2,4},{3,5},{4,2},{5,3},{6,0},{7,1},{8,14},{9,15},{10,... | collective-permute-start | bytes 98312 | tf_op jit(solution)/shard_map/ppermute | solution.py:217
  28.7 5.2 %collective-permute-start.16 = (f32[64,128]{1,0:T(8,128)S(1)}, f32[64,128]{1,0:T(8,128)S(1)}, u32[]{:S(2)}, u32[]{:S(2)}) collective-permute-start(f32[64,128]{1,0:T(8,128)S(1)} %shard_map.117.refs_0_.refs_6_), channel_id=1, source_target_pairs={{0,6},{1,7},{2,4},{3,5},{4,2},{5,3},{6,0},{7,1},{8,14},{9,15},{10,... | collective-permute-start | bytes 98312 | tf_op jit(solution)/shard_map/ppermute | solution.py:217
  29.0 5.4 %collective-permute-start.15 = (f32[64,128]{1,0:T(8,128)S(1)}, f32[64,128]{1,0:T(8,128)S(1)}, u32[]{:S(2)}, u32[]{:S(2)}) collective-permute-start(f32[64,128]{1,0:T(8,128)S(1)} %shard_map.117.refs_0_.refs_6_), channel_id=1, source_target_pairs={{0,4},{1,5},{2,6},{3,7},{4,0},{5,1},{6,2},{7,3},{8,12},{9,13},{10,... | collective-permute-start | bytes 98312 | tf_op jit(solution)/shard_map/ppermute | solution.py:217
  29.8 5.3 %collective-permute-start.14 = (f32[64,128]{1,0:T(8,128)S(1)}, f32[64,128]{1,0:T(8,128)S(1)}, u32[]{:S(2)}, u32[]{:S(2)}) collective-permute-start(f32[64,128]{1,0:T(8,128)S(1)} %shard_map.117.refs_0_.refs_6_), channel_id=1, source_target_pairs={{0,2},{1,3},{2,0},{3,1},{4,6},{5,7},{6,4},{7,5},{8,10},{9,11},{10,... | collective-permute-start | bytes 98312 | tf_op jit(solution)/shard_map/ppermute | solution.py:217
  32.8 2.2 %collective-permute-start.17 = (f32[64,128]{1,0:T(8,128)S(1)}, f32[64,128]{1,0:T(8,128)S(1)}, u32[]{:S(2)}, u32[]{:S(2)}) collective-permute-start(f32[64,128]{1,0:T(8,128)S(1)} %shard_map.117.refs_0_.refs_6_), channel_id=1, source_target_pairs={{0,1},{1,0},{2,3},{3,2},{4,5},{5,4},{6,7},{7,6},{8,9},{9,8},{10,11... | collective-permute-start | bytes 98312 | tf_op jit(solution)/shard_map/ppermute | solution.py:217
  32.9 4.0 %collective-permute-start.13 = (f32[64,128]{1,0:T(8,128)S(1)}, f32[64,128]{1,0:T(8,128)S(1)}, u32[]{:S(2)}, u32[]{:S(2)}) collective-permute-start(f32[64,128]{1,0:T(8,128)S(1)} %shard_map.117.refs_0_.refs_6_), channel_id=1, source_target_pairs={{0,8},{8,16},{16,24},{24,32},{32,40},{40,48},{48,56},{56,64},{64,7... | collective-permute-start | bytes 98312 | tf_op jit(solution)/shard_map/ppermute | solution.py:222
  33.9 3.0 %collective-permute-start.20 = (f32[64,128]{1,0:T(8,128)S(1)}, f32[64,128]{1,0:T(8,128)S(1)}, u32[]{:S(2)}, u32[]{:S(2)}) collective-permute-start(f32[64,128]{1,0:T(8,128)S(1)} %collective-permute-done.16.refs_3_), channel_id=1, source_target_pairs={{0,1},{1,0},{2,3},{3,2},{4,5},{5,4},{6,7},{7,6},{8,9},{9,8},{10,11... | collective-permute-start | bytes 98312 | tf_op jit(solution)/shard_map/ppermute | solution.py:217
  34.4 2.5 %collective-permute-start.19 = (f32[64,128]{1,0:T(8,128)S(1)}, f32[64,128]{1,0:T(8,128)S(1)}, u32[]{:S(2)}, u32[]{:S(2)}) collective-permute-start(f32[64,128]{1,0:T(8,128)S(1)} %collective-permute-done.15.refs_2_), channel_id=1, source_target_pairs={{0,1},{1,0},{2,3},{3,2},{4,5},{5,4},{6,7},{7,6},{8,9},{9,8},{10,11... | collective-permute-start | bytes 98312 | tf_op jit(solution)/shard_map/ppermute | solution.py:217
  35.1 1.8 %collective-permute-start.18 = (f32[64,128]{1,0:T(8,128)S(1)}, f32[64,128]{1,0:T(8,128)S(1)}, u32[]{:S(2)}, u32[]{:S(2)}) collective-permute-start(f32[64,128]{1,0:T(8,128)S(1)} %collective-permute-done.14.refs_1_), channel_id=1, source_target_pairs={{0,1},{1,0},{2,3},{3,2},{4,5},{5,4},{6,7},{7,6},{8,9},{9,8},{10,11... | collective-permute-start | bytes 98312 | tf_op jit(solution)/shard_map/ppermute | solution.py:217
  38.2 5.4 %collective-permute-start.21 = (f32[256,128]{1,0:T(8,128)S(1)}, f32[256,128]{1,0:T(8,128)S(1)}, u32[]{:S(2)}, u32[]{:S(2)}) collective-permute-start(f32[256,128]{1,0:T(8,128)S(1)} %get-tuple-element.41), channel_id=1, source_target_pairs={{0,1},{1,0},{2,3},{3,2},{4,5},{5,4},{6,7},{7,6},{8,9},{9,8},{10,11... | collective-permute-start | bytes 393224 | tf_op jit(solution)/shard_map/ppermute | solution.py:217
  38.3 10.1 %collective-permute-start.25 = (f32[64,128]{1,0:T(8,128)S(1)}, f32[64,128]{1,0:T(8,128)S(1)}, u32[]{:S(2)}, u32[]{:S(2)}) collective-permute-start(f32[64,128]{1,0:T(8,128)S(1)} %get-tuple-element.46), channel_id=1, source_target_pairs={{0,248},{8,0},{16,8},{24,16},{32,24},{40,32},{48,40},{56,48},{64,5... | collective-permute-start | bytes 98312 | tf_op jit(solution)/shard_map/ppermute | solution.py:222
  43.6 4.8 %collective-permute-start.22 = (f32[64,128]{1,0:T(8,128)S(1)}, f32[64,128]{1,0:T(8,128)S(1)}, u32[]{:S(2)}, u32[]{:S(2)}) collective-permute-start(f32[64,128]{1,0:T(8,128)S(1)} %get-tuple-element.43), channel_id=1, source_target_pairs={{0,2},{1,3},{2,0},{3,1},{4,6},{5,7},{6,4},{7,5},{8,10},{9,11},{10,... | collective-permute-start | bytes 98312 | tf_op jit(solution)/shard_map/ppermute | solution.py:217
  43.7 5.6 %collective-permute-start.23 = (f32[64,128]{1,0:T(8,128)S(1)}, f32[64,128]{1,0:T(8,128)S(1)}, u32[]{:S(2)}, u32[]{:S(2)}) collective-permute-start(f32[64,128]{1,0:T(8,128)S(1)} %get-tuple-element.44), channel_id=1, source_target_pairs={{0,4},{1,5},{2,6},{3,7},{4,0},{5,1},{6,2},{7,3},{8,12},{9,13},{10,... | collective-permute-start | bytes 98312 | tf_op jit(solution)/shard_map/ppermute | solution.py:217
  47.0 5.1 %collective-permute-start.24 = (f32[64,128]{1,0:T(8,128)S(1)}, f32[64,128]{1,0:T(8,128)S(1)}, u32[]{:S(2)}, u32[]{:S(2)}) collective-permute-start(f32[64,128]{1,0:T(8,128)S(1)} %get-tuple-element.45), channel_id=1, source_target_pairs={{0,6},{1,7},{2,4},{3,5},{4,2},{5,3},{6,0},{7,1},{8,14},{9,15},{10,... | collective-permute-start | bytes 98312 | tf_op jit(solution)/shard_map/ppermute | solution.py:217
  52.2 5.2 %collective-permute-start.29 = (f32[64,128]{1,0:T(8,128)S(1)}, f32[64,128]{1,0:T(8,128)S(1)}, u32[]{:S(2)}, u32[]{:S(2)}) collective-permute-start(f32[64,128]{1,0:T(8,128)S(1)} %shard_map.120.refs_0_.refs_7_), channel_id=1, source_target_pairs={{0,6},{1,7},{2,4},{3,5},{4,2},{5,3},{6,0},{7,1},{8,14},{9,15},{10,... | collective-permute-start | bytes 98312 | tf_op jit(solution)/shard_map/ppermute | solution.py:217
  53.6 5.4 %collective-permute-start.28 = (f32[64,128]{1,0:T(8,128)S(1)}, f32[64,128]{1,0:T(8,128)S(1)}, u32[]{:S(2)}, u32[]{:S(2)}) collective-permute-start(f32[64,128]{1,0:T(8,128)S(1)} %shard_map.120.refs_0_.refs_7_), channel_id=1, source_target_pairs={{0,4},{1,5},{2,6},{3,7},{4,0},{5,1},{6,2},{7,3},{8,12},{9,13},{10,... | collective-permute-start | bytes 98312 | tf_op jit(solution)/shard_map/ppermute | solution.py:217
  53.6 5.4 %collective-permute-start.27 = (f32[64,128]{1,0:T(8,128)S(1)}, f32[64,128]{1,0:T(8,128)S(1)}, u32[]{:S(2)}, u32[]{:S(2)}) collective-permute-start(f32[64,128]{1,0:T(8,128)S(1)} %shard_map.120.refs_0_.refs_7_), channel_id=1, source_target_pairs={{0,2},{1,3},{2,0},{3,1},{4,6},{5,7},{6,4},{7,5},{8,10},{9,11},{10,... | collective-permute-start | bytes 98312 | tf_op jit(solution)/shard_map/ppermute | solution.py:217
  56.4 3.2 %collective-permute-start.30 = (f32[64,128]{1,0:T(8,128)S(1)}, f32[64,128]{1,0:T(8,128)S(1)}, u32[]{:S(2)}, u32[]{:S(2)}) collective-permute-start(f32[64,128]{1,0:T(8,128)S(1)} %shard_map.120.refs_0_.refs_7_), channel_id=1, source_target_pairs={{0,1},{1,0},{2,3},{3,2},{4,5},{5,4},{6,7},{7,6},{8,9},{9,8},{10,11... | collective-permute-start | bytes 98312 | tf_op jit(solution)/shard_map/ppermute | solution.py:217
  56.4 3.9 %collective-permute-start.26 = (f32[64,128]{1,0:T(8,128)S(1)}, f32[64,128]{1,0:T(8,128)S(1)}, u32[]{:S(2)}, u32[]{:S(2)}) collective-permute-start(f32[64,128]{1,0:T(8,128)S(1)} %shard_map.120.refs_0_.refs_7_), channel_id=1, source_target_pairs={{0,8},{8,16},{16,24},{24,32},{32,40},{40,48},{48,56},{56,64},{64,7... | collective-permute-start | bytes 98312 | tf_op jit(solution)/shard_map/ppermute | solution.py:222
  57.4 2.9 %collective-permute-start.33 = (f32[64,128]{1,0:T(8,128)S(1)}, f32[64,128]{1,0:T(8,128)S(1)}, u32[]{:S(2)}, u32[]{:S(2)}) collective-permute-start(f32[64,128]{1,0:T(8,128)S(1)} %collective-permute-done.29.refs_3_), channel_id=1, source_target_pairs={{0,1},{1,0},{2,3},{3,2},{4,5},{5,4},{6,7},{7,6},{8,9},{9,8},{10,11... | collective-permute-start | bytes 98312 | tf_op jit(solution)/shard_map/ppermute | solution.py:217
  59.0 1.3 %collective-permute-start.32 = (f32[64,128]{1,0:T(8,128)S(1)}, f32[64,128]{1,0:T(8,128)S(1)}, u32[]{:S(2)}, u32[]{:S(2)}) collective-permute-start(f32[64,128]{1,0:T(8,128)S(1)} %collective-permute-done.28.refs_2_), channel_id=1, source_target_pairs={{0,1},{1,0},{2,3},{3,2},{4,5},{5,4},{6,7},{7,6},{8,9},{9,8},{10,11... | collective-permute-start | bytes 98312 | tf_op jit(solution)/shard_map/ppermute | solution.py:217
  59.0 1.4 %collective-permute-start.31 = (f32[64,128]{1,0:T(8,128)S(1)}, f32[64,128]{1,0:T(8,128)S(1)}, u32[]{:S(2)}, u32[]{:S(2)}) collective-permute-start(f32[64,128]{1,0:T(8,128)S(1)} %collective-permute-done.27.refs_1_), channel_id=1, source_target_pairs={{0,1},{1,0},{2,3},{3,2},{4,5},{5,4},{6,7},{7,6},{8,9},{9,8},{10,11... | collective-permute-start | bytes 98312 | tf_op jit(solution)/shard_map/ppermute | solution.py:217
  62.2 1.4 %collective-permute-start.34 = (f32[288,128]{1,0:T(8,128)S(1)}, f32[288,128]{1,0:T(8,128)S(1)}, u32[]{:S(2)}, u32[]{:S(2)}) collective-permute-start(f32[288,128]{1,0:T(8,128)S(1)} %get-tuple-element.48), channel_id=1, source_target_pairs={{0,1},{1,0},{2,3},{3,2},{4,5},{5,4},{6,7},{7,6},{8,9},{9,8},{10,11... | collective-permute-start | bytes 442376 | tf_op jit(solution)/shard_map/ppermute | solution.py:217
  63.6 4.8 %collective-permute-start.35 = (f32[72,128]{1,0:T(8,128)S(1)}, f32[72,128]{1,0:T(8,128)S(1)}, u32[]{:S(2)}, u32[]{:S(2)}) collective-permute-start(f32[72,128]{1,0:T(8,128)S(1)} %get-tuple-element.50), channel_id=1, source_target_pairs={{0,2},{1,3},{2,0},{3,1},{4,6},{5,7},{6,4},{7,5},{8,10},{9,11},{10,... | collective-permute-start | bytes 110600 | tf_op jit(solution)/shard_map/ppermute | solution.py:217
  64.8 5.5 %collective-permute-start.36 = (f32[72,128]{1,0:T(8,128)S(1)}, f32[72,128]{1,0:T(8,128)S(1)}, u32[]{:S(2)}, u32[]{:S(2)}) collective-permute-start(f32[72,128]{1,0:T(8,128)S(1)} %get-tuple-element.51), channel_id=1, source_target_pairs={{0,4},{1,5},{2,6},{3,7},{4,0},{5,1},{6,2},{7,3},{8,12},{9,13},{10,... | collective-permute-start | bytes 110600 | tf_op jit(solution)/shard_map/ppermute | solution.py:217
  67.0 5.2 %collective-permute-start.37 = (f32[72,128]{1,0:T(8,128)S(1)}, f32[72,128]{1,0:T(8,128)S(1)}, u32[]{:S(2)}, u32[]{:S(2)}) collective-permute-start(f32[72,128]{1,0:T(8,128)S(1)} %get-tuple-element.52), channel_id=1, source_target_pairs={{0,6},{1,7},{2,4},{3,5},{4,2},{5,3},{6,0},{7,1},{8,14},{9,15},{10,... | collective-permute-start | bytes 110600 | tf_op jit(solution)/shard_map/ppermute | solution.py:217
  72.9 17.2 %all-to-all-start = ((f32[32,8,128]{2,1,0:T(8,128)}), f32[32,8,128]{2,1,0:T(8,128)S(1)}, u32[]{:S(2)}, u32[]{:S(2)}) async-start(f32[32,8,128]{2,1,0:T(8,128)} %shard_map.123), calls=%async_computation | async-start | bytes 262144 | tf_op jit(solution)/shard_map/all_to_all | solution.py:276
  80.3 4.1 %collective-permute-start.38 = (f32[64,128]{1,0:T(8,128)S(1)}, f32[64,128]{1,0:T(8,128)S(1)}, u32[]{:S(2)}, u32[]{:S(2)}) collective-permute-start(f32[64,128]{1,0:T(8,128)S(1)} %get-tuple-element.53), channel_id=1, source_target_pairs={{0,248},{8,0},{16,8},{24,16},{32,24},{40,32},{48,40},{56,48},{64,5... | collective-permute-start | bytes 98312 | tf_op jit(solution)/shard_map/ppermute | solution.py:222
  (2 other events, 2.2 us)

commit v3 on v2

--- a/solution.py
+++ b/solution.py
@@ -8,10 +8,9 @@
 from jax.sharding import PartitionSpec as P
 
 ITERS = 3
+LARGE, ROUNDS = 1e37, 8
 ROWS = 8
-HOTFLOPS = 20000000000
-OPFLOPS = 0
-SCATTER = "three"
+PASS_FLOPS = 20_000_000_000
 F32, BF16 = jnp.float32, jnp.bfloat16
 VMEM = pl.BlockSpec(memory_space=pltpu.VMEM)
 CONTRACT_ROWS = (((0,), (0,)), ((), ()))
@@ -28,7 +27,7 @@
     return x[:, :half] + x[:, half:]
 
 
-def springs(hot, field, stiff_ref, u_ref):
+def springs(hot, field, stiff_ref, scale, u_ref):
     slots, node = u_ref.shape
     diff = fold(lax.dot_general(hot, split(field), CONTRACT_ROWS, preferred_element_type=F32))
     rows = lax.broadcasted_iota(jnp.int32, (2 * GROUP, GROUP * node), 0) % GROUP
@@ -42,7 +41,7 @@
         block = stiff_ref[0, 0, start : start + GROUP].reshape(GROUP * node, node)
         got = jnp.dot(wide, block, preferred_element_type=F32)
         u_ref[start : start + GROUP, :] = got[:GROUP] + got[GROUP:]
-    u = u_ref[...]
+    u = u_ref[...] * scale
     spread = fold(jnp.dot(hot, split(u), preferred_element_type=F32))
     return spread, jnp.sum(diff * u, axis=0, keepdims=True)
 
@@ -79,7 +78,7 @@
 
 def hot_kernel(section, tile, count, count_ex, *refs):
     own, far, near, prev = [r[...] for r in refs[:4]]
-    hot_in, hot_ex = refs[4:]
+    hot_in, hot_ex = refs[5:]
     blk = hot_ex.shape[0] // 2
     far = far[0]
     there = tile[0] ^ (far // blk)
@@ -88,20 +87,27 @@
     hot_ex[...] = one_hot(near[0], prev[0] + blk, count_ex[0], 2 * blk, section[0] > 0)
 
 
-def pass_kernel(v_ref, out_ref):
+def zero_kernel(*outs):
+    for out in outs:
+        out[...] = jnp.zeros(out.shape, F32)
+
+
+def pass_kernel(inverse, v_ref, out_ref, scale_ref):
     out_ref[...] = v_ref[...]
-
-
-def operator_kernel(step, n_fields, hot_in, hot_ex, in_ref, ex_ref, anchor_ref, row_ref, before_ref, *refs):
+    scale_ref[...] = jnp.full(scale_ref.shape, inverse[0], F32)
+
+
+def operator_kernel(step, n_fields, hot_in, hot_ex, scale_ref, in_ref, ex_ref, anchor_ref, row_ref, before_ref, *refs):
     fields = refs[:n_fields]
     mine_ref, other_ref, back_ref, row_out, u_in, u_ex = refs[n_fields:]
     blk = before_ref.shape[0]
+    scale = scale_ref[...]
     field = jnp.concatenate([f[...] for f in fields], 0)
-    spread, energy = springs(hot_in[...], field, in_ref, u_in)
+    spread, energy = springs(hot_in[...], field, in_ref, scale, u_in)
     v = field[:blk]
-    spread_ex, energy_ex = springs(hot_ex[...], jnp.concatenate([v, before_ref[...]], 0), ex_ref, u_ex)
+    spread_ex, energy_ex = springs(hot_ex[...], jnp.concatenate([v, before_ref[...]], 0), ex_ref, scale, u_ex)
     back_ref[...] = spread_ex[blk:]
-    image = anchor_ref[...] * v
+    image = anchor_ref[...] * v * scale
     energy = jnp.sum(image * v, axis=0, keepdims=True) + energy + energy_ex
     square = jnp.sum(v * v, axis=0, keepdims=True)
     rows = lax.broadcasted_iota(jnp.int32, row_ref.shape, 0)
@@ -123,17 +129,8 @@
 
 def pair_kernel(mine_ref, got_ref, *outs):
     tall = mine_ref.shape[0] // 4
-    per = 4 // len(outs)
-    for place, j in enumerate((0, 3, 1, 2)):
-        block = mine_ref[j * tall : (j + 1) * tall] + got_ref[j * tall : (j + 1) * tall]
-        at = (place % per) * tall
-        outs[place // per][at : at + tall, :] = block
-
-
-def half_kernel(a_ref, b_ref, keep_ref, send_ref):
-    tall = keep_ref.shape[0]
-    keep_ref[...] = a_ref[:tall] + b_ref[:tall]
-    send_ref[...] = a_ref[tall:] + b_ref[tall:]
+    for out, j in zip(outs, (0, 3, 1, 2)):
+        out[...] = mine_ref[j * tall : (j + 1) * tall] + got_ref[j * tall : (j + 1) * tall]
 
 
 def tree(values):
@@ -161,9 +158,9 @@
     return total
 
 
-def final_kernel(n, sums_ref, *refs):
+def final_kernel(n, sums_ref, scale_ref, *refs):
     parts, incoming = refs[:n], refs[n]
-    *vs, x_ref, r_ref = refs[n + 1 :]
+    *vs, x_ref, r_ref, again_ref, ratio_ref = refs[n + 1 :]
     blk = incoming.shape[0]
     vs = [v[...] for v in vs] + [tree([p[:blk] for p in parts]) + incoming[...]]
     rows = jnp.sum(jnp.sum(sums_ref[...], axis=0), axis=1, keepdims=True)
@@ -194,11 +191,17 @@
         power = power * inverse
         if k < ITERS:
             x_sum = x_sum + (x[k] * power) * v
-    x_ref[...] = x_sum
+    x_ref[...] = x_sum * scale_ref[...]
     r_ref[...] = r_sum
-
-
-def call(kernel, outs, *args, scratch=(), scalars=0, dtype=F32, flops=0, hbm=False, limit=16):
+    fine, ratio = jnp.abs(raw[1]) < LARGE, raw[0] / raw[1]
+    for before, m in zip(raw[1:], raw[2:]):
+        ratio = jnp.where(m < LARGE, before / m, ratio)
+        fine = fine & (m < LARGE)
+    again_ref[0] = jnp.max(jnp.where(fine, 0, 1))
+    ratio_ref[0] = jnp.max(ratio)
+
+
+def call(kernel, outs, *args, scratch=(), scalars=0, dtype=F32, flops=0, hbm=False, limit=16, scalar_outs=0):
     specs = [pl.BlockSpec(memory_space=pltpu.SMEM)] * scalars
     specs += [pl.BlockSpec(memory_space=pltpu.HBM) if hbm else VMEM] * (len(args) - scalars)
     dtypes = dtype if isinstance(dtype, tuple) else (dtype,) * len(outs)
@@ -206,7 +209,7 @@
         kernel,
         out_shape=[jax.ShapeDtypeStruct(o, d) for o, d in zip(outs, dtypes)],
         in_specs=specs,
-        out_specs=[VMEM] * len(outs),
+        out_specs=[VMEM] * (len(outs) - scalar_outs) + [pl.BlockSpec(memory_space=pltpu.SMEM)] * scalar_outs,
         scratch_shapes=scratch,
         compiler_params=pltpu.CompilerParams(vmem_limit_bytes=limit * 2**20),
         cost_estimate=pl.CostEstimate(flops=flops, bytes_accessed=0, transcendentals=0) if flops else None,
@@ -222,7 +225,8 @@
     return lax.ppermute(x, "sec", [(i, (i + by) % peers) for i in range(peers)])
 
 
-def per_device(
+def one_round(
+    inverse,
     right_side,
     anchor_diag,
     intra_own,
@@ -241,40 +245,49 @@
     field, row = (blk, node), (ROWS, node)
     vs, moments = [right_side[0, 0]], jnp.zeros(row, F32)
     sections = lax.axis_size("sec")
+    vs[0], scale = call(pass_kernel, (field, (1, node)), inverse, vs[0], scalars=1, flops=PASS_FLOPS)
     hot = call(
         hot_kernel, ((lax.axis_size("tile") * blk, intra_own.shape[2]), (2 * blk, inter_own.shape[2])),
-        section, tile, intra_count.reshape(1), inter_count.reshape(1), intra_own, intra_far, inter_own, inter_prev, scalars=4, dtype=BF16,
+        section, tile, intra_count.reshape(1), inter_count.reshape(1), intra_own, intra_far, inter_own, inter_prev, scale,
+        scalars=4, dtype=BF16,
     )
-    (early,) = call(pass_kernel, (field,), vs[0], flops=HOTFLOPS)
     for step in range(ITERS):
         last = step == ITERS - 1
         tall = blk + ROWS if last else blk
         v = vs[-1]
         here = [v] + [swap(v, 2 * j) for j in (1, 2, 3)]
-        if step == 0:
-            v = early
-        fields = here + [swap(h, 1) for h in [v] + here[1:]]
+        fields = here + [swap(h, 1) for h in here]
         before = shifted(v, 1)
         mine, other, back, moments = call(
             functools.partial(operator_kernel, step, len(fields)), ((4 * tall, node), (4 * tall, node), field, row),
-            *hot, intra_stiff, inter_stiff, anchor, moments, before, *fields,
-            scratch=[pltpu.VMEM((intra_own.shape[2], node), F32), pltpu.VMEM((inter_own.shape[2], node), F32)], flops=OPFLOPS,
+            *hot, scale, intra_stiff, inter_stiff, anchor, moments, before, *fields,
+            scratch=[pltpu.VMEM((intra_own.shape[2], node), F32), pltpu.VMEM((inter_own.shape[2], node), F32)],
         )
         incoming = shifted(back, -1)
         got = swap(other, 1)
-        if SCATTER == "three":
-            p0, p3, p1, p2 = call(pair_kernel, ((tall, node),) * 4, mine, got)
-            parts = [p0] + [swap(p, 2 * j) for j, p in ((1, p1), (2, p2), (3, p3))]
-        else:
-            keep, send = call(pair_kernel, ((2 * tall, node),) * 2, mine, got)
-            keep, send = call(half_kernel, ((tall, node),) * 2, keep, swap(send, 2))
-            parts = [keep, swap(send, 6)]
+        p0, p3, p1, p2 = call(pair_kernel, ((tall, node),) * 4, mine, got)
+        parts = [p0] + [swap(p, 2 * j) for j, p in ((1, p1), (2, p2), (3, p3))]
         if not last:
             (nxt,) = call(functools.partial(sum_kernel, len(parts)), (field,), *parts, incoming)
             vs.append(nxt)
     (sums,) = call(functools.partial(row_kernel, len(parts)), ((sections, ROWS, node),), *parts)
     sums = lax.all_to_all(sums, "sec", 0, 0, tiled=True)
-    x, r = call(functools.partial(final_kernel, len(parts)), (field, field), sums, *parts, incoming, *vs)
+    x, r, again, ratio = call(
+        functools.partial(final_kernel, len(parts)), (field, field, (1,), (1,)), sums, scale, *parts, incoming, *vs,
+        dtype=(F32, F32, jnp.int32, F32), scalar_outs=2,
+    )
+    return again, ratio, x, r
+
+
+def per_device(*arrays):
+    def body(state):
+        rounds, inverse, *_ = state
+        again, ratio, x, r = one_round(inverse, *arrays)
+        return jnp.where(again > 0, rounds - 1, 0), inverse * ratio, x, r
+
+    field = arrays[0].shape[2:]
+    start = (jnp.full((1,), ROUNDS, jnp.int32), jnp.ones((1,), F32), *call(zero_kernel, (field, field)))
+    _, _, x, r = lax.while_loop(lambda state: state[0][0] > 0, body, start)
     return x[None, None], r[None, None]
 
 

time: 91.2 us -> 93.7 us (1.027)
  Pallas kernels: 6.17 us -> 10.6 us
  local copies, waits for them, and re-layouts: 2.23 us -> 0.03 us
  between operations: 2.21 us -> 0.63 us
  loops' own time: 0 us -> 1.54 us
  waiting for transfers between devices: 31.9 us -> 33.4 us
  starting transfers between devices: 48.4 us -> 47.3 us
    pallas_call x12 -> x13, Pallas kernels: 6.17 us -> 10.6 us  [call(): pl.pallas_call(kernel, out_shape=[jax.ShapeDtypeStruct(o, d) for o, d in...]
    unnamed x20 -> x0, local copies, waits for them, and re-layouts: 2.23 us -> none
    another operation x0 -> x1, loops' own time: none -> 1.54 us  [per_device(): _, _, x, r = lax.while_loop(lambda state: state[0][0] > 0, body, start)]
  transfers between devices with their start and end apart: 40 -> 40, of which waited for: 18 -> 17; matrix products, arithmetic and copies ran while one was open for 0% -> 0% of each run, Pallas kernels for 0% -> 2%
where the time goes in v3:
time: 93.7 us; the launch traced here: 93.5 us
  starting transfers between devices  47.3 us (50%)
  waiting for transfers between devices  33.4 us (36%)
  Pallas kernels  10.6 us (11%)
  loops' own time  1.54 us (2%)
    ppermute x33, starting transfers between devices, swap(): lax.ppermute(x, 'tile', [(i, i ^ by) for i in range(lax.axis_size('tile'))])  28.6 us
    ppermute x33, waiting for transfers between devices, swap(): lax.ppermute(x, 'tile', [(i, i ^ by) for i in range(lax.axis_size('tile'))])  20.8 us
    ppermute x6, starting transfers between devices, shifted(): return lax.ppermute(x, 'sec', [(i, (i + by) % peers) for i in range(peers)])  11.5 us
    pallas_call x13, Pallas kernels, call(): pl.pallas_call(kernel, out_shape=[jax.ShapeDtypeStruct(o, d) for o, d in...  10.6 us
    all_to_all x1, starting transfers between devices, one_round(): sums = lax.all_to_all(sums, 'sec', 0, 0, tiled=True)  7.28 us
    ppermute x6, waiting for transfers between devices, shifted(): return lax.ppermute(x, 'sec', [(i, (i + by) % peers) for i in range(peers)])  6.96 us
    all_to_all x1, waiting for transfers between devices, one_round(): sums = lax.all_to_all(sums, 'sec', 0, 0, tiled=True)  5.66 us
  transfers between devices with their start and end apart: 40, of which 17 were waited for; matrix products, arithmetic and copies ran while one was open for 0% of the time, Pallas kernels for 2%

profile of v3, /device:TPU:32, one launch (start us, length us, event | category | flops | bytes accessed | tf_op | source)
XLA Modules:
  0.0 93.5 jit_solution(10620522284007575083)
XLA Ops:
  0.6 0.6 shard_map.113
  1.3 92.2 %while.16 = (s32[1]{0:T(128)}, f32[1]{0:T(128)}, f32[64,128]{1,0:T(8,128)}, f32[64,128]{1,0:T(8,128)}, s32[1,1]{1,0:T(1,128)}, /*index=5*/s32[1,1]{1,0:T(1,128)}...) while((s32[1]{0:T(128)}, f32[1]{0:T(128)}, ...), condition=%wide.region_1.2_spmd, body=%wide.region_0.1_spmd.sunk | while | flops 20000000000 | bytes 25815560 | solution.py:290
  1.3 0.9 body.42
  2.2 3.0 %collective-permute-start.3 = (f32[64,128]{1,0:T(8,128)S(1)}, f32[64,128]{1,0:T(8,128)S(1)}, u32[]{:S(2)}, u32[]{:S(2)}) collective-permute-start(f32[64,128]{1,0:T(8,128)S(1)} %get-tuple-element.344.refs_0_.refs_5_), channel_id=1, source_target_pairs={{0,6},{1,7},{2,4},{3,5},{4,2},{5,3},{6,0},{7,1},{8,14},{9,15},{10,... | collective-permute-start | bytes 98312 | tf_op jit(solution)/shard_map/while/body/ppermute | solution.py:220
  5.2 0.6 collective-permute-start.2
  5.9 0.5 collective-permute-start.1
  6.3 1.9 %collective-permute-start = (f32[64,128]{1,0:T(8,128)S(1)}, f32[64,128]{1,0:T(8,128)S(1)}, u32[]{:S(2)}, u32[]{:S(2)}) collective-permute-start(f32[64,128]{1,0:T(8,128)S(1)} %get-tuple-element.344.refs_0_.refs_5_), channel_id=1, source_target_pairs={{0,8},{8,16},{16,24},{24,32},{32,40},{40,48},{48,56},{56,64},{64,7... | collective-permute-start | bytes 98312 | tf_op jit(solution)/shard_map/while/body/ppermute | solution.py:225
  8.5 2.2 %collective-permute-done.2.refs_2_ = f32[64,128]{1,0:T(8,128)S(1)} collective-permute-done((f32[64,128]{1,0:T(8,128)S(1)}, f32[64,128]{1,0:T(8,128)S(1)}, u32[]{:S(2)}, u32[]{:S(2)}) %collective-permute-start.2) | collective-permute-done | bytes 32800 | tf_op jit(solution)/shard_map/while/body/ppermute | solution.py:220
  10.7 0.5 collective-permute-start.5
  11.2 1.5 %body.43 = (bf16[512,96]{1,0:T(8,128)(2,1)S(1)}, bf16[128,48]{1,0:T(8,128)(2,1)S(1)}) custom-call(s32[1]{0:T(128)} %bitcast.16.section, s32[1]{0:T(128)} %bitcast.17.tile, s32[1]{0:T(128)} %bitcast.18.count, s32[1]{0:T(128)} %bitcast.19.count_ex, s32[1,1,96]{2,1,0:T(1,128)S(1)} %copy-done.3, s32[1,1,96]{2,1,0:T(1,128)S(1)} %copy-done.4, ...), custom_call_target="tpu_custom_call" | custom-call | tf_op jit(solution)/shard_map/while/body/pallas_call | solution.py:208
  12.8 2.7 %body.44 = (f32[256,128]{1,0:T(8,128)S(1)}, f32[256,128]{1,0:T(8,128)S(1)}, f32[64,128]{1,0:T(8,128)S(1)}, f32[8,128]{1,0:T(8,128)S(1)}) custom-call(bf16[512,96]{1,0:T(8,128)(2,1)S(1)} %get-tuple-element.342.hot_in, bf16[128,48]{1,0:T(8,128)(2,1)S(1)} %get-tuple-element.343.hot_ex, f32[1,128]{1,0:T(1,128)S(1)} %get-tuple-element.341.refs_4_.scale_ref, ...), custom_call_target="tpu_custom_call" | custom-call | tf_op jit(solution)/shard_map/while/body/pallas_call | solution.py:208
  15.6 3.9 %collective-permute-start.12 = (f32[64,128]{1,0:T(8,128)S(1)}, f32[64,128]{1,0:T(8,128)S(1)}, u32[]{:S(2)}, u32[]{:S(2)}) collective-permute-start(f32[64,128]{1,0:T(8,128)S(1)} %get-tuple-element.352), channel_id=1, source_target_pairs={{0,248},{8,0},{16,8},{24,16},{32,24},{40,32},{48,40},{56,48},{64,5... | collective-permute-start | bytes 98312 | tf_op jit(solution)/shard_map/while/body/ppermute | solution.py:225
  19.5 1.7 %collective-permute-start.9 = (f32[64,128]{1,0:T(8,128)S(1)}, f32[64,128]{1,0:T(8,128)S(1)}, u32[]{:S(2)}, u32[]{:S(2)}) collective-permute-start(f32[64,128]{1,0:T(8,128)S(1)} %get-tuple-element.349), channel_id=1, source_target_pairs={{0,2},{1,3},{2,0},{3,1},{4,6},{5,7},{6,4},{7,5},{8,10},{9,11},{10,... | collective-permute-start | bytes 98312 | tf_op jit(solution)/shard_map/while/body/ppermute | solution.py:220
  21.2 2.9 %collective-permute-start.10 = (f32[64,128]{1,0:T(8,128)S(1)}, f32[64,128]{1,0:T(8,128)S(1)}, u32[]{:S(2)}, u32[]{:S(2)}) collective-permute-start(f32[64,128]{1,0:T(8,128)S(1)} %get-tuple-element.350), channel_id=1, source_target_pairs={{0,4},{1,5},{2,6},{3,7},{4,0},{5,1},{6,2},{7,3},{8,12},{9,13},{10,... | collective-permute-start | bytes 98312 | tf_op jit(solution)/shard_map/while/body/ppermute | solution.py:220
  24.3 2.3 %collective-permute-done.10.refs_2_ = f32[64,128]{1,0:T(8,128)S(1)} collective-permute-done((f32[64,128]{1,0:T(8,128)S(1)}, f32[64,128]{1,0:T(8,128)S(1)}, u32[]{:S(2)}, u32[]{:S(2)}) %collective-permute-start.10) | collective-permute-done | bytes 32800 | tf_op jit(solution)/shard_map/while/body/ppermute | solution.py:220
  26.6 2.6 %collective-permute-done.11.refs_3_ = f32[64,128]{1,0:T(8,128)S(1)} collective-permute-done((f32[64,128]{1,0:T(8,128)S(1)}, f32[64,128]{1,0:T(8,128)S(1)}, u32[]{:S(2)}, u32[]{:S(2)}) %collective-permute-start.11) | collective-permute-done | bytes 32800 | tf_op jit(solution)/shard_map/while/body/ppermute | solution.py:220
  29.5 0.8 collective-permute-start.15
  30.3 3.1 %collective-permute-start.14 = (f32[64,128]{1,0:T(8,128)S(1)}, f32[64,128]{1,0:T(8,128)S(1)}, u32[]{:S(2)}, u32[]{:S(2)}) collective-permute-start(f32[64,128]{1,0:T(8,128)S(1)} %body.46.refs_0_.refs_6_), channel_id=1, source_target_pairs={{0,2},{1,3},{2,0},{3,1},{4,6},{5,7},{6,4},{7,5},{8,10},{9,11},{10,... | collective-permute-start | bytes 98312 | tf_op jit(solution)/shard_map/while/body/ppermute | solution.py:220
  33.4 1.0 %collective-permute-done.16.refs_3_ = f32[64,128]{1,0:T(8,128)S(1)} collective-permute-done((f32[64,128]{1,0:T(8,128)S(1)}, f32[64,128]{1,0:T(8,128)S(1)}, u32[]{:S(2)}, u32[]{:S(2)}) %collective-permute-start.16) | collective-permute-done | bytes 32800 | tf_op jit(solution)/shard_map/while/body/ppermute | solution.py:220
  34.4 0.5 collective-permute-done.15.refs_2_
  35.0 0.7 collective-permute-done.14.refs_1_
  35.7 2.4 %collective-permute-done.13.before_ref = f32[64,128]{1,0:T(8,128)S(1)} collective-permute-done((f32[64,128]{1,0:T(8,128)S(1)}, f32[64,128]{1,0:T(8,128)S(1)}, u32[]{:S(2)}, u32[]{:S(2)}) %collective-permute-start.13) | collective-permute-done | bytes 32800 | tf_op jit(solution)/shard_map/while/body/ppermute | solution.py:225
  38.1 1.3 %body.47 = (f32[256,128]{1,0:T(8,128)S(1)}, f32[256,128]{1,0:T(8,128)S(1)}, f32[64,128]{1,0:T(8,128)S(1)}, f32[8,128]{1,0:T(8,128)S(1)}) custom-call(bf16[512,96]{1,0:T(8,128)(2,1)S(1)} %get-tuple-element.342.hot_in, bf16[128,48]{1,0:T(8,128)(2,1)S(1)} %get-tuple-element.343.hot_ex, f32[1,128]{1,0:T(1,128)S(1)} %get-tuple-element.341.refs_4_.scale_ref, ...), custom_call_target="tpu_custom_call" | custom-call | tf_op jit(solution)/shard_map/while/body/pallas_call | solution.py:208
  39.5 5.3 %collective-permute-start.25 = (f32[64,128]{1,0:T(8,128)S(1)}, f32[64,128]{1,0:T(8,128)S(1)}, u32[]{:S(2)}, u32[]{:S(2)}) collective-permute-start(f32[64,128]{1,0:T(8,128)S(1)} %get-tuple-element.360), channel_id=1, source_target_pairs={{0,248},{8,0},{16,8},{24,16},{32,24},{40,32},{48,40},{56,48},{64,5... | collective-permute-start | bytes 98312 | tf_op jit(solution)/shard_map/while/body/ppermute | solution.py:225
  44.9 3.5 %collective-permute-start.23 = (f32[64,128]{1,0:T(8,128)S(1)}, f32[64,128]{1,0:T(8,128)S(1)}, u32[]{:S(2)}, u32[]{:S(2)}) collective-permute-start(f32[64,128]{1,0:T(8,128)S(1)} %get-tuple-element.358), channel_id=1, source_target_pairs={{0,4},{1,5},{2,6},{3,7},{4,0},{5,1},{6,2},{7,3},{8,12},{9,13},{10,... | collective-permute-start | bytes 98312 | tf_op jit(solution)/shard_map/while/body/ppermute | solution.py:220
  48.4 1.2 %collective-permute-start.24 = (f32[64,128]{1,0:T(8,128)S(1)}, f32[64,128]{1,0:T(8,128)S(1)}, u32[]{:S(2)}, u32[]{:S(2)}) collective-permute-start(f32[64,128]{1,0:T(8,128)S(1)} %get-tuple-element.359), channel_id=1, source_target_pairs={{0,6},{1,7},{2,4},{3,5},{4,2},{5,3},{6,0},{7,1},{8,14},{9,15},{10,... | collective-permute-start | bytes 98312 | tf_op jit(solution)/shard_map/while/body/ppermute | solution.py:220
  49.6 1.0 %collective-permute-done.23.refs_2_ = f32[64,128]{1,0:T(8,128)S(1)} collective-permute-done((f32[64,128]{1,0:T(8,128)S(1)}, f32[64,128]{1,0:T(8,128)S(1)}, u32[]{:S(2)}, u32[]{:S(2)}) %collective-permute-start.23) | collective-permute-done | bytes 32800 | tf_op jit(solution)/shard_map/while/body/ppermute | solution.py:220
  50.6 2.9 %collective-permute-done.24.refs_3_ = f32[64,128]{1,0:T(8,128)S(1)} collective-permute-done((f32[64,128]{1,0:T(8,128)S(1)}, f32[64,128]{1,0:T(8,128)S(1)}, u32[]{:S(2)}, u32[]{:S(2)}) %collective-permute-start.24) | collective-permute-done | bytes 32800 | tf_op jit(solution)/shard_map/while/body/ppermute | solution.py:220
  53.5 1.3 %collective-permute-start.29 = (f32[64,128]{1,0:T(8,128)S(1)}, f32[64,128]{1,0:T(8,128)S(1)}, u32[]{:S(2)}, u32[]{:S(2)}) collective-permute-start(f32[64,128]{1,0:T(8,128)S(1)} %body.49.refs_0_.refs_7_), channel_id=1, source_target_pairs={{0,6},{1,7},{2,4},{3,5},{4,2},{5,3},{6,0},{7,1},{8,14},{9,15},{10,... | collective-permute-start | bytes 98312 | tf_op jit(solution)/shard_map/while/body/ppermute | solution.py:220
  54.8 2.9 %collective-permute-start.27 = (f32[64,128]{1,0:T(8,128)S(1)}, f32[64,128]{1,0:T(8,128)S(1)}, u32[]{:S(2)}, u32[]{:S(2)}) collective-permute-start(f32[64,128]{1,0:T(8,128)S(1)} %body.49.refs_0_.refs_7_), channel_id=1, source_target_pairs={{0,2},{1,3},{2,0},{3,1},{4,6},{5,7},{6,4},{7,5},{8,10},{9,11},{10,... | collective-permute-start | bytes 98312 | tf_op jit(solution)/shard_map/while/body/ppermute | solution.py:220
  57.7 1.0 %collective-permute-done.29.refs_3_ = f32[64,128]{1,0:T(8,128)S(1)} collective-permute-done((f32[64,128]{1,0:T(8,128)S(1)}, f32[64,128]{1,0:T(8,128)S(1)}, u32[]{:S(2)}, u32[]{:S(2)}) %collective-permute-start.29) | collective-permute-done | bytes 32800 | tf_op jit(solution)/shard_map/while/body/ppermute | solution.py:220
  58.7 1.5 %collective-permute-done.28.refs_2_ = f32[64,128]{1,0:T(8,128)S(1)} collective-permute-done((f32[64,128]{1,0:T(8,128)S(1)}, f32[64,128]{1,0:T(8,128)S(1)}, u32[]{:S(2)}, u32[]{:S(2)}) %collective-permute-start.28) | collective-permute-done | bytes 32800 | tf_op jit(solution)/shard_map/while/body/ppermute | solution.py:220
  60.2 0.5 collective-permute-start.31
  60.7 0.9 collective-permute-done.26.before_ref
  61.6 1.8 %body.50 = (f32[288,128]{1,0:T(8,128)S(1)}, f32[288,128]{1,0:T(8,128)S(1)}, f32[64,128]{1,0:T(8,128)S(1)}, f32[8,128]{1,0:T(8,128)}) custom-call(bf16[512,96]{1,0:T(8,128)(2,1)S(1)} %get-tuple-element.342.hot_in, bf16[128,48]{1,0:T(8,128)(2,1)S(1)} %get-tuple-element.343.hot_ex, f32[1,128]{1,0:T(1,128)S(1)} %get-tuple-element.341.refs_4_.scale_ref, ...), custom_call_target="tpu_custom_call" | custom-call | tf_op jit(solution)/shard_map/while/body/pallas_call | solution.py:208
  63.4 0.3 collective-permute-start.34
  63.7 1.0 %collective-permute-done.34.got_ref = f32[288,128]{1,0:T(8,128)S(1)} collective-permute-done((f32[288,128]{1,0:T(8,128)S(1)}, f32[288,128]{1,0:T(8,128)S(1)}, u32[]{:S(2)}, u32[]{:S(2)}) %collective-permute-start.34) | collective-permute-done | bytes 147488 | tf_op jit(solution)/shard_map/while/body/ppermute | solution.py:220
  64.8 1.3 %collective-permute-start.35 = (f32[72,128]{1,0:T(8,128)S(1)}, f32[72,128]{1,0:T(8,128)S(1)}, u32[]{:S(2)}, u32[]{:S(2)}) collective-permute-start(f32[72,128]{1,0:T(8,128)S(1)} %get-tuple-element.364), channel_id=1, source_target_pairs={{0,2},{1,3},{2,0},{3,1},{4,6},{5,7},{6,4},{7,5},{8,10},{9,11},{10,... | collective-permute-start | bytes 110600 | tf_op jit(solution)/shard_map/while/body/ppermute | solution.py:220
  66.1 2.3 %collective-permute-start.36 = (f32[72,128]{1,0:T(8,128)S(1)}, f32[72,128]{1,0:T(8,128)S(1)}, u32[]{:S(2)}, u32[]{:S(2)}) collective-permute-start(f32[72,128]{1,0:T(8,128)S(1)} %get-tuple-element.365), channel_id=1, source_target_pairs={{0,4},{1,5},{2,6},{3,7},{4,0},{5,1},{6,2},{7,3},{8,12},{9,13},{10,... | collective-permute-start | bytes 110600 | tf_op jit(solution)/shard_map/while/body/ppermute | solution.py:220
  68.4 1.2 %collective-permute-start.37 = (f32[72,128]{1,0:T(8,128)S(1)}, f32[72,128]{1,0:T(8,128)S(1)}, u32[]{:S(2)}, u32[]{:S(2)}) collective-permute-start(f32[72,128]{1,0:T(8,128)S(1)} %get-tuple-element.366), channel_id=1, source_target_pairs={{0,6},{1,7},{2,4},{3,5},{4,2},{5,3},{6,0},{7,1},{8,14},{9,15},{10,... | collective-permute-start | bytes 110600 | tf_op jit(solution)/shard_map/while/body/ppermute | solution.py:220
  69.6 1.9 %collective-permute-done.36.refs_2_ = f32[72,128]{1,0:T(8,128)S(1)} collective-permute-done((f32[72,128]{1,0:T(8,128)S(1)}, f32[72,128]{1,0:T(8,128)S(1)}, u32[]{:S(2)}, u32[]{:S(2)}) %collective-permute-start.36) | collective-permute-done | bytes 36896 | tf_op jit(solution)/shard_map/while/body/ppermute | solution.py:220
  71.5 2.0 %collective-permute-done.37.refs_3_ = f32[72,128]{1,0:T(8,128)S(1)} collective-permute-done((f32[72,128]{1,0:T(8,128)S(1)}, f32[72,128]{1,0:T(8,128)S(1)}, u32[]{:S(2)}, u32[]{:S(2)}) %collective-permute-start.37) | collective-permute-done | bytes 36896 | tf_op jit(solution)/shard_map/while/body/ppermute | solution.py:220
  73.5 0.7 body.52
  74.2 7.3 %all-to-all-start = ((f32[32,8,128]{2,1,0:T(8,128)}), f32[32,8,128]{2,1,0:T(8,128)S(1)}, u32[]{:S(2)}, u32[]{:S(2)}) async-start(f32[32,8,128]{2,1,0:T(8,128)} %body.52), calls=%async_computation | async-start | bytes 262144 | tf_op jit(solution)/shard_map/while/body/all_to_all | solution.py:274
  81.5 0.4 collective-permute-start.38
  81.9 3.7 %collective-permute-done.38.refs_4_ = f32[64,128]{1,0:T(8,128)S(1)} collective-permute-done((f32[64,128]{1,0:T(8,128)S(1)}, f32[64,128]{1,0:T(8,128)S(1)}, u32[]{:S(2)}, u32[]{:S(2)}) %collective-permute-start.38) | collective-permute-done | bytes 32800 | tf_op jit(solution)/shard_map/while/body/ppermute | solution.py:225
  85.6 5.7 %all-to-all-done.sums_ref = f32[32,8,128]{2,1,0:T(8,128)S(1)} async-done(((f32[32,8,128]{2,1,0:T(8,128)}), f32[32,8,128]{2,1,0:T(8,128)S(1)}, u32[]{:S(2)}, u32[]{:S(2)}) %all-to-all-start) | async-done | bytes 131104 | tf_op jit(solution)/shard_map/while/body/all_to_all | solution.py:274
  91.3 0.9 body.53
  (61 shorter events, 1.3 us)
Async XLA Ops:
  1.3 9.9 %copy-start.3 = (s32[1,1,96]{2,1,0:T(1,128)S(1)}, s32[1,1,96]{2,1,0:T(1,128)}, u32[]{:S(2)}) copy-start(s32[1,1,96]{2,1,0:T(1,128)} %get-tuple-element.419.refs_0_) | copy-start | bytes 1156 | tf_op jit(solution)/shard_map/while
  1.3 9.9 %copy-start.4 = (s32[1,1,96]{2,1,0:T(1,128)S(1)}, s32[1,1,96]{2,1,0:T(1,128)}, u32[]{:S(2)}) copy-start(s32[1,1,96]{2,1,0:T(1,128)} %get-tuple-element.420.refs_1_) | copy-start | bytes 1156 | tf_op jit(solution)/shard_map/while
  1.3 9.9 %copy-start.5 = (s32[1,1,48]{2,1,0:T(1,128)S(1)}, s32[1,1,48]{2,1,0:T(1,128)}, u32[]{:S(2)}) copy-start(s32[1,1,48]{2,1,0:T(1,128)} %get-tuple-element.421.refs_2_) | copy-start | bytes 580 | tf_op jit(solution)/shard_map/while
  1.3 9.9 %copy-start.6 = (s32[1,1,48]{2,1,0:T(1,128)S(1)}, s32[1,1,48]{2,1,0:T(1,128)}, u32[]{:S(2)}) copy-start(s32[1,1,48]{2,1,0:T(1,128)} %get-tuple-element.422.refs_3_) | copy-start | bytes 580 | tf_op jit(solution)/shard_map/while
  1.3 11.5 %copy-start = (bf16[1,1,96,128,128]{4,3,2,1,0:T(8,128)(2,1)S(1)}, bf16[1,1,96,128,128]{4,3,2,1,0:T(8,128)(2,1)}, u32[]{:S(2)}) copy-start(bf16[1,1,96,128,128]{4,3,2,1,0:T(8,128)(2,1)} %get-tuple-element.424.in_ref) | copy-start | bytes 9437188 | tf_op jit(solution)/shard_map/while
  1.3 11.5 %copy-start.2 = (f32[1,1,64,128]{3,2,1,0:T(8,128)S(1)}, f32[1,1,64,128]{3,2,1,0:T(8,128)}, u32[]{:S(2)}) copy-start(f32[1,1,64,128]{3,2,1,0:T(8,128)} %get-tuple-element.423) | copy-start | bytes 98308 | tf_op jit(solution)/shard_map/while
  2.2 6.0 %collective-permute-start.3 = (f32[64,128]{1,0:T(8,128)S(1)}, f32[64,128]{1,0:T(8,128)S(1)}, u32[]{:S(2)}, u32[]{:S(2)}) collective-permute-start(f32[64,128]{1,0:T(8,128)S(1)} %get-tuple-element.344.refs_0_.refs_5_), channel_id=1, source_target_pairs={{0,6},{1,7},{2,4},{3,5},{4,2},{5,3},{6,0},{7,1},{8,14},{9,15},{10,... | collective-permute-start | bytes 98312 | tf_op jit(solution)/shard_map/while/body/ppermute | solution.py:220
  5.2 5.4 %collective-permute-start.2 = (f32[64,128]{1,0:T(8,128)S(1)}, f32[64,128]{1,0:T(8,128)S(1)}, u32[]{:S(2)}, u32[]{:S(2)}) collective-permute-start(f32[64,128]{1,0:T(8,128)S(1)} %get-tuple-element.344.refs_0_.refs_5_), channel_id=1, source_target_pairs={{0,4},{1,5},{2,6},{3,7},{4,0},{5,1},{6,2},{7,3},{8,12},{9,13},{10,... | collective-permute-start | bytes 98312 | tf_op jit(solution)/shard_map/while/body/ppermute | solution.py:220
  5.9 4.8 %collective-permute-start.1 = (f32[64,128]{1,0:T(8,128)S(1)}, f32[64,128]{1,0:T(8,128)S(1)}, u32[]{:S(2)}, u32[]{:S(2)}) collective-permute-start(f32[64,128]{1,0:T(8,128)S(1)} %get-tuple-element.344.refs_0_.refs_5_), channel_id=1, source_target_pairs={{0,2},{1,3},{2,0},{3,1},{4,6},{5,7},{6,4},{7,5},{8,10},{9,11},{10,... | collective-permute-start | bytes 98312 | tf_op jit(solution)/shard_map/while/body/ppermute | solution.py:220
  6.3 6.4 %collective-permute-start.4 = (f32[64,128]{1,0:T(8,128)S(1)}, f32[64,128]{1,0:T(8,128)S(1)}, u32[]{:S(2)}, u32[]{:S(2)}) collective-permute-start(f32[64,128]{1,0:T(8,128)S(1)} %get-tuple-element.344.refs_0_.refs_5_), channel_id=1, source_target_pairs={{0,1},{1,0},{2,3},{3,2},{4,5},{5,4},{6,7},{7,6},{8,9},{9,8},{10,11... | collective-permute-start | bytes 98312 | tf_op jit(solution)/shard_map/while/body/ppermute | solution.py:220
  6.3 6.4 %collective-permute-start = (f32[64,128]{1,0:T(8,128)S(1)}, f32[64,128]{1,0:T(8,128)S(1)}, u32[]{:S(2)}, u32[]{:S(2)}) collective-permute-start(f32[64,128]{1,0:T(8,128)S(1)} %get-tuple-element.344.refs_0_.refs_5_), channel_id=1, source_target_pairs={{0,8},{8,16},{16,24},{24,32},{32,40},{40,48},{48,56},{56,64},{64,7... | collective-permute-start | bytes 98312 | tf_op jit(solution)/shard_map/while/body/ppermute | solution.py:225
  8.2 4.5 %collective-permute-start.7 = (f32[64,128]{1,0:T(8,128)S(1)}, f32[64,128]{1,0:T(8,128)S(1)}, u32[]{:S(2)}, u32[]{:S(2)}) collective-permute-start(f32[64,128]{1,0:T(8,128)S(1)} %collective-permute-done.3.refs_3_), channel_id=1, source_target_pairs={{0,1},{1,0},{2,3},{3,2},{4,5},{5,4},{6,7},{7,6},{8,9},{9,8},{10,11... | collective-permute-start | bytes 98312 | tf_op jit(solution)/shard_map/while/body/ppermute | solution.py:220
  10.6 2.1 %collective-permute-start.6 = (f32[64,128]{1,0:T(8,128)S(1)}, f32[64,128]{1,0:T(8,128)S(1)}, u32[]{:S(2)}, u32[]{:S(2)}) collective-permute-start(f32[64,128]{1,0:T(8,128)S(1)} %collective-permute-done.2.refs_2_), channel_id=1, source_target_pairs={{0,1},{1,0},{2,3},{3,2},{4,5},{5,4},{6,7},{7,6},{8,9},{9,8},{10,11... | collective-permute-start | bytes 98312 | tf_op jit(solution)/shard_map/while/body/ppermute | solution.py:220
  10.7 2.1 %collective-permute-start.5 = (f32[64,128]{1,0:T(8,128)S(1)}, f32[64,128]{1,0:T(8,128)S(1)}, u32[]{:S(2)}, u32[]{:S(2)}) collective-permute-start(f32[64,128]{1,0:T(8,128)S(1)} %collective-permute-done.1.refs_1_), channel_id=1, source_target_pairs={{0,1},{1,0},{2,3},{3,2},{4,5},{5,4},{6,7},{7,6},{8,9},{9,8},{10,11... | collective-permute-start | bytes 98312 | tf_op jit(solution)/shard_map/while/body/ppermute | solution.py:220
  11.2 26.9 %copy-start.1 = (bf16[1,1,48,128,128]{4,3,2,1,0:T(8,128)(2,1)S(1)}, bf16[1,1,48,128,128]{4,3,2,1,0:T(8,128)(2,1)}, u32[]{:S(2)}) copy-start(bf16[1,1,48,128,128]{4,3,2,1,0:T(8,128)(2,1)} %get-tuple-element.425.ex_ref) | copy-start | bytes 4718596 | tf_op jit(solution)/shard_map/while
  15.5 4.0 %collective-permute-start.8 = (f32[256,128]{1,0:T(8,128)S(1)}, f32[256,128]{1,0:T(8,128)S(1)}, u32[]{:S(2)}, u32[]{:S(2)}) collective-permute-start(f32[256,128]{1,0:T(8,128)S(1)} %get-tuple-element.347), channel_id=1, source_target_pairs={{0,1},{1,0},{2,3},{3,2},{4,5},{5,4},{6,7},{7,6},{8,9},{9,8},{10,11... | collective-permute-start | bytes 393224 | tf_op jit(solution)/shard_map/while/body/ppermute | solution.py:220
  15.6 8.7 %collective-permute-start.12 = (f32[64,128]{1,0:T(8,128)S(1)}, f32[64,128]{1,0:T(8,128)S(1)}, u32[]{:S(2)}, u32[]{:S(2)}) collective-permute-start(f32[64,128]{1,0:T(8,128)S(1)} %get-tuple-element.352), channel_id=1, source_target_pairs={{0,248},{8,0},{16,8},{24,16},{32,24},{40,32},{48,40},{56,48},{64,5... | collective-permute-start | bytes 98312 | tf_op jit(solution)/shard_map/while/body/ppermute | solution.py:225
  19.5 4.8 %collective-permute-start.9 = (f32[64,128]{1,0:T(8,128)S(1)}, f32[64,128]{1,0:T(8,128)S(1)}, u32[]{:S(2)}, u32[]{:S(2)}) collective-permute-start(f32[64,128]{1,0:T(8,128)S(1)} %get-tuple-element.349), channel_id=1, source_target_pairs={{0,2},{1,3},{2,0},{3,1},{4,6},{5,7},{6,4},{7,5},{8,10},{9,11},{10,... | collective-permute-start | bytes 98312 | tf_op jit(solution)/shard_map/while/body/ppermute | solution.py:220
  21.2 5.4 %collective-permute-start.10 = (f32[64,128]{1,0:T(8,128)S(1)}, f32[64,128]{1,0:T(8,128)S(1)}, u32[]{:S(2)}, u32[]{:S(2)}) collective-permute-start(f32[64,128]{1,0:T(8,128)S(1)} %get-tuple-element.350), channel_id=1, source_target_pairs={{0,4},{1,5},{2,6},{3,7},{4,0},{5,1},{6,2},{7,3},{8,12},{9,13},{10,... | collective-permute-start | bytes 98312 | tf_op jit(solution)/shard_map/while/body/ppermute | solution.py:220
  24.1 5.1 %collective-permute-start.11 = (f32[64,128]{1,0:T(8,128)S(1)}, f32[64,128]{1,0:T(8,128)S(1)}, u32[]{:S(2)}, u32[]{:S(2)}) collective-permute-start(f32[64,128]{1,0:T(8,128)S(1)} %get-tuple-element.351), channel_id=1, source_target_pairs={{0,6},{1,7},{2,4},{3,5},{4,2},{5,3},{6,0},{7,1},{8,14},{9,15},{10,... | collective-permute-start | bytes 98312 | tf_op jit(solution)/shard_map/while/body/ppermute | solution.py:220
  29.2 5.2 %collective-permute-start.16 = (f32[64,128]{1,0:T(8,128)S(1)}, f32[64,128]{1,0:T(8,128)S(1)}, u32[]{:S(2)}, u32[]{:S(2)}) collective-permute-start(f32[64,128]{1,0:T(8,128)S(1)} %body.46.refs_0_.refs_6_), channel_id=1, source_target_pairs={{0,6},{1,7},{2,4},{3,5},{4,2},{5,3},{6,0},{7,1},{8,14},{9,15},{10,... | collective-permute-start | bytes 98312 | tf_op jit(solution)/shard_map/while/body/ppermute | solution.py:220
  29.5 5.4 %collective-permute-start.15 = (f32[64,128]{1,0:T(8,128)S(1)}, f32[64,128]{1,0:T(8,128)S(1)}, u32[]{:S(2)}, u32[]{:S(2)}) collective-permute-start(f32[64,128]{1,0:T(8,128)S(1)} %body.46.refs_0_.refs_6_), channel_id=1, source_target_pairs={{0,4},{1,5},{2,6},{3,7},{4,0},{5,1},{6,2},{7,3},{8,12},{9,13},{10,... | collective-permute-start | bytes 98312 | tf_op jit(solution)/shard_map/while/body/ppermute | solution.py:220
  30.3 5.3 %collective-permute-start.14 = (f32[64,128]{1,0:T(8,128)S(1)}, f32[64,128]{1,0:T(8,128)S(1)}, u32[]{:S(2)}, u32[]{:S(2)}) collective-permute-start(f32[64,128]{1,0:T(8,128)S(1)} %body.46.refs_0_.refs_6_), channel_id=1, source_target_pairs={{0,2},{1,3},{2,0},{3,1},{4,6},{5,7},{6,4},{7,5},{8,10},{9,11},{10,... | collective-permute-start | bytes 98312 | tf_op jit(solution)/shard_map/while/body/ppermute | solution.py:220
  33.4 2.2 %collective-permute-start.17 = (f32[64,128]{1,0:T(8,128)S(1)}, f32[64,128]{1,0:T(8,128)S(1)}, u32[]{:S(2)}, u32[]{:S(2)}) collective-permute-start(f32[64,128]{1,0:T(8,128)S(1)} %body.46.refs_0_.refs_6_), channel_id=1, source_target_pairs={{0,1},{1,0},{2,3},{3,2},{4,5},{5,4},{6,7},{7,6},{8,9},{9,8},{10,11... | collective-permute-start | bytes 98312 | tf_op jit(solution)/shard_map/while/body/ppermute | solution.py:220
  33.4 4.6 %collective-permute-start.13 = (f32[64,128]{1,0:T(8,128)S(1)}, f32[64,128]{1,0:T(8,128)S(1)}, u32[]{:S(2)}, u32[]{:S(2)}) collective-permute-start(f32[64,128]{1,0:T(8,128)S(1)} %body.46.refs_0_.refs_6_), channel_id=1, source_target_pairs={{0,8},{8,16},{16,24},{24,32},{32,40},{40,48},{48,56},{56,64},{64,7... | collective-permute-start | bytes 98312 | tf_op jit(solution)/shard_map/while/body/ppermute | solution.py:225
  34.4 3.6 %collective-permute-start.20 = (f32[64,128]{1,0:T(8,128)S(1)}, f32[64,128]{1,0:T(8,128)S(1)}, u32[]{:S(2)}, u32[]{:S(2)}) collective-permute-start(f32[64,128]{1,0:T(8,128)S(1)} %collective-permute-done.16.refs_3_), channel_id=1, source_target_pairs={{0,1},{1,0},{2,3},{3,2},{4,5},{5,4},{6,7},{7,6},{8,9},{9,8},{10,11... | collective-permute-start | bytes 98312 | tf_op jit(solution)/shard_map/while/body/ppermute | solution.py:220
  35.0 3.1 %collective-permute-start.19 = (f32[64,128]{1,0:T(8,128)S(1)}, f32[64,128]{1,0:T(8,128)S(1)}, u32[]{:S(2)}, u32[]{:S(2)}) collective-permute-start(f32[64,128]{1,0:T(8,128)S(1)} %collective-permute-done.15.refs_2_), channel_id=1, source_target_pairs={{0,1},{1,0},{2,3},{3,2},{4,5},{5,4},{6,7},{7,6},{8,9},{9,8},{10,11... | collective-permute-start | bytes 98312 | tf_op jit(solution)/shard_map/while/body/ppermute | solution.py:220
  35.6 2.4 %collective-permute-start.18 = (f32[64,128]{1,0:T(8,128)S(1)}, f32[64,128]{1,0:T(8,128)S(1)}, u32[]{:S(2)}, u32[]{:S(2)}) collective-permute-start(f32[64,128]{1,0:T(8,128)S(1)} %collective-permute-done.14.refs_1_), channel_id=1, source_target_pairs={{0,1},{1,0},{2,3},{3,2},{4,5},{5,4},{6,7},{7,6},{8,9},{9,8},{10,11... | collective-permute-start | bytes 98312 | tf_op jit(solution)/shard_map/while/body/ppermute | solution.py:220
  39.4 5.4 %collective-permute-start.21 = (f32[256,128]{1,0:T(8,128)S(1)}, f32[256,128]{1,0:T(8,128)S(1)}, u32[]{:S(2)}, u32[]{:S(2)}) collective-permute-start(f32[256,128]{1,0:T(8,128)S(1)} %get-tuple-element.355), channel_id=1, source_target_pairs={{0,1},{1,0},{2,3},{3,2},{4,5},{5,4},{6,7},{7,6},{8,9},{9,8},{10,11... | collective-permute-start | bytes 393224 | tf_op jit(solution)/shard_map/while/body/ppermute | solution.py:220
  39.5 10.1 %collective-permute-start.25 = (f32[64,128]{1,0:T(8,128)S(1)}, f32[64,128]{1,0:T(8,128)S(1)}, u32[]{:S(2)}, u32[]{:S(2)}) collective-permute-start(f32[64,128]{1,0:T(8,128)S(1)} %get-tuple-element.360), channel_id=1, source_target_pairs={{0,248},{8,0},{16,8},{24,16},{32,24},{40,32},{48,40},{56,48},{64,5... | collective-permute-start | bytes 98312 | tf_op jit(solution)/shard_map/while/body/ppermute | solution.py:225
  44.8 4.8 %collective-permute-start.22 = (f32[64,128]{1,0:T(8,128)S(1)}, f32[64,128]{1,0:T(8,128)S(1)}, u32[]{:S(2)}, u32[]{:S(2)}) collective-permute-start(f32[64,128]{1,0:T(8,128)S(1)} %get-tuple-element.357), channel_id=1, source_target_pairs={{0,2},{1,3},{2,0},{3,1},{4,6},{5,7},{6,4},{7,5},{8,10},{9,11},{10,... | collective-permute-start | bytes 98312 | tf_op jit(solution)/shard_map/while/body/ppermute | solution.py:220
  44.9 5.7 %collective-permute-start.23 = (f32[64,128]{1,0:T(8,128)S(1)}, f32[64,128]{1,0:T(8,128)S(1)}, u32[]{:S(2)}, u32[]{:S(2)}) collective-permute-start(f32[64,128]{1,0:T(8,128)S(1)} %get-tuple-element.358), channel_id=1, source_target_pairs={{0,4},{1,5},{2,6},{3,7},{4,0},{5,1},{6,2},{7,3},{8,12},{9,13},{10,... | collective-permute-start | bytes 98312 | tf_op jit(solution)/shard_map/while/body/ppermute | solution.py:220
  48.4 5.1 %collective-permute-start.24 = (f32[64,128]{1,0:T(8,128)S(1)}, f32[64,128]{1,0:T(8,128)S(1)}, u32[]{:S(2)}, u32[]{:S(2)}) collective-permute-start(f32[64,128]{1,0:T(8,128)S(1)} %get-tuple-element.359), channel_id=1, source_target_pairs={{0,6},{1,7},{2,4},{3,5},{4,2},{5,3},{6,0},{7,1},{8,14},{9,15},{10,... | collective-permute-start | bytes 98312 | tf_op jit(solution)/shard_map/while/body/ppermute | solution.py:220
  53.5 5.2 %collective-permute-start.29 = (f32[64,128]{1,0:T(8,128)S(1)}, f32[64,128]{1,0:T(8,128)S(1)}, u32[]{:S(2)}, u32[]{:S(2)}) collective-permute-start(f32[64,128]{1,0:T(8,128)S(1)} %body.49.refs_0_.refs_7_), channel_id=1, source_target_pairs={{0,6},{1,7},{2,4},{3,5},{4,2},{5,3},{6,0},{7,1},{8,14},{9,15},{10,... | collective-permute-start | bytes 98312 | tf_op jit(solution)/shard_map/while/body/ppermute | solution.py:220
  54.8 5.4 %collective-permute-start.28 = (f32[64,128]{1,0:T(8,128)S(1)}, f32[64,128]{1,0:T(8,128)S(1)}, u32[]{:S(2)}, u32[]{:S(2)}) collective-permute-start(f32[64,128]{1,0:T(8,128)S(1)} %body.49.refs_0_.refs_7_), channel_id=1, source_target_pairs={{0,4},{1,5},{2,6},{3,7},{4,0},{5,1},{6,2},{7,3},{8,12},{9,13},{10,... | collective-permute-start | bytes 98312 | tf_op jit(solution)/shard_map/while/body/ppermute | solution.py:220
  54.8 5.4 %collective-permute-start.27 = (f32[64,128]{1,0:T(8,128)S(1)}, f32[64,128]{1,0:T(8,128)S(1)}, u32[]{:S(2)}, u32[]{:S(2)}) collective-permute-start(f32[64,128]{1,0:T(8,128)S(1)} %body.49.refs_0_.refs_7_), channel_id=1, source_target_pairs={{0,2},{1,3},{2,0},{3,1},{4,6},{5,7},{6,4},{7,5},{8,10},{9,11},{10,... | collective-permute-start | bytes 98312 | tf_op jit(solution)/shard_map/while/body/ppermute | solution.py:220
  57.7 3.1 %collective-permute-start.30 = (f32[64,128]{1,0:T(8,128)S(1)}, f32[64,128]{1,0:T(8,128)S(1)}, u32[]{:S(2)}, u32[]{:S(2)}) collective-permute-start(f32[64,128]{1,0:T(8,128)S(1)} %body.49.refs_0_.refs_7_), channel_id=1, source_target_pairs={{0,1},{1,0},{2,3},{3,2},{4,5},{5,4},{6,7},{7,6},{8,9},{9,8},{10,11... | collective-permute-start | bytes 98312 | tf_op jit(solution)/shard_map/while/body/ppermute | solution.py:220
  57.7 3.9 %collective-permute-start.26 = (f32[64,128]{1,0:T(8,128)S(1)}, f32[64,128]{1,0:T(8,128)S(1)}, u32[]{:S(2)}, u32[]{:S(2)}) collective-permute-start(f32[64,128]{1,0:T(8,128)S(1)} %body.49.refs_0_.refs_7_), channel_id=1, source_target_pairs={{0,8},{8,16},{16,24},{24,32},{32,40},{40,48},{48,56},{56,64},{64,7... | collective-permute-start | bytes 98312 | tf_op jit(solution)/shard_map/while/body/ppermute | solution.py:225
  58.7 2.9 %collective-permute-start.33 = (f32[64,128]{1,0:T(8,128)S(1)}, f32[64,128]{1,0:T(8,128)S(1)}, u32[]{:S(2)}, u32[]{:S(2)}) collective-permute-start(f32[64,128]{1,0:T(8,128)S(1)} %collective-permute-done.29.refs_3_), channel_id=1, source_target_pairs={{0,1},{1,0},{2,3},{3,2},{4,5},{5,4},{6,7},{7,6},{8,9},{9,8},{10,11... | collective-permute-start | bytes 98312 | tf_op jit(solution)/shard_map/while/body/ppermute | solution.py:220
  60.2 1.4 %collective-permute-start.32 = (f32[64,128]{1,0:T(8,128)S(1)}, f32[64,128]{1,0:T(8,128)S(1)}, u32[]{:S(2)}, u32[]{:S(2)}) collective-permute-start(f32[64,128]{1,0:T(8,128)S(1)} %collective-permute-done.28.refs_2_), channel_id=1, source_target_pairs={{0,1},{1,0},{2,3},{3,2},{4,5},{5,4},{6,7},{7,6},{8,9},{9,8},{10,11... | collective-permute-start | bytes 98312 | tf_op jit(solution)/shard_map/while/body/ppermute | solution.py:220
  60.2 1.4 %collective-permute-start.31 = (f32[64,128]{1,0:T(8,128)S(1)}, f32[64,128]{1,0:T(8,128)S(1)}, u32[]{:S(2)}, u32[]{:S(2)}) collective-permute-start(f32[64,128]{1,0:T(8,128)S(1)} %collective-permute-done.27.refs_1_), channel_id=1, source_target_pairs={{0,1},{1,0},{2,3},{3,2},{4,5},{5,4},{6,7},{7,6},{8,9},{9,8},{10,11... | collective-permute-start | bytes 98312 | tf_op jit(solution)/shard_map/while/body/ppermute | solution.py:220
  63.4 1.4 %collective-permute-start.34 = (f32[288,128]{1,0:T(8,128)S(1)}, f32[288,128]{1,0:T(8,128)S(1)}, u32[]{:S(2)}, u32[]{:S(2)}) collective-permute-start(f32[288,128]{1,0:T(8,128)S(1)} %get-tuple-element.362), channel_id=1, source_target_pairs={{0,1},{1,0},{2,3},{3,2},{4,5},{5,4},{6,7},{7,6},{8,9},{9,8},{10,11... | collective-permute-start | bytes 442376 | tf_op jit(solution)/shard_map/while/body/ppermute | solution.py:220
  64.8 4.8 %collective-permute-start.35 = (f32[72,128]{1,0:T(8,128)S(1)}, f32[72,128]{1,0:T(8,128)S(1)}, u32[]{:S(2)}, u32[]{:S(2)}) collective-permute-start(f32[72,128]{1,0:T(8,128)S(1)} %get-tuple-element.364), channel_id=1, source_target_pairs={{0,2},{1,3},{2,0},{3,1},{4,6},{5,7},{6,4},{7,5},{8,10},{9,11},{10,... | collective-permute-start | bytes 110600 | tf_op jit(solution)/shard_map/while/body/ppermute | solution.py:220
  66.1 5.5 %collective-permute-start.36 = (f32[72,128]{1,0:T(8,128)S(1)}, f32[72,128]{1,0:T(8,128)S(1)}, u32[]{:S(2)}, u32[]{:S(2)}) collective-permute-start(f32[72,128]{1,0:T(8,128)S(1)} %get-tuple-element.365), channel_id=1, source_target_pairs={{0,4},{1,5},{2,6},{3,7},{4,0},{5,1},{6,2},{7,3},{8,12},{9,13},{10,... | collective-permute-start | bytes 110600 | tf_op jit(solution)/shard_map/while/body/ppermute | solution.py:220
  68.4 5.2 %collective-permute-start.37 = (f32[72,128]{1,0:T(8,128)S(1)}, f32[72,128]{1,0:T(8,128)S(1)}, u32[]{:S(2)}, u32[]{:S(2)}) collective-permute-start(f32[72,128]{1,0:T(8,128)S(1)} %get-tuple-element.366), channel_id=1, source_target_pairs={{0,6},{1,7},{2,4},{3,5},{4,2},{5,3},{6,0},{7,1},{8,14},{9,15},{10,... | collective-permute-start | bytes 110600 | tf_op jit(solution)/shard_map/while/body/ppermute | solution.py:220
  74.2 17.1 %all-to-all-start = ((f32[32,8,128]{2,1,0:T(8,128)}), f32[32,8,128]{2,1,0:T(8,128)S(1)}, u32[]{:S(2)}, u32[]{:S(2)}) async-start(f32[32,8,128]{2,1,0:T(8,128)} %body.52), calls=%async_computation | async-start | bytes 262144 | tf_op jit(solution)/shard_map/while/body/all_to_all | solution.py:274
  81.5 4.1 %collective-permute-start.38 = (f32[64,128]{1,0:T(8,128)S(1)}, f32[64,128]{1,0:T(8,128)S(1)}, u32[]{:S(2)}, u32[]{:S(2)}) collective-permute-start(f32[64,128]{1,0:T(8,128)S(1)} %get-tuple-element.367), channel_id=1, source_target_pairs={{0,248},{8,0},{16,8},{24,16},{32,24},{40,32},{48,40},{56,48},{64,5... | collective-permute-start | bytes 98312 | tf_op jit(solution)/shard_map/while/body/ppermute | solution.py:225

commit v4 on v3

--- a/solution.py
+++ b/solution.py
@@ -99,12 +99,18 @@
 
 def operator_kernel(step, n_fields, hot_in, hot_ex, scale_ref, in_ref, ex_ref, anchor_ref, row_ref, before_ref, *refs):
     fields = refs[:n_fields]
-    mine_ref, other_ref, back_ref, row_out, u_in, u_ex = refs[n_fields:]
+    mine_ref, other_ref, back_ref, row_out, u_in, u_ex, *held = refs[n_fields:]
+    if held:
+        copy = pltpu.make_async_copy(ex_ref, held[0], held[1])
+        copy.start()
     blk = before_ref.shape[0]
     scale = scale_ref[...]
     field = jnp.concatenate([f[...] for f in fields], 0)
     spread, energy = springs(hot_in[...], field, in_ref, scale, u_in)
     v = field[:blk]
+    if held:
+        copy.wait()
+        ex_ref = held[0]
     spread_ex, energy_ex = springs(hot_ex[...], jnp.concatenate([v, before_ref[...]], 0), ex_ref, scale, u_ex)
     back_ref[...] = spread_ex[blk:]
     image = anchor_ref[...] * v * scale
@@ -201,9 +207,11 @@
     ratio_ref[0] = jnp.max(ratio)
 
 
-def call(kernel, outs, *args, scratch=(), scalars=0, dtype=F32, flops=0, hbm=False, limit=16, scalar_outs=0):
+def call(kernel, outs, *args, scratch=(), scalars=0, dtype=F32, flops=0, hbm=(), limit=16, scalar_outs=0):
     specs = [pl.BlockSpec(memory_space=pltpu.SMEM)] * scalars
-    specs += [pl.BlockSpec(memory_space=pltpu.HBM) if hbm else VMEM] * (len(args) - scalars)
+    specs += [VMEM] * (len(args) - scalars)
+    for i in hbm:
+        specs[i] = pl.BlockSpec(memory_space=pltpu.HBM)
     dtypes = dtype if isinstance(dtype, tuple) else (dtype,) * len(outs)
     return pl.pallas_call(
         kernel,
@@ -258,10 +266,13 @@
         here = [v] + [swap(v, 2 * j) for j in (1, 2, 3)]
         fields = here + [swap(h, 1) for h in here]
         before = shifted(v, 1)
+        scratch = [pltpu.VMEM((intra_own.shape[2], node), F32), pltpu.VMEM((inter_own.shape[2], node), F32)]
+        if step == 0:
+            scratch += [pltpu.VMEM(inter_stiff.shape, BF16), pltpu.SemaphoreType.DMA]
         mine, other, back, moments = call(
             functools.partial(operator_kernel, step, len(fields)), ((4 * tall, node), (4 * tall, node), field, row),
             *hot, scale, intra_stiff, inter_stiff, anchor, moments, before, *fields,
-            scratch=[pltpu.VMEM((intra_own.shape[2], node), F32), pltpu.VMEM((inter_own.shape[2], node), F32)],
+            scratch=scratch, hbm=(4,) if step == 0 else (),
         )
         incoming = shifted(back, -1)
         got = swap(other, 1)

time: 93.7 us -> 93.9 us (level)
  no operation moved by 1% of the time
where the time goes in v4:
time: 93.9 us; the launch traced here: 93.7 us
  starting transfers between devices  47.3 us (50%)
  waiting for transfers between devices  33.4 us (36%)
  Pallas kernels  10.8 us (12%)
  loops' own time  1.53 us (2%)
    ppermute x33, starting transfers between devices, swap(): lax.ppermute(x, 'tile', [(i, i ^ by) for i in range(lax.axis_size('tile'))])  28.6 us
    ppermute x33, waiting for transfers between devices, swap(): lax.ppermute(x, 'tile', [(i, i ^ by) for i in range(lax.axis_size('tile'))])  20.8 us
    ppermute x6, starting transfers between devices, shifted(): return lax.ppermute(x, 'sec', [(i, (i + by) % peers) for i in range(peers)])  11.5 us
    pallas_call x13, Pallas kernels, call(): pl.pallas_call(kernel, out_shape=[jax.ShapeDtypeStruct(o, d) for o, d in...  10.8 us
    all_to_all x1, starting transfers between devices, one_round(): sums = lax.all_to_all(sums, 'sec', 0, 0, tiled=True)  7.28 us
    ppermute x6, waiting for transfers between devices, shifted(): return lax.ppermute(x, 'sec', [(i, (i + by) % peers) for i in range(peers)])  6.96 us
    all_to_all x1, waiting for transfers between devices, one_round(): sums = lax.all_to_all(sums, 'sec', 0, 0, tiled=True)  5.66 us
  transfers between devices with their start and end apart: 40, of which 17 were waited for; matrix products, arithmetic and copies ran while one was open for 0% of the time, Pallas kernels for 2%

profile of v4, /device:TPU:32, one launch (start us, length us, event | category | flops | bytes accessed | tf_op | source)
XLA Modules:
  0.0 93.7 jit_solution(110321011583453882)
XLA Ops:
  0.6 0.6 shard_map.113
  1.3 92.4 %while.16 = (s32[1]{0:T(128)}, f32[1]{0:T(128)}, f32[64,128]{1,0:T(8,128)}, f32[64,128]{1,0:T(8,128)}, s32[1,1]{1,0:T(1,128)}, /*index=5*/s32[1,1]{1,0:T(1,128)}...) while((s32[1]{0:T(128)}, f32[1]{0:T(128)}, ...), condition=%wide.region_1.2_spmd, body=%wide.region_0.1_spmd.sunk | while | flops 20000000000 | bytes 25815560 | solution.py:301
  1.3 0.9 body.42
  2.2 3.0 %collective-permute-start.3 = (f32[64,128]{1,0:T(8,128)S(1)}, f32[64,128]{1,0:T(8,128)S(1)}, u32[]{:S(2)}, u32[]{:S(2)}) collective-permute-start(f32[64,128]{1,0:T(8,128)S(1)} %get-tuple-element.344.refs_0_.refs_5_), channel_id=1, source_target_pairs={{0,6},{1,7},{2,4},{3,5},{4,2},{5,3},{6,0},{7,1},{8,14},{9,15},{10,... | collective-permute-start | bytes 98312 | tf_op jit(solution)/shard_map/while/body/ppermute | solution.py:228
  5.2 0.6 collective-permute-start.2
  5.9 0.5 collective-permute-start.1
  6.3 1.9 %collective-permute-start = (f32[64,128]{1,0:T(8,128)S(1)}, f32[64,128]{1,0:T(8,128)S(1)}, u32[]{:S(2)}, u32[]{:S(2)}) collective-permute-start(f32[64,128]{1,0:T(8,128)S(1)} %get-tuple-element.344.refs_0_.refs_5_), channel_id=1, source_target_pairs={{0,8},{8,16},{16,24},{24,32},{32,40},{40,48},{48,56},{56,64},{64,7... | collective-permute-start | bytes 98312 | tf_op jit(solution)/shard_map/while/body/ppermute | solution.py:233
  8.5 2.2 %collective-permute-done.2.refs_2_ = f32[64,128]{1,0:T(8,128)S(1)} collective-permute-done((f32[64,128]{1,0:T(8,128)S(1)}, f32[64,128]{1,0:T(8,128)S(1)}, u32[]{:S(2)}, u32[]{:S(2)}) %collective-permute-start.2) | collective-permute-done | bytes 32800 | tf_op jit(solution)/shard_map/while/body/ppermute | solution.py:228
  10.7 0.5 collective-permute-start.5
  11.2 1.5 %body.43 = (bf16[512,96]{1,0:T(8,128)(2,1)S(1)}, bf16[128,48]{1,0:T(8,128)(2,1)S(1)}) custom-call(s32[1]{0:T(128)} %bitcast.16.section, s32[1]{0:T(128)} %bitcast.17.tile, s32[1]{0:T(128)} %bitcast.18.count, s32[1]{0:T(128)} %bitcast.19.count_ex, s32[1,1,96]{2,1,0:T(1,128)S(1)} %copy-done.3, s32[1,1,96]{2,1,0:T(1,128)S(1)} %copy-done.4, ...), custom_call_target="tpu_custom_call" | custom-call | tf_op jit(solution)/shard_map/while/body/pallas_call | solution.py:216
  12.8 3.0 %body.44 = (f32[256,128]{1,0:T(8,128)S(1)}, f32[256,128]{1,0:T(8,128)S(1)}, f32[64,128]{1,0:T(8,128)S(1)}, f32[8,128]{1,0:T(8,128)S(1)}) custom-call(bf16[512,96]{1,0:T(8,128)(2,1)S(1)} %get-tuple-element.342.hot_in, bf16[128,48]{1,0:T(8,128)(2,1)S(1)} %get-tuple-element.343.hot_ex, f32[1,128]{1,0:T(1,128)S(1)} %get-tuple-element.341.refs_4_.scale_ref, ...), custom_call_target="tpu_custom_call" | custom-call | tf_op jit(solution)/shard_map/while/body/pallas_call | solution.py:216
  15.9 3.9 %collective-permute-start.12 = (f32[64,128]{1,0:T(8,128)S(1)}, f32[64,128]{1,0:T(8,128)S(1)}, u32[]{:S(2)}, u32[]{:S(2)}) collective-permute-start(f32[64,128]{1,0:T(8,128)S(1)} %get-tuple-element.352), channel_id=1, source_target_pairs={{0,248},{8,0},{16,8},{24,16},{32,24},{40,32},{48,40},{56,48},{64,5... | collective-permute-start | bytes 98312 | tf_op jit(solution)/shard_map/while/body/ppermute | solution.py:233
  19.7 1.7 %collective-permute-start.9 = (f32[64,128]{1,0:T(8,128)S(1)}, f32[64,128]{1,0:T(8,128)S(1)}, u32[]{:S(2)}, u32[]{:S(2)}) collective-permute-start(f32[64,128]{1,0:T(8,128)S(1)} %get-tuple-element.349), channel_id=1, source_target_pairs={{0,2},{1,3},{2,0},{3,1},{4,6},{5,7},{6,4},{7,5},{8,10},{9,11},{10,... | collective-permute-start | bytes 98312 | tf_op jit(solution)/shard_map/while/body/ppermute | solution.py:228
  21.4 2.9 %collective-permute-start.10 = (f32[64,128]{1,0:T(8,128)S(1)}, f32[64,128]{1,0:T(8,128)S(1)}, u32[]{:S(2)}, u32[]{:S(2)}) collective-permute-start(f32[64,128]{1,0:T(8,128)S(1)} %get-tuple-element.350), channel_id=1, source_target_pairs={{0,4},{1,5},{2,6},{3,7},{4,0},{5,1},{6,2},{7,3},{8,12},{9,13},{10,... | collective-permute-start | bytes 98312 | tf_op jit(solution)/shard_map/while/body/ppermute | solution.py:228
  24.5 2.3 %collective-permute-done.10.refs_2_ = f32[64,128]{1,0:T(8,128)S(1)} collective-permute-done((f32[64,128]{1,0:T(8,128)S(1)}, f32[64,128]{1,0:T(8,128)S(1)}, u32[]{:S(2)}, u32[]{:S(2)}) %collective-permute-start.10) | collective-permute-done | bytes 32800 | tf_op jit(solution)/shard_map/while/body/ppermute | solution.py:228
  26.8 2.6 %collective-permute-done.11.refs_3_ = f32[64,128]{1,0:T(8,128)S(1)} collective-permute-done((f32[64,128]{1,0:T(8,128)S(1)}, f32[64,128]{1,0:T(8,128)S(1)}, u32[]{:S(2)}, u32[]{:S(2)}) %collective-permute-start.11) | collective-permute-done | bytes 32800 | tf_op jit(solution)/shard_map/while/body/ppermute | solution.py:228
  29.8 0.8 collective-permute-start.15
  30.5 3.1 %collective-permute-start.14 = (f32[64,128]{1,0:T(8,128)S(1)}, f32[64,128]{1,0:T(8,128)S(1)}, u32[]{:S(2)}, u32[]{:S(2)}) collective-permute-start(f32[64,128]{1,0:T(8,128)S(1)} %body.46.refs_0_.refs_6_), channel_id=1, source_target_pairs={{0,2},{1,3},{2,0},{3,1},{4,6},{5,7},{6,4},{7,5},{8,10},{9,11},{10,... | collective-permute-start | bytes 98312 | tf_op jit(solution)/shard_map/while/body/ppermute | solution.py:228
  33.6 1.0 %collective-permute-done.16.refs_3_ = f32[64,128]{1,0:T(8,128)S(1)} collective-permute-done((f32[64,128]{1,0:T(8,128)S(1)}, f32[64,128]{1,0:T(8,128)S(1)}, u32[]{:S(2)}, u32[]{:S(2)}) %collective-permute-start.16) | collective-permute-done | bytes 32800 | tf_op jit(solution)/shard_map/while/body/ppermute | solution.py:228
  34.7 0.5 collective-permute-done.15.refs_2_
  35.2 0.7 collective-permute-done.14.refs_1_
  35.9 2.4 %collective-permute-done.13.before_ref = f32[64,128]{1,0:T(8,128)S(1)} collective-permute-done((f32[64,128]{1,0:T(8,128)S(1)}, f32[64,128]{1,0:T(8,128)S(1)}, u32[]{:S(2)}, u32[]{:S(2)}) %collective-permute-start.13) | collective-permute-done | bytes 32800 | tf_op jit(solution)/shard_map/while/body/ppermute | solution.py:233
  38.3 1.3 %body.47 = (f32[256,128]{1,0:T(8,128)S(1)}, f32[256,128]{1,0:T(8,128)S(1)}, f32[64,128]{1,0:T(8,128)S(1)}, f32[8,128]{1,0:T(8,128)S(1)}) custom-call(bf16[512,96]{1,0:T(8,128)(2,1)S(1)} %get-tuple-element.342.hot_in, bf16[128,48]{1,0:T(8,128)(2,1)S(1)} %get-tuple-element.343.hot_ex, f32[1,128]{1,0:T(1,128)S(1)} %get-tuple-element.341.refs_4_.scale_ref, ...), custom_call_target="tpu_custom_call" | custom-call | tf_op jit(solution)/shard_map/while/body/pallas_call | solution.py:216
  39.7 5.3 %collective-permute-start.25 = (f32[64,128]{1,0:T(8,128)S(1)}, f32[64,128]{1,0:T(8,128)S(1)}, u32[]{:S(2)}, u32[]{:S(2)}) collective-permute-start(f32[64,128]{1,0:T(8,128)S(1)} %get-tuple-element.360), channel_id=1, source_target_pairs={{0,248},{8,0},{16,8},{24,16},{32,24},{40,32},{48,40},{56,48},{64,5... | collective-permute-start | bytes 98312 | tf_op jit(solution)/shard_map/while/body/ppermute | solution.py:233
  45.1 3.5 %collective-permute-start.23 = (f32[64,128]{1,0:T(8,128)S(1)}, f32[64,128]{1,0:T(8,128)S(1)}, u32[]{:S(2)}, u32[]{:S(2)}) collective-permute-start(f32[64,128]{1,0:T(8,128)S(1)} %get-tuple-element.358), channel_id=1, source_target_pairs={{0,4},{1,5},{2,6},{3,7},{4,0},{5,1},{6,2},{7,3},{8,12},{9,13},{10,... | collective-permute-start | bytes 98312 | tf_op jit(solution)/shard_map/while/body/ppermute | solution.py:228
  48.6 1.2 %collective-permute-start.24 = (f32[64,128]{1,0:T(8,128)S(1)}, f32[64,128]{1,0:T(8,128)S(1)}, u32[]{:S(2)}, u32[]{:S(2)}) collective-permute-start(f32[64,128]{1,0:T(8,128)S(1)} %get-tuple-element.359), channel_id=1, source_target_pairs={{0,6},{1,7},{2,4},{3,5},{4,2},{5,3},{6,0},{7,1},{8,14},{9,15},{10,... | collective-permute-start | bytes 98312 | tf_op jit(solution)/shard_map/while/body/ppermute | solution.py:228
  49.8 1.0 %collective-permute-done.23.refs_2_ = f32[64,128]{1,0:T(8,128)S(1)} collective-permute-done((f32[64,128]{1,0:T(8,128)S(1)}, f32[64,128]{1,0:T(8,128)S(1)}, u32[]{:S(2)}, u32[]{:S(2)}) %collective-permute-start.23) | collective-permute-done | bytes 32800 | tf_op jit(solution)/shard_map/while/body/ppermute | solution.py:228
  50.8 2.9 %collective-permute-done.24.refs_3_ = f32[64,128]{1,0:T(8,128)S(1)} collective-permute-done((f32[64,128]{1,0:T(8,128)S(1)}, f32[64,128]{1,0:T(8,128)S(1)}, u32[]{:S(2)}, u32[]{:S(2)}) %collective-permute-start.24) | collective-permute-done | bytes 32800 | tf_op jit(solution)/shard_map/while/body/ppermute | solution.py:228
  53.7 1.3 %collective-permute-start.29 = (f32[64,128]{1,0:T(8,128)S(1)}, f32[64,128]{1,0:T(8,128)S(1)}, u32[]{:S(2)}, u32[]{:S(2)}) collective-permute-start(f32[64,128]{1,0:T(8,128)S(1)} %body.49.refs_0_.refs_7_), channel_id=1, source_target_pairs={{0,6},{1,7},{2,4},{3,5},{4,2},{5,3},{6,0},{7,1},{8,14},{9,15},{10,... | collective-permute-start | bytes 98312 | tf_op jit(solution)/shard_map/while/body/ppermute | solution.py:228
  55.0 2.9 %collective-permute-start.27 = (f32[64,128]{1,0:T(8,128)S(1)}, f32[64,128]{1,0:T(8,128)S(1)}, u32[]{:S(2)}, u32[]{:S(2)}) collective-permute-start(f32[64,128]{1,0:T(8,128)S(1)} %body.49.refs_0_.refs_7_), channel_id=1, source_target_pairs={{0,2},{1,3},{2,0},{3,1},{4,6},{5,7},{6,4},{7,5},{8,10},{9,11},{10,... | collective-permute-start | bytes 98312 | tf_op jit(solution)/shard_map/while/body/ppermute | solution.py:228
  57.9 1.0 %collective-permute-done.29.refs_3_ = f32[64,128]{1,0:T(8,128)S(1)} collective-permute-done((f32[64,128]{1,0:T(8,128)S(1)}, f32[64,128]{1,0:T(8,128)S(1)}, u32[]{:S(2)}, u32[]{:S(2)}) %collective-permute-start.29) | collective-permute-done | bytes 32800 | tf_op jit(solution)/shard_map/while/body/ppermute | solution.py:228
  58.9 1.5 %collective-permute-done.28.refs_2_ = f32[64,128]{1,0:T(8,128)S(1)} collective-permute-done((f32[64,128]{1,0:T(8,128)S(1)}, f32[64,128]{1,0:T(8,128)S(1)}, u32[]{:S(2)}, u32[]{:S(2)}) %collective-permute-start.28) | collective-permute-done | bytes 32800 | tf_op jit(solution)/shard_map/while/body/ppermute | solution.py:228
  60.5 0.5 collective-permute-start.31
  61.0 0.9 collective-permute-done.26.before_ref
  61.8 1.8 %body.50 = (f32[288,128]{1,0:T(8,128)S(1)}, f32[288,128]{1,0:T(8,128)S(1)}, f32[64,128]{1,0:T(8,128)S(1)}, f32[8,128]{1,0:T(8,128)}) custom-call(bf16[512,96]{1,0:T(8,128)(2,1)S(1)} %get-tuple-element.342.hot_in, bf16[128,48]{1,0:T(8,128)(2,1)S(1)} %get-tuple-element.343.hot_ex, f32[1,128]{1,0:T(1,128)S(1)} %get-tuple-element.341.refs_4_.scale_ref, ...), custom_call_target="tpu_custom_call" | custom-call | tf_op jit(solution)/shard_map/while/body/pallas_call | solution.py:216
  63.6 0.3 collective-permute-start.34
  64.0 1.0 %collective-permute-done.34.got_ref = f32[288,128]{1,0:T(8,128)S(1)} collective-permute-done((f32[288,128]{1,0:T(8,128)S(1)}, f32[288,128]{1,0:T(8,128)S(1)}, u32[]{:S(2)}, u32[]{:S(2)}) %collective-permute-start.34) | collective-permute-done | bytes 147488 | tf_op jit(solution)/shard_map/while/body/ppermute | solution.py:228
  65.0 1.3 %collective-permute-start.35 = (f32[72,128]{1,0:T(8,128)S(1)}, f32[72,128]{1,0:T(8,128)S(1)}, u32[]{:S(2)}, u32[]{:S(2)}) collective-permute-start(f32[72,128]{1,0:T(8,128)S(1)} %get-tuple-element.364), channel_id=1, source_target_pairs={{0,2},{1,3},{2,0},{3,1},{4,6},{5,7},{6,4},{7,5},{8,10},{9,11},{10,... | collective-permute-start | bytes 110600 | tf_op jit(solution)/shard_map/while/body/ppermute | solution.py:228
  66.3 2.3 %collective-permute-start.36 = (f32[72,128]{1,0:T(8,128)S(1)}, f32[72,128]{1,0:T(8,128)S(1)}, u32[]{:S(2)}, u32[]{:S(2)}) collective-permute-start(f32[72,128]{1,0:T(8,128)S(1)} %get-tuple-element.365), channel_id=1, source_target_pairs={{0,4},{1,5},{2,6},{3,7},{4,0},{5,1},{6,2},{7,3},{8,12},{9,13},{10,... | collective-permute-start | bytes 110600 | tf_op jit(solution)/shard_map/while/body/ppermute | solution.py:228
  68.6 1.2 %collective-permute-start.37 = (f32[72,128]{1,0:T(8,128)S(1)}, f32[72,128]{1,0:T(8,128)S(1)}, u32[]{:S(2)}, u32[]{:S(2)}) collective-permute-start(f32[72,128]{1,0:T(8,128)S(1)} %get-tuple-element.366), channel_id=1, source_target_pairs={{0,6},{1,7},{2,4},{3,5},{4,2},{5,3},{6,0},{7,1},{8,14},{9,15},{10,... | collective-permute-start | bytes 110600 | tf_op jit(solution)/shard_map/while/body/ppermute | solution.py:228
  69.8 1.9 %collective-permute-done.36.refs_2_ = f32[72,128]{1,0:T(8,128)S(1)} collective-permute-done((f32[72,128]{1,0:T(8,128)S(1)}, f32[72,128]{1,0:T(8,128)S(1)}, u32[]{:S(2)}, u32[]{:S(2)}) %collective-permute-start.36) | collective-permute-done | bytes 36896 | tf_op jit(solution)/shard_map/while/body/ppermute | solution.py:228
  71.8 2.0 %collective-permute-done.37.refs_3_ = f32[72,128]{1,0:T(8,128)S(1)} collective-permute-done((f32[72,128]{1,0:T(8,128)S(1)}, f32[72,128]{1,0:T(8,128)S(1)}, u32[]{:S(2)}, u32[]{:S(2)}) %collective-permute-start.37) | collective-permute-done | bytes 36896 | tf_op jit(solution)/shard_map/while/body/ppermute | solution.py:228
  73.7 0.7 body.52
  74.4 7.3 %all-to-all-start = ((f32[32,8,128]{2,1,0:T(8,128)}), f32[32,8,128]{2,1,0:T(8,128)S(1)}, u32[]{:S(2)}, u32[]{:S(2)}) async-start(f32[32,8,128]{2,1,0:T(8,128)} %body.52), calls=%async_computation | async-start | bytes 262144 | tf_op jit(solution)/shard_map/while/body/all_to_all | solution.py:285
  81.7 0.4 collective-permute-start.38
  82.1 3.7 %collective-permute-done.38.refs_4_ = f32[64,128]{1,0:T(8,128)S(1)} collective-permute-done((f32[64,128]{1,0:T(8,128)S(1)}, f32[64,128]{1,0:T(8,128)S(1)}, u32[]{:S(2)}, u32[]{:S(2)}) %collective-permute-start.38) | collective-permute-done | bytes 32800 | tf_op jit(solution)/shard_map/while/body/ppermute | solution.py:233
  85.8 5.7 %all-to-all-done.sums_ref = f32[32,8,128]{2,1,0:T(8,128)S(1)} async-done(((f32[32,8,128]{2,1,0:T(8,128)}), f32[32,8,128]{2,1,0:T(8,128)S(1)}, u32[]{:S(2)}, u32[]{:S(2)}) %all-to-all-start) | async-done | bytes 131104 | tf_op jit(solution)/shard_map/while/body/all_to_all | solution.py:285
  91.5 0.9 body.53
  (61 shorter events, 1.2 us)
Async XLA Ops:
  1.3 9.9 %copy-start.3 = (s32[1,1,96]{2,1,0:T(1,128)S(1)}, s32[1,1,96]{2,1,0:T(1,128)}, u32[]{:S(2)}) copy-start(s32[1,1,96]{2,1,0:T(1,128)} %get-tuple-element.419.refs_0_) | copy-start | bytes 1156 | tf_op jit(solution)/shard_map/while
  1.3 9.9 %copy-start.4 = (s32[1,1,96]{2,1,0:T(1,128)S(1)}, s32[1,1,96]{2,1,0:T(1,128)}, u32[]{:S(2)}) copy-start(s32[1,1,96]{2,1,0:T(1,128)} %get-tuple-element.420.refs_1_) | copy-start | bytes 1156 | tf_op jit(solution)/shard_map/while
  1.3 9.9 %copy-start.5 = (s32[1,1,48]{2,1,0:T(1,128)S(1)}, s32[1,1,48]{2,1,0:T(1,128)}, u32[]{:S(2)}) copy-start(s32[1,1,48]{2,1,0:T(1,128)} %get-tuple-element.421.refs_2_) | copy-start | bytes 580 | tf_op jit(solution)/shard_map/while
  1.3 9.9 %copy-start.6 = (s32[1,1,48]{2,1,0:T(1,128)S(1)}, s32[1,1,48]{2,1,0:T(1,128)}, u32[]{:S(2)}) copy-start(s32[1,1,48]{2,1,0:T(1,128)} %get-tuple-element.422.refs_3_) | copy-start | bytes 580 | tf_op jit(solution)/shard_map/while
  1.3 11.5 %copy-start = (bf16[1,1,96,128,128]{4,3,2,1,0:T(8,128)(2,1)S(1)}, bf16[1,1,96,128,128]{4,3,2,1,0:T(8,128)(2,1)}, u32[]{:S(2)}) copy-start(bf16[1,1,96,128,128]{4,3,2,1,0:T(8,128)(2,1)} %get-tuple-element.424.in_ref) | copy-start | bytes 9437188 | tf_op jit(solution)/shard_map/while
  1.3 11.5 %copy-start.2 = (f32[1,1,64,128]{3,2,1,0:T(8,128)S(1)}, f32[1,1,64,128]{3,2,1,0:T(8,128)}, u32[]{:S(2)}) copy-start(f32[1,1,64,128]{3,2,1,0:T(8,128)} %get-tuple-element.423) | copy-start | bytes 98308 | tf_op jit(solution)/shard_map/while
  2.2 6.0 %collective-permute-start.3 = (f32[64,128]{1,0:T(8,128)S(1)}, f32[64,128]{1,0:T(8,128)S(1)}, u32[]{:S(2)}, u32[]{:S(2)}) collective-permute-start(f32[64,128]{1,0:T(8,128)S(1)} %get-tuple-element.344.refs_0_.refs_5_), channel_id=1, source_target_pairs={{0,6},{1,7},{2,4},{3,5},{4,2},{5,3},{6,0},{7,1},{8,14},{9,15},{10,... | collective-permute-start | bytes 98312 | tf_op jit(solution)/shard_map/while/body/ppermute | solution.py:228
  5.2 5.4 %collective-permute-start.2 = (f32[64,128]{1,0:T(8,128)S(1)}, f32[64,128]{1,0:T(8,128)S(1)}, u32[]{:S(2)}, u32[]{:S(2)}) collective-permute-start(f32[64,128]{1,0:T(8,128)S(1)} %get-tuple-element.344.refs_0_.refs_5_), channel_id=1, source_target_pairs={{0,4},{1,5},{2,6},{3,7},{4,0},{5,1},{6,2},{7,3},{8,12},{9,13},{10,... | collective-permute-start | bytes 98312 | tf_op jit(solution)/shard_map/while/body/ppermute | solution.py:228
  5.9 4.8 %collective-permute-start.1 = (f32[64,128]{1,0:T(8,128)S(1)}, f32[64,128]{1,0:T(8,128)S(1)}, u32[]{:S(2)}, u32[]{:S(2)}) collective-permute-start(f32[64,128]{1,0:T(8,128)S(1)} %get-tuple-element.344.refs_0_.refs_5_), channel_id=1, source_target_pairs={{0,2},{1,3},{2,0},{3,1},{4,6},{5,7},{6,4},{7,5},{8,10},{9,11},{10,... | collective-permute-start | bytes 98312 | tf_op jit(solution)/shard_map/while/body/ppermute | solution.py:228
  6.3 6.4 %collective-permute-start.4 = (f32[64,128]{1,0:T(8,128)S(1)}, f32[64,128]{1,0:T(8,128)S(1)}, u32[]{:S(2)}, u32[]{:S(2)}) collective-permute-start(f32[64,128]{1,0:T(8,128)S(1)} %get-tuple-element.344.refs_0_.refs_5_), channel_id=1, source_target_pairs={{0,1},{1,0},{2,3},{3,2},{4,5},{5,4},{6,7},{7,6},{8,9},{9,8},{10,11... | collective-permute-start | bytes 98312 | tf_op jit(solution)/shard_map/while/body/ppermute | solution.py:228
  6.3 6.4 %collective-permute-start = (f32[64,128]{1,0:T(8,128)S(1)}, f32[64,128]{1,0:T(8,128)S(1)}, u32[]{:S(2)}, u32[]{:S(2)}) collective-permute-start(f32[64,128]{1,0:T(8,128)S(1)} %get-tuple-element.344.refs_0_.refs_5_), channel_id=1, source_target_pairs={{0,8},{8,16},{16,24},{24,32},{32,40},{40,48},{48,56},{56,64},{64,7... | collective-permute-start | bytes 98312 | tf_op jit(solution)/shard_map/while/body/ppermute | solution.py:233
  8.2 4.5 %collective-permute-start.7 = (f32[64,128]{1,0:T(8,128)S(1)}, f32[64,128]{1,0:T(8,128)S(1)}, u32[]{:S(2)}, u32[]{:S(2)}) collective-permute-start(f32[64,128]{1,0:T(8,128)S(1)} %collective-permute-done.3.refs_3_), channel_id=1, source_target_pairs={{0,1},{1,0},{2,3},{3,2},{4,5},{5,4},{6,7},{7,6},{8,9},{9,8},{10,11... | collective-permute-start | bytes 98312 | tf_op jit(solution)/shard_map/while/body/ppermute | solution.py:228
  10.6 2.1 %collective-permute-start.6 = (f32[64,128]{1,0:T(8,128)S(1)}, f32[64,128]{1,0:T(8,128)S(1)}, u32[]{:S(2)}, u32[]{:S(2)}) collective-permute-start(f32[64,128]{1,0:T(8,128)S(1)} %collective-permute-done.2.refs_2_), channel_id=1, source_target_pairs={{0,1},{1,0},{2,3},{3,2},{4,5},{5,4},{6,7},{7,6},{8,9},{9,8},{10,11... | collective-permute-start | bytes 98312 | tf_op jit(solution)/shard_map/while/body/ppermute | solution.py:228
  10.7 2.1 %collective-permute-start.5 = (f32[64,128]{1,0:T(8,128)S(1)}, f32[64,128]{1,0:T(8,128)S(1)}, u32[]{:S(2)}, u32[]{:S(2)}) collective-permute-start(f32[64,128]{1,0:T(8,128)S(1)} %collective-permute-done.1.refs_1_), channel_id=1, source_target_pairs={{0,1},{1,0},{2,3},{3,2},{4,5},{5,4},{6,7},{7,6},{8,9},{9,8},{10,11... | collective-permute-start | bytes 98312 | tf_op jit(solution)/shard_map/while/body/ppermute | solution.py:228
  11.2 27.1 %copy-start.1 = (bf16[1,1,48,128,128]{4,3,2,1,0:T(8,128)(2,1)S(1)}, bf16[1,1,48,128,128]{4,3,2,1,0:T(8,128)(2,1)}, u32[]{:S(2)}) copy-start(bf16[1,1,48,128,128]{4,3,2,1,0:T(8,128)(2,1)} %get-tuple-element.425.ex_ref) | copy-start | bytes 4718596 | tf_op jit(solution)/shard_map/while
  15.8 4.0 %collective-permute-start.8 = (f32[256,128]{1,0:T(8,128)S(1)}, f32[256,128]{1,0:T(8,128)S(1)}, u32[]{:S(2)}, u32[]{:S(2)}) collective-permute-start(f32[256,128]{1,0:T(8,128)S(1)} %get-tuple-element.347), channel_id=1, source_target_pairs={{0,1},{1,0},{2,3},{3,2},{4,5},{5,4},{6,7},{7,6},{8,9},{9,8},{10,11... | collective-permute-start | bytes 393224 | tf_op jit(solution)/shard_map/while/body/ppermute | solution.py:228
  15.9 8.7 %collective-permute-start.12 = (f32[64,128]{1,0:T(8,128)S(1)}, f32[64,128]{1,0:T(8,128)S(1)}, u32[]{:S(2)}, u32[]{:S(2)}) collective-permute-start(f32[64,128]{1,0:T(8,128)S(1)} %get-tuple-element.352), channel_id=1, source_target_pairs={{0,248},{8,0},{16,8},{24,16},{32,24},{40,32},{48,40},{56,48},{64,5... | collective-permute-start | bytes 98312 | tf_op jit(solution)/shard_map/while/body/ppermute | solution.py:233
  19.7 4.8 %collective-permute-start.9 = (f32[64,128]{1,0:T(8,128)S(1)}, f32[64,128]{1,0:T(8,128)S(1)}, u32[]{:S(2)}, u32[]{:S(2)}) collective-permute-start(f32[64,128]{1,0:T(8,128)S(1)} %get-tuple-element.349), channel_id=1, source_target_pairs={{0,2},{1,3},{2,0},{3,1},{4,6},{5,7},{6,4},{7,5},{8,10},{9,11},{10,... | collective-permute-start | bytes 98312 | tf_op jit(solution)/shard_map/while/body/ppermute | solution.py:228
  21.4 5.4 %collective-permute-start.10 = (f32[64,128]{1,0:T(8,128)S(1)}, f32[64,128]{1,0:T(8,128)S(1)}, u32[]{:S(2)}, u32[]{:S(2)}) collective-permute-start(f32[64,128]{1,0:T(8,128)S(1)} %get-tuple-element.350), channel_id=1, source_target_pairs={{0,4},{1,5},{2,6},{3,7},{4,0},{5,1},{6,2},{7,3},{8,12},{9,13},{10,... | collective-permute-start | bytes 98312 | tf_op jit(solution)/shard_map/while/body/ppermute | solution.py:228
  24.3 5.1 %collective-permute-start.11 = (f32[64,128]{1,0:T(8,128)S(1)}, f32[64,128]{1,0:T(8,128)S(1)}, u32[]{:S(2)}, u32[]{:S(2)}) collective-permute-start(f32[64,128]{1,0:T(8,128)S(1)} %get-tuple-element.351), channel_id=1, source_target_pairs={{0,6},{1,7},{2,4},{3,5},{4,2},{5,3},{6,0},{7,1},{8,14},{9,15},{10,... | collective-permute-start | bytes 98312 | tf_op jit(solution)/shard_map/while/body/ppermute | solution.py:228
  29.4 5.2 %collective-permute-start.16 = (f32[64,128]{1,0:T(8,128)S(1)}, f32[64,128]{1,0:T(8,128)S(1)}, u32[]{:S(2)}, u32[]{:S(2)}) collective-permute-start(f32[64,128]{1,0:T(8,128)S(1)} %body.46.refs_0_.refs_6_), channel_id=1, source_target_pairs={{0,6},{1,7},{2,4},{3,5},{4,2},{5,3},{6,0},{7,1},{8,14},{9,15},{10,... | collective-permute-start | bytes 98312 | tf_op jit(solution)/shard_map/while/body/ppermute | solution.py:228
  29.8 5.4 %collective-permute-start.15 = (f32[64,128]{1,0:T(8,128)S(1)}, f32[64,128]{1,0:T(8,128)S(1)}, u32[]{:S(2)}, u32[]{:S(2)}) collective-permute-start(f32[64,128]{1,0:T(8,128)S(1)} %body.46.refs_0_.refs_6_), channel_id=1, source_target_pairs={{0,4},{1,5},{2,6},{3,7},{4,0},{5,1},{6,2},{7,3},{8,12},{9,13},{10,... | collective-permute-start | bytes 98312 | tf_op jit(solution)/shard_map/while/body/ppermute | solution.py:228
  30.5 5.3 %collective-permute-start.14 = (f32[64,128]{1,0:T(8,128)S(1)}, f32[64,128]{1,0:T(8,128)S(1)}, u32[]{:S(2)}, u32[]{:S(2)}) collective-permute-start(f32[64,128]{1,0:T(8,128)S(1)} %body.46.refs_0_.refs_6_), channel_id=1, source_target_pairs={{0,2},{1,3},{2,0},{3,1},{4,6},{5,7},{6,4},{7,5},{8,10},{9,11},{10,... | collective-permute-start | bytes 98312 | tf_op jit(solution)/shard_map/while/body/ppermute | solution.py:228
  33.6 2.2 %collective-permute-start.17 = (f32[64,128]{1,0:T(8,128)S(1)}, f32[64,128]{1,0:T(8,128)S(1)}, u32[]{:S(2)}, u32[]{:S(2)}) collective-permute-start(f32[64,128]{1,0:T(8,128)S(1)} %body.46.refs_0_.refs_6_), channel_id=1, source_target_pairs={{0,1},{1,0},{2,3},{3,2},{4,5},{5,4},{6,7},{7,6},{8,9},{9,8},{10,11... | collective-permute-start | bytes 98312 | tf_op jit(solution)/shard_map/while/body/ppermute | solution.py:228
  33.6 4.6 %collective-permute-start.13 = (f32[64,128]{1,0:T(8,128)S(1)}, f32[64,128]{1,0:T(8,128)S(1)}, u32[]{:S(2)}, u32[]{:S(2)}) collective-permute-start(f32[64,128]{1,0:T(8,128)S(1)} %body.46.refs_0_.refs_6_), channel_id=1, source_target_pairs={{0,8},{8,16},{16,24},{24,32},{32,40},{40,48},{48,56},{56,64},{64,7... | collective-permute-start | bytes 98312 | tf_op jit(solution)/shard_map/while/body/ppermute | solution.py:233
  34.7 3.6 %collective-permute-start.20 = (f32[64,128]{1,0:T(8,128)S(1)}, f32[64,128]{1,0:T(8,128)S(1)}, u32[]{:S(2)}, u32[]{:S(2)}) collective-permute-start(f32[64,128]{1,0:T(8,128)S(1)} %collective-permute-done.16.refs_3_), channel_id=1, source_target_pairs={{0,1},{1,0},{2,3},{3,2},{4,5},{5,4},{6,7},{7,6},{8,9},{9,8},{10,11... | collective-permute-start | bytes 98312 | tf_op jit(solution)/shard_map/while/body/ppermute | solution.py:228
  35.2 3.1 %collective-permute-start.19 = (f32[64,128]{1,0:T(8,128)S(1)}, f32[64,128]{1,0:T(8,128)S(1)}, u32[]{:S(2)}, u32[]{:S(2)}) collective-permute-start(f32[64,128]{1,0:T(8,128)S(1)} %collective-permute-done.15.refs_2_), channel_id=1, source_target_pairs={{0,1},{1,0},{2,3},{3,2},{4,5},{5,4},{6,7},{7,6},{8,9},{9,8},{10,11... | collective-permute-start | bytes 98312 | tf_op jit(solution)/shard_map/while/body/ppermute | solution.py:228
  35.9 2.4 %collective-permute-start.18 = (f32[64,128]{1,0:T(8,128)S(1)}, f32[64,128]{1,0:T(8,128)S(1)}, u32[]{:S(2)}, u32[]{:S(2)}) collective-permute-start(f32[64,128]{1,0:T(8,128)S(1)} %collective-permute-done.14.refs_1_), channel_id=1, source_target_pairs={{0,1},{1,0},{2,3},{3,2},{4,5},{5,4},{6,7},{7,6},{8,9},{9,8},{10,11... | collective-permute-start | bytes 98312 | tf_op jit(solution)/shard_map/while/body/ppermute | solution.py:228
  39.6 5.4 %collective-permute-start.21 = (f32[256,128]{1,0:T(8,128)S(1)}, f32[256,128]{1,0:T(8,128)S(1)}, u32[]{:S(2)}, u32[]{:S(2)}) collective-permute-start(f32[256,128]{1,0:T(8,128)S(1)} %get-tuple-element.355), channel_id=1, source_target_pairs={{0,1},{1,0},{2,3},{3,2},{4,5},{5,4},{6,7},{7,6},{8,9},{9,8},{10,11... | collective-permute-start | bytes 393224 | tf_op jit(solution)/shard_map/while/body/ppermute | solution.py:228
  39.7 10.1 %collective-permute-start.25 = (f32[64,128]{1,0:T(8,128)S(1)}, f32[64,128]{1,0:T(8,128)S(1)}, u32[]{:S(2)}, u32[]{:S(2)}) collective-permute-start(f32[64,128]{1,0:T(8,128)S(1)} %get-tuple-element.360), channel_id=1, source_target_pairs={{0,248},{8,0},{16,8},{24,16},{32,24},{40,32},{48,40},{56,48},{64,5... | collective-permute-start | bytes 98312 | tf_op jit(solution)/shard_map/while/body/ppermute | solution.py:233
  45.0 4.8 %collective-permute-start.22 = (f32[64,128]{1,0:T(8,128)S(1)}, f32[64,128]{1,0:T(8,128)S(1)}, u32[]{:S(2)}, u32[]{:S(2)}) collective-permute-start(f32[64,128]{1,0:T(8,128)S(1)} %get-tuple-element.357), channel_id=1, source_target_pairs={{0,2},{1,3},{2,0},{3,1},{4,6},{5,7},{6,4},{7,5},{8,10},{9,11},{10,... | collective-permute-start | bytes 98312 | tf_op jit(solution)/shard_map/while/body/ppermute | solution.py:228
  45.1 5.7 %collective-permute-start.23 = (f32[64,128]{1,0:T(8,128)S(1)}, f32[64,128]{1,0:T(8,128)S(1)}, u32[]{:S(2)}, u32[]{:S(2)}) collective-permute-start(f32[64,128]{1,0:T(8,128)S(1)} %get-tuple-element.358), channel_id=1, source_target_pairs={{0,4},{1,5},{2,6},{3,7},{4,0},{5,1},{6,2},{7,3},{8,12},{9,13},{10,... | collective-permute-start | bytes 98312 | tf_op jit(solution)/shard_map/while/body/ppermute | solution.py:228
  48.6 5.1 %collective-permute-start.24 = (f32[64,128]{1,0:T(8,128)S(1)}, f32[64,128]{1,0:T(8,128)S(1)}, u32[]{:S(2)}, u32[]{:S(2)}) collective-permute-start(f32[64,128]{1,0:T(8,128)S(1)} %get-tuple-element.359), channel_id=1, source_target_pairs={{0,6},{1,7},{2,4},{3,5},{4,2},{5,3},{6,0},{7,1},{8,14},{9,15},{10,... | collective-permute-start | bytes 98312 | tf_op jit(solution)/shard_map/while/body/ppermute | solution.py:228
  53.7 5.2 %collective-permute-start.29 = (f32[64,128]{1,0:T(8,128)S(1)}, f32[64,128]{1,0:T(8,128)S(1)}, u32[]{:S(2)}, u32[]{:S(2)}) collective-permute-start(f32[64,128]{1,0:T(8,128)S(1)} %body.49.refs_0_.refs_7_), channel_id=1, source_target_pairs={{0,6},{1,7},{2,4},{3,5},{4,2},{5,3},{6,0},{7,1},{8,14},{9,15},{10,... | collective-permute-start | bytes 98312 | tf_op jit(solution)/shard_map/while/body/ppermute | solution.py:228
  55.0 5.4 %collective-permute-start.28 = (f32[64,128]{1,0:T(8,128)S(1)}, f32[64,128]{1,0:T(8,128)S(1)}, u32[]{:S(2)}, u32[]{:S(2)}) collective-permute-start(f32[64,128]{1,0:T(8,128)S(1)} %body.49.refs_0_.refs_7_), channel_id=1, source_target_pairs={{0,4},{1,5},{2,6},{3,7},{4,0},{5,1},{6,2},{7,3},{8,12},{9,13},{10,... | collective-permute-start | bytes 98312 | tf_op jit(solution)/shard_map/while/body/ppermute | solution.py:228
  55.0 5.4 %collective-permute-start.27 = (f32[64,128]{1,0:T(8,128)S(1)}, f32[64,128]{1,0:T(8,128)S(1)}, u32[]{:S(2)}, u32[]{:S(2)}) collective-permute-start(f32[64,128]{1,0:T(8,128)S(1)} %body.49.refs_0_.refs_7_), channel_id=1, source_target_pairs={{0,2},{1,3},{2,0},{3,1},{4,6},{5,7},{6,4},{7,5},{8,10},{9,11},{10,... | collective-permute-start | bytes 98312 | tf_op jit(solution)/shard_map/while/body/ppermute | solution.py:228
  57.9 3.1 %collective-permute-start.30 = (f32[64,128]{1,0:T(8,128)S(1)}, f32[64,128]{1,0:T(8,128)S(1)}, u32[]{:S(2)}, u32[]{:S(2)}) collective-permute-start(f32[64,128]{1,0:T(8,128)S(1)} %body.49.refs_0_.refs_7_), channel_id=1, source_target_pairs={{0,1},{1,0},{2,3},{3,2},{4,5},{5,4},{6,7},{7,6},{8,9},{9,8},{10,11... | collective-permute-start | bytes 98312 | tf_op jit(solution)/shard_map/while/body/ppermute | solution.py:228
  57.9 3.9 %collective-permute-start.26 = (f32[64,128]{1,0:T(8,128)S(1)}, f32[64,128]{1,0:T(8,128)S(1)}, u32[]{:S(2)}, u32[]{:S(2)}) collective-permute-start(f32[64,128]{1,0:T(8,128)S(1)} %body.49.refs_0_.refs_7_), channel_id=1, source_target_pairs={{0,8},{8,16},{16,24},{24,32},{32,40},{40,48},{48,56},{56,64},{64,7... | collective-permute-start | bytes 98312 | tf_op jit(solution)/shard_map/while/body/ppermute | solution.py:233
  58.9 2.9 %collective-permute-start.33 = (f32[64,128]{1,0:T(8,128)S(1)}, f32[64,128]{1,0:T(8,128)S(1)}, u32[]{:S(2)}, u32[]{:S(2)}) collective-permute-start(f32[64,128]{1,0:T(8,128)S(1)} %collective-permute-done.29.refs_3_), channel_id=1, source_target_pairs={{0,1},{1,0},{2,3},{3,2},{4,5},{5,4},{6,7},{7,6},{8,9},{9,8},{10,11... | collective-permute-start | bytes 98312 | tf_op jit(solution)/shard_map/while/body/ppermute | solution.py:228
  60.4 1.4 %collective-permute-start.32 = (f32[64,128]{1,0:T(8,128)S(1)}, f32[64,128]{1,0:T(8,128)S(1)}, u32[]{:S(2)}, u32[]{:S(2)}) collective-permute-start(f32[64,128]{1,0:T(8,128)S(1)} %collective-permute-done.28.refs_2_), channel_id=1, source_target_pairs={{0,1},{1,0},{2,3},{3,2},{4,5},{5,4},{6,7},{7,6},{8,9},{9,8},{10,11... | collective-permute-start | bytes 98312 | tf_op jit(solution)/shard_map/while/body/ppermute | solution.py:228
  60.5 1.4 %collective-permute-start.31 = (f32[64,128]{1,0:T(8,128)S(1)}, f32[64,128]{1,0:T(8,128)S(1)}, u32[]{:S(2)}, u32[]{:S(2)}) collective-permute-start(f32[64,128]{1,0:T(8,128)S(1)} %collective-permute-done.27.refs_1_), channel_id=1, source_target_pairs={{0,1},{1,0},{2,3},{3,2},{4,5},{5,4},{6,7},{7,6},{8,9},{9,8},{10,11... | collective-permute-start | bytes 98312 | tf_op jit(solution)/shard_map/while/body/ppermute | solution.py:228
  63.6 1.4 %collective-permute-start.34 = (f32[288,128]{1,0:T(8,128)S(1)}, f32[288,128]{1,0:T(8,128)S(1)}, u32[]{:S(2)}, u32[]{:S(2)}) collective-permute-start(f32[288,128]{1,0:T(8,128)S(1)} %get-tuple-element.362), channel_id=1, source_target_pairs={{0,1},{1,0},{2,3},{3,2},{4,5},{5,4},{6,7},{7,6},{8,9},{9,8},{10,11... | collective-permute-start | bytes 442376 | tf_op jit(solution)/shard_map/while/body/ppermute | solution.py:228
  65.0 4.8 %collective-permute-start.35 = (f32[72,128]{1,0:T(8,128)S(1)}, f32[72,128]{1,0:T(8,128)S(1)}, u32[]{:S(2)}, u32[]{:S(2)}) collective-permute-start(f32[72,128]{1,0:T(8,128)S(1)} %get-tuple-element.364), channel_id=1, source_target_pairs={{0,2},{1,3},{2,0},{3,1},{4,6},{5,7},{6,4},{7,5},{8,10},{9,11},{10,... | collective-permute-start | bytes 110600 | tf_op jit(solution)/shard_map/while/body/ppermute | solution.py:228
  66.3 5.5 %collective-permute-start.36 = (f32[72,128]{1,0:T(8,128)S(1)}, f32[72,128]{1,0:T(8,128)S(1)}, u32[]{:S(2)}, u32[]{:S(2)}) collective-permute-start(f32[72,128]{1,0:T(8,128)S(1)} %get-tuple-element.365), channel_id=1, source_target_pairs={{0,4},{1,5},{2,6},{3,7},{4,0},{5,1},{6,2},{7,3},{8,12},{9,13},{10,... | collective-permute-start | bytes 110600 | tf_op jit(solution)/shard_map/while/body/ppermute | solution.py:228
  68.6 5.2 %collective-permute-start.37 = (f32[72,128]{1,0:T(8,128)S(1)}, f32[72,128]{1,0:T(8,128)S(1)}, u32[]{:S(2)}, u32[]{:S(2)}) collective-permute-start(f32[72,128]{1,0:T(8,128)S(1)} %get-tuple-element.366), channel_id=1, source_target_pairs={{0,6},{1,7},{2,4},{3,5},{4,2},{5,3},{6,0},{7,1},{8,14},{9,15},{10,... | collective-permute-start | bytes 110600 | tf_op jit(solution)/shard_map/while/body/ppermute | solution.py:228
  74.4 17.1 %all-to-all-start = ((f32[32,8,128]{2,1,0:T(8,128)}), f32[32,8,128]{2,1,0:T(8,128)S(1)}, u32[]{:S(2)}, u32[]{:S(2)}) async-start(f32[32,8,128]{2,1,0:T(8,128)} %body.52), calls=%async_computation | async-start | bytes 262144 | tf_op jit(solution)/shard_map/while/body/all_to_all | solution.py:285
  81.7 4.1 %collective-permute-start.38 = (f32[64,128]{1,0:T(8,128)S(1)}, f32[64,128]{1,0:T(8,128)S(1)}, u32[]{:S(2)}, u32[]{:S(2)}) collective-permute-start(f32[64,128]{1,0:T(8,128)S(1)} %get-tuple-element.367), channel_id=1, source_target_pairs={{0,248},{8,0},{16,8},{24,16},{32,24},{40,32},{48,40},{56,48},{64,5... | collective-permute-start | bytes 98312 | tf_op jit(solution)/shard_map/while/body/ppermute | solution.py:233

commit v5 on v3

--- a/solution.py
+++ b/solution.py
@@ -220,9 +220,9 @@
     return lax.ppermute(x, "tile", [(i, i ^ by) for i in range(lax.axis_size("tile"))])
 
 
-def shifted(x, by):
+def shifted(x, by, wrap=True):
     peers = lax.axis_size("sec")
-    return lax.ppermute(x, "sec", [(i, (i + by) % peers) for i in range(peers)])
+    return lax.ppermute(x, "sec", [(i, (i + by) % peers) for i in range(peers) if wrap or 0 <= i + by < peers])
 
 
 def one_round(
@@ -263,7 +263,7 @@
             *hot, scale, intra_stiff, inter_stiff, anchor, moments, before, *fields,
             scratch=[pltpu.VMEM((intra_own.shape[2], node), F32), pltpu.VMEM((inter_own.shape[2], node), F32)],
         )
-        incoming = shifted(back, -1)
+        incoming = shifted(back, -1, not last)
         got = swap(other, 1)
         p0, p3, p1, p2 = call(pair_kernel, ((tall, node),) * 4, mine, got)
         parts = [p0] + [swap(p, 2 * j) for j, p in ((1, p1), (2, p2), (3, p3))]

time: 93.7 us -> 93.7 us (level)
  waiting for transfers between devices: 33.4 us -> 31.4 us
  starting transfers between devices: 47.3 us -> 49.2 us
    ppermute x6, starting transfers between devices: 11.5 us -> 13.3 us  [shifted(): lax.ppermute(x, 'sec', [(i, (i + by) % peers) for i in range(peers) if wr...]
    all_to_all x1, waiting for transfers between devices: 5.66 us -> 3.87 us  [one_round(): sums = lax.all_to_all(sums, 'sec', 0, 0, tiled=True)]
where the time goes in v5:
time: 93.7 us; the launch traced here: 93.4 us
  starting transfers between devices  49.2 us (53%)
  waiting for transfers between devices  31.4 us (34%)
  Pallas kernels  10.6 us (11%)
  loops' own time  1.54 us (2%)
    ppermute x33, starting transfers between devices, swap(): lax.ppermute(x, 'tile', [(i, i ^ by) for i in range(lax.axis_size('tile'))])  28.6 us
    ppermute x33, waiting for transfers between devices, swap(): lax.ppermute(x, 'tile', [(i, i ^ by) for i in range(lax.axis_size('tile'))])  20.8 us
    ppermute x6, starting transfers between devices, shifted(): lax.ppermute(x, 'sec', [(i, (i + by) % peers) for i in range(peers) if wr...  13.3 us
    pallas_call x13, Pallas kernels, call(): pl.pallas_call(kernel, out_shape=[jax.ShapeDtypeStruct(o, d) for o, d in...  10.6 us
    all_to_all x1, starting transfers between devices, one_round(): sums = lax.all_to_all(sums, 'sec', 0, 0, tiled=True)  7.28 us
    ppermute x6, waiting for transfers between devices, shifted(): lax.ppermute(x, 'sec', [(i, (i + by) % peers) for i in range(peers) if wr...  6.81 us
    all_to_all x1, waiting for transfers between devices, one_round(): sums = lax.all_to_all(sums, 'sec', 0, 0, tiled=True)  3.87 us
  transfers between devices with their start and end apart: 40, of which 17 were waited for; matrix products, arithmetic and copies ran while one was open for 0% of the time, Pallas kernels for 2%

profile of v5, /device:TPU:32, one launch (start us, length us, event | category | flops | bytes accessed | tf_op | source)
XLA Modules:
  0.0 93.4 jit_solution(7218914949441414481)
XLA Ops:
  0.6 0.6 shard_map.113
  1.3 92.1 %while.16 = (s32[1]{0:T(128)}, f32[1]{0:T(128)}, f32[64,128]{1,0:T(8,128)}, f32[64,128]{1,0:T(8,128)}, s32[1,1]{1,0:T(1,128)}, /*index=5*/s32[1,1]{1,0:T(1,128)}...) while((s32[1]{0:T(128)}, f32[1]{0:T(128)}, ...), condition=%wide.region_1.2_spmd, body=%wide.region_0.1_spmd.sunk | while | flops 20000000000 | bytes 25815560 | solution.py:290
  1.3 0.9 body.42
  2.2 3.0 %collective-permute-start.3 = (f32[64,128]{1,0:T(8,128)S(1)}, f32[64,128]{1,0:T(8,128)S(1)}, u32[]{:S(2)}, u32[]{:S(2)}) collective-permute-start(f32[64,128]{1,0:T(8,128)S(1)} %get-tuple-element.344.refs_0_.refs_5_), channel_id=1, source_target_pairs={{0,6},{1,7},{2,4},{3,5},{4,2},{5,3},{6,0},{7,1},{8,14},{9,15},{10,... | collective-permute-start | bytes 98312 | tf_op jit(solution)/shard_map/while/body/ppermute | solution.py:220
  5.2 0.6 collective-permute-start.2
  5.9 0.5 collective-permute-start.1
  6.3 1.9 %collective-permute-start = (f32[64,128]{1,0:T(8,128)S(1)}, f32[64,128]{1,0:T(8,128)S(1)}, u32[]{:S(2)}, u32[]{:S(2)}) collective-permute-start(f32[64,128]{1,0:T(8,128)S(1)} %get-tuple-element.344.refs_0_.refs_5_), channel_id=1, source_target_pairs={{0,8},{8,16},{16,24},{24,32},{32,40},{40,48},{48,56},{56,64},{64,7... | collective-permute-start | bytes 98312 | tf_op jit(solution)/shard_map/while/body/ppermute | solution.py:225
  8.5 2.2 %collective-permute-done.2.refs_2_ = f32[64,128]{1,0:T(8,128)S(1)} collective-permute-done((f32[64,128]{1,0:T(8,128)S(1)}, f32[64,128]{1,0:T(8,128)S(1)}, u32[]{:S(2)}, u32[]{:S(2)}) %collective-permute-start.2) | collective-permute-done | bytes 32800 | tf_op jit(solution)/shard_map/while/body/ppermute | solution.py:220
  10.7 0.5 collective-permute-start.5
  11.2 1.5 %body.43 = (bf16[512,96]{1,0:T(8,128)(2,1)S(1)}, bf16[128,48]{1,0:T(8,128)(2,1)S(1)}) custom-call(s32[1]{0:T(128)} %bitcast.16.section, s32[1]{0:T(128)} %bitcast.17.tile, s32[1]{0:T(128)} %bitcast.18.count, s32[1]{0:T(128)} %bitcast.19.count_ex, s32[1,1,96]{2,1,0:T(1,128)S(1)} %copy-done.3, s32[1,1,96]{2,1,0:T(1,128)S(1)} %copy-done.4, ...), custom_call_target="tpu_custom_call" | custom-call | tf_op jit(solution)/shard_map/while/body/pallas_call | solution.py:208
  12.8 2.7 %body.44 = (f32[256,128]{1,0:T(8,128)S(1)}, f32[256,128]{1,0:T(8,128)S(1)}, f32[64,128]{1,0:T(8,128)S(1)}, f32[8,128]{1,0:T(8,128)S(1)}) custom-call(bf16[512,96]{1,0:T(8,128)(2,1)S(1)} %get-tuple-element.342.hot_in, bf16[128,48]{1,0:T(8,128)(2,1)S(1)} %get-tuple-element.343.hot_ex, f32[1,128]{1,0:T(1,128)S(1)} %get-tuple-element.341.refs_4_.scale_ref, ...), custom_call_target="tpu_custom_call" | custom-call | tf_op jit(solution)/shard_map/while/body/pallas_call | solution.py:208
  15.6 3.9 %collective-permute-start.12 = (f32[64,128]{1,0:T(8,128)S(1)}, f32[64,128]{1,0:T(8,128)S(1)}, u32[]{:S(2)}, u32[]{:S(2)}) collective-permute-start(f32[64,128]{1,0:T(8,128)S(1)} %get-tuple-element.352), channel_id=1, source_target_pairs={{0,248},{8,0},{16,8},{24,16},{32,24},{40,32},{48,40},{56,48},{64,5... | collective-permute-start | bytes 98312 | tf_op jit(solution)/shard_map/while/body/ppermute | solution.py:225
  19.5 1.7 %collective-permute-start.9 = (f32[64,128]{1,0:T(8,128)S(1)}, f32[64,128]{1,0:T(8,128)S(1)}, u32[]{:S(2)}, u32[]{:S(2)}) collective-permute-start(f32[64,128]{1,0:T(8,128)S(1)} %get-tuple-element.349), channel_id=1, source_target_pairs={{0,2},{1,3},{2,0},{3,1},{4,6},{5,7},{6,4},{7,5},{8,10},{9,11},{10,... | collective-permute-start | bytes 98312 | tf_op jit(solution)/shard_map/while/body/ppermute | solution.py:220
  21.2 2.9 %collective-permute-start.10 = (f32[64,128]{1,0:T(8,128)S(1)}, f32[64,128]{1,0:T(8,128)S(1)}, u32[]{:S(2)}, u32[]{:S(2)}) collective-permute-start(f32[64,128]{1,0:T(8,128)S(1)} %get-tuple-element.350), channel_id=1, source_target_pairs={{0,4},{1,5},{2,6},{3,7},{4,0},{5,1},{6,2},{7,3},{8,12},{9,13},{10,... | collective-permute-start | bytes 98312 | tf_op jit(solution)/shard_map/while/body/ppermute | solution.py:220
  24.3 2.3 %collective-permute-done.10.refs_2_ = f32[64,128]{1,0:T(8,128)S(1)} collective-permute-done((f32[64,128]{1,0:T(8,128)S(1)}, f32[64,128]{1,0:T(8,128)S(1)}, u32[]{:S(2)}, u32[]{:S(2)}) %collective-permute-start.10) | collective-permute-done | bytes 32800 | tf_op jit(solution)/shard_map/while/body/ppermute | solution.py:220
  26.6 2.6 %collective-permute-done.11.refs_3_ = f32[64,128]{1,0:T(8,128)S(1)} collective-permute-done((f32[64,128]{1,0:T(8,128)S(1)}, f32[64,128]{1,0:T(8,128)S(1)}, u32[]{:S(2)}, u32[]{:S(2)}) %collective-permute-start.11) | collective-permute-done | bytes 32800 | tf_op jit(solution)/shard_map/while/body/ppermute | solution.py:220
  29.5 0.8 collective-permute-start.15
  30.3 3.1 %collective-permute-start.14 = (f32[64,128]{1,0:T(8,128)S(1)}, f32[64,128]{1,0:T(8,128)S(1)}, u32[]{:S(2)}, u32[]{:S(2)}) collective-permute-start(f32[64,128]{1,0:T(8,128)S(1)} %body.46.refs_0_.refs_6_), channel_id=1, source_target_pairs={{0,2},{1,3},{2,0},{3,1},{4,6},{5,7},{6,4},{7,5},{8,10},{9,11},{10,... | collective-permute-start | bytes 98312 | tf_op jit(solution)/shard_map/while/body/ppermute | solution.py:220
  33.4 1.0 %collective-permute-done.16.refs_3_ = f32[64,128]{1,0:T(8,128)S(1)} collective-permute-done((f32[64,128]{1,0:T(8,128)S(1)}, f32[64,128]{1,0:T(8,128)S(1)}, u32[]{:S(2)}, u32[]{:S(2)}) %collective-permute-start.16) | collective-permute-done | bytes 32800 | tf_op jit(solution)/shard_map/while/body/ppermute | solution.py:220
  34.4 0.5 collective-permute-done.15.refs_2_
  35.0 0.7 collective-permute-done.14.refs_1_
  35.7 2.4 %collective-permute-done.13.before_ref = f32[64,128]{1,0:T(8,128)S(1)} collective-permute-done((f32[64,128]{1,0:T(8,128)S(1)}, f32[64,128]{1,0:T(8,128)S(1)}, u32[]{:S(2)}, u32[]{:S(2)}) %collective-permute-start.13) | collective-permute-done | bytes 32800 | tf_op jit(solution)/shard_map/while/body/ppermute | solution.py:225
  38.1 1.3 %body.47 = (f32[256,128]{1,0:T(8,128)S(1)}, f32[256,128]{1,0:T(8,128)S(1)}, f32[64,128]{1,0:T(8,128)S(1)}, f32[8,128]{1,0:T(8,128)S(1)}) custom-call(bf16[512,96]{1,0:T(8,128)(2,1)S(1)} %get-tuple-element.342.hot_in, bf16[128,48]{1,0:T(8,128)(2,1)S(1)} %get-tuple-element.343.hot_ex, f32[1,128]{1,0:T(1,128)S(1)} %get-tuple-element.341.refs_4_.scale_ref, ...), custom_call_target="tpu_custom_call" | custom-call | tf_op jit(solution)/shard_map/while/body/pallas_call | solution.py:208
  39.5 5.3 %collective-permute-start.25 = (f32[64,128]{1,0:T(8,128)S(1)}, f32[64,128]{1,0:T(8,128)S(1)}, u32[]{:S(2)}, u32[]{:S(2)}) collective-permute-start(f32[64,128]{1,0:T(8,128)S(1)} %get-tuple-element.360), channel_id=1, source_target_pairs={{0,248},{8,0},{16,8},{24,16},{32,24},{40,32},{48,40},{56,48},{64,5... | collective-permute-start | bytes 98312 | tf_op jit(solution)/shard_map/while/body/ppermute | solution.py:225
  44.9 3.5 %collective-permute-start.23 = (f32[64,128]{1,0:T(8,128)S(1)}, f32[64,128]{1,0:T(8,128)S(1)}, u32[]{:S(2)}, u32[]{:S(2)}) collective-permute-start(f32[64,128]{1,0:T(8,128)S(1)} %get-tuple-element.358), channel_id=1, source_target_pairs={{0,4},{1,5},{2,6},{3,7},{4,0},{5,1},{6,2},{7,3},{8,12},{9,13},{10,... | collective-permute-start | bytes 98312 | tf_op jit(solution)/shard_map/while/body/ppermute | solution.py:220
  48.4 1.2 %collective-permute-start.24 = (f32[64,128]{1,0:T(8,128)S(1)}, f32[64,128]{1,0:T(8,128)S(1)}, u32[]{:S(2)}, u32[]{:S(2)}) collective-permute-start(f32[64,128]{1,0:T(8,128)S(1)} %get-tuple-element.359), channel_id=1, source_target_pairs={{0,6},{1,7},{2,4},{3,5},{4,2},{5,3},{6,0},{7,1},{8,14},{9,15},{10,... | collective-permute-start | bytes 98312 | tf_op jit(solution)/shard_map/while/body/ppermute | solution.py:220
  49.6 1.0 %collective-permute-done.23.refs_2_ = f32[64,128]{1,0:T(8,128)S(1)} collective-permute-done((f32[64,128]{1,0:T(8,128)S(1)}, f32[64,128]{1,0:T(8,128)S(1)}, u32[]{:S(2)}, u32[]{:S(2)}) %collective-permute-start.23) | collective-permute-done | bytes 32800 | tf_op jit(solution)/shard_map/while/body/ppermute | solution.py:220
  50.6 2.9 %collective-permute-done.24.refs_3_ = f32[64,128]{1,0:T(8,128)S(1)} collective-permute-done((f32[64,128]{1,0:T(8,128)S(1)}, f32[64,128]{1,0:T(8,128)S(1)}, u32[]{:S(2)}, u32[]{:S(2)}) %collective-permute-start.24) | collective-permute-done | bytes 32800 | tf_op jit(solution)/shard_map/while/body/ppermute | solution.py:220
  53.5 1.3 %collective-permute-start.29 = (f32[64,128]{1,0:T(8,128)S(1)}, f32[64,128]{1,0:T(8,128)S(1)}, u32[]{:S(2)}, u32[]{:S(2)}) collective-permute-start(f32[64,128]{1,0:T(8,128)S(1)} %body.49.refs_0_.refs_7_), channel_id=1, source_target_pairs={{0,6},{1,7},{2,4},{3,5},{4,2},{5,3},{6,0},{7,1},{8,14},{9,15},{10,... | collective-permute-start | bytes 98312 | tf_op jit(solution)/shard_map/while/body/ppermute | solution.py:220
  54.8 2.9 %collective-permute-start.27 = (f32[64,128]{1,0:T(8,128)S(1)}, f32[64,128]{1,0:T(8,128)S(1)}, u32[]{:S(2)}, u32[]{:S(2)}) collective-permute-start(f32[64,128]{1,0:T(8,128)S(1)} %body.49.refs_0_.refs_7_), channel_id=1, source_target_pairs={{0,2},{1,3},{2,0},{3,1},{4,6},{5,7},{6,4},{7,5},{8,10},{9,11},{10,... | collective-permute-start | bytes 98312 | tf_op jit(solution)/shard_map/while/body/ppermute | solution.py:220
  57.7 1.0 %collective-permute-done.29.refs_3_ = f32[64,128]{1,0:T(8,128)S(1)} collective-permute-done((f32[64,128]{1,0:T(8,128)S(1)}, f32[64,128]{1,0:T(8,128)S(1)}, u32[]{:S(2)}, u32[]{:S(2)}) %collective-permute-start.29) | collective-permute-done | bytes 32800 | tf_op jit(solution)/shard_map/while/body/ppermute | solution.py:220
  58.7 1.5 %collective-permute-done.28.refs_2_ = f32[64,128]{1,0:T(8,128)S(1)} collective-permute-done((f32[64,128]{1,0:T(8,128)S(1)}, f32[64,128]{1,0:T(8,128)S(1)}, u32[]{:S(2)}, u32[]{:S(2)}) %collective-permute-start.28) | collective-permute-done | bytes 32800 | tf_op jit(solution)/shard_map/while/body/ppermute | solution.py:220
  60.2 0.5 collective-permute-start.31
  60.7 0.9 collective-permute-done.26.before_ref
  61.6 1.8 %body.50 = (f32[288,128]{1,0:T(8,128)S(1)}, f32[288,128]{1,0:T(8,128)S(1)}, f32[64,128]{1,0:T(8,128)S(1)}, f32[8,128]{1,0:T(8,128)}) custom-call(bf16[512,96]{1,0:T(8,128)(2,1)S(1)} %get-tuple-element.342.hot_in, bf16[128,48]{1,0:T(8,128)(2,1)S(1)} %get-tuple-element.343.hot_ex, f32[1,128]{1,0:T(1,128)S(1)} %get-tuple-element.341.refs_4_.scale_ref, ...), custom_call_target="tpu_custom_call" | custom-call | tf_op jit(solution)/shard_map/while/body/pallas_call | solution.py:208
  63.4 0.3 collective-permute-start.34
  63.7 1.0 %collective-permute-done.34.got_ref = f32[288,128]{1,0:T(8,128)S(1)} collective-permute-done((f32[288,128]{1,0:T(8,128)S(1)}, f32[288,128]{1,0:T(8,128)S(1)}, u32[]{:S(2)}, u32[]{:S(2)}) %collective-permute-start.34) | collective-permute-done | bytes 147488 | tf_op jit(solution)/shard_map/while/body/ppermute | solution.py:220
  64.8 1.3 %collective-permute-start.35 = (f32[72,128]{1,0:T(8,128)S(1)}, f32[72,128]{1,0:T(8,128)S(1)}, u32[]{:S(2)}, u32[]{:S(2)}) collective-permute-start(f32[72,128]{1,0:T(8,128)S(1)} %get-tuple-element.364), channel_id=1, source_target_pairs={{0,2},{1,3},{2,0},{3,1},{4,6},{5,7},{6,4},{7,5},{8,10},{9,11},{10,... | collective-permute-start | bytes 110600 | tf_op jit(solution)/shard_map/while/body/ppermute | solution.py:220
  66.1 2.3 %collective-permute-start.36 = (f32[72,128]{1,0:T(8,128)S(1)}, f32[72,128]{1,0:T(8,128)S(1)}, u32[]{:S(2)}, u32[]{:S(2)}) collective-permute-start(f32[72,128]{1,0:T(8,128)S(1)} %get-tuple-element.365), channel_id=1, source_target_pairs={{0,4},{1,5},{2,6},{3,7},{4,0},{5,1},{6,2},{7,3},{8,12},{9,13},{10,... | collective-permute-start | bytes 110600 | tf_op jit(solution)/shard_map/while/body/ppermute | solution.py:220
  68.4 1.2 %collective-permute-start.37 = (f32[72,128]{1,0:T(8,128)S(1)}, f32[72,128]{1,0:T(8,128)S(1)}, u32[]{:S(2)}, u32[]{:S(2)}) collective-permute-start(f32[72,128]{1,0:T(8,128)S(1)} %get-tuple-element.366), channel_id=1, source_target_pairs={{0,6},{1,7},{2,4},{3,5},{4,2},{5,3},{6,0},{7,1},{8,14},{9,15},{10,... | collective-permute-start | bytes 110600 | tf_op jit(solution)/shard_map/while/body/ppermute | solution.py:220
  69.6 1.9 %collective-permute-done.36.refs_2_ = f32[72,128]{1,0:T(8,128)S(1)} collective-permute-done((f32[72,128]{1,0:T(8,128)S(1)}, f32[72,128]{1,0:T(8,128)S(1)}, u32[]{:S(2)}, u32[]{:S(2)}) %collective-permute-start.36) | collective-permute-done | bytes 36896 | tf_op jit(solution)/shard_map/while/body/ppermute | solution.py:220
  71.5 2.0 %collective-permute-done.37.refs_3_ = f32[72,128]{1,0:T(8,128)S(1)} collective-permute-done((f32[72,128]{1,0:T(8,128)S(1)}, f32[72,128]{1,0:T(8,128)S(1)}, u32[]{:S(2)}, u32[]{:S(2)}) %collective-permute-start.37) | collective-permute-done | bytes 36896 | tf_op jit(solution)/shard_map/while/body/ppermute | solution.py:220
  73.5 0.7 body.52
  74.2 7.3 %all-to-all-start = ((f32[32,8,128]{2,1,0:T(8,128)}), f32[32,8,128]{2,1,0:T(8,128)S(1)}, u32[]{:S(2)}, u32[]{:S(2)}) async-start(f32[32,8,128]{2,1,0:T(8,128)} %body.52), calls=%async_computation | async-start | bytes 262144 | tf_op jit(solution)/shard_map/while/body/all_to_all | solution.py:274
  81.5 2.3 %collective-permute-start.38 = (f32[64,128]{1,0:T(8,128)S(1)}, f32[64,128]{1,0:T(8,128)S(1)}, u32[]{:S(2)}, u32[]{:S(2)}) collective-permute-start(f32[64,128]{1,0:T(8,128)S(1)} %get-tuple-element.367), channel_id=1, source_target_pairs={{8,0},{16,8},{24,16},{32,24},{40,32},{48,40},{56,48},{64,56},{72,6... | collective-permute-start | bytes 98312 | tf_op jit(solution)/shard_map/while/body/ppermute | solution.py:225
  83.8 3.5 %collective-permute-done.38.refs_4_ = f32[64,128]{1,0:T(8,128)S(1)} collective-permute-done((f32[64,128]{1,0:T(8,128)S(1)}, f32[64,128]{1,0:T(8,128)S(1)}, u32[]{:S(2)}, u32[]{:S(2)}) %collective-permute-start.38) | collective-permute-done | bytes 32800 | tf_op jit(solution)/shard_map/while/body/ppermute | solution.py:225
  87.3 3.9 %all-to-all-done.sums_ref = f32[32,8,128]{2,1,0:T(8,128)S(1)} async-done(((f32[32,8,128]{2,1,0:T(8,128)}), f32[32,8,128]{2,1,0:T(8,128)S(1)}, u32[]{:S(2)}, u32[]{:S(2)}) %all-to-all-start) | async-done | bytes 131104 | tf_op jit(solution)/shard_map/while/body/all_to_all | solution.py:274
  91.2 0.9 body.53
  (61 shorter events, 1.3 us)
Async XLA Ops:
  1.3 9.9 %copy-start.3 = (s32[1,1,96]{2,1,0:T(1,128)S(1)}, s32[1,1,96]{2,1,0:T(1,128)}, u32[]{:S(2)}) copy-start(s32[1,1,96]{2,1,0:T(1,128)} %get-tuple-element.419.refs_0_) | copy-start | bytes 1156 | tf_op jit(solution)/shard_map/while
  1.3 9.9 %copy-start.4 = (s32[1,1,96]{2,1,0:T(1,128)S(1)}, s32[1,1,96]{2,1,0:T(1,128)}, u32[]{:S(2)}) copy-start(s32[1,1,96]{2,1,0:T(1,128)} %get-tuple-element.420.refs_1_) | copy-start | bytes 1156 | tf_op jit(solution)/shard_map/while
  1.3 9.9 %copy-start.5 = (s32[1,1,48]{2,1,0:T(1,128)S(1)}, s32[1,1,48]{2,1,0:T(1,128)}, u32[]{:S(2)}) copy-start(s32[1,1,48]{2,1,0:T(1,128)} %get-tuple-element.421.refs_2_) | copy-start | bytes 580 | tf_op jit(solution)/shard_map/while
  1.3 9.9 %copy-start.6 = (s32[1,1,48]{2,1,0:T(1,128)S(1)}, s32[1,1,48]{2,1,0:T(1,128)}, u32[]{:S(2)}) copy-start(s32[1,1,48]{2,1,0:T(1,128)} %get-tuple-element.422.refs_3_) | copy-start | bytes 580 | tf_op jit(solution)/shard_map/while
  1.3 11.5 %copy-start = (bf16[1,1,96,128,128]{4,3,2,1,0:T(8,128)(2,1)S(1)}, bf16[1,1,96,128,128]{4,3,2,1,0:T(8,128)(2,1)}, u32[]{:S(2)}) copy-start(bf16[1,1,96,128,128]{4,3,2,1,0:T(8,128)(2,1)} %get-tuple-element.424.in_ref) | copy-start | bytes 9437188 | tf_op jit(solution)/shard_map/while
  1.3 11.5 %copy-start.2 = (f32[1,1,64,128]{3,2,1,0:T(8,128)S(1)}, f32[1,1,64,128]{3,2,1,0:T(8,128)}, u32[]{:S(2)}) copy-start(f32[1,1,64,128]{3,2,1,0:T(8,128)} %get-tuple-element.423) | copy-start | bytes 98308 | tf_op jit(solution)/shard_map/while
  2.2 6.0 %collective-permute-start.3 = (f32[64,128]{1,0:T(8,128)S(1)}, f32[64,128]{1,0:T(8,128)S(1)}, u32[]{:S(2)}, u32[]{:S(2)}) collective-permute-start(f32[64,128]{1,0:T(8,128)S(1)} %get-tuple-element.344.refs_0_.refs_5_), channel_id=1, source_target_pairs={{0,6},{1,7},{2,4},{3,5},{4,2},{5,3},{6,0},{7,1},{8,14},{9,15},{10,... | collective-permute-start | bytes 98312 | tf_op jit(solution)/shard_map/while/body/ppermute | solution.py:220
  5.2 5.4 %collective-permute-start.2 = (f32[64,128]{1,0:T(8,128)S(1)}, f32[64,128]{1,0:T(8,128)S(1)}, u32[]{:S(2)}, u32[]{:S(2)}) collective-permute-start(f32[64,128]{1,0:T(8,128)S(1)} %get-tuple-element.344.refs_0_.refs_5_), channel_id=1, source_target_pairs={{0,4},{1,5},{2,6},{3,7},{4,0},{5,1},{6,2},{7,3},{8,12},{9,13},{10,... | collective-permute-start | bytes 98312 | tf_op jit(solution)/shard_map/while/body/ppermute | solution.py:220
  5.9 4.8 %collective-permute-start.1 = (f32[64,128]{1,0:T(8,128)S(1)}, f32[64,128]{1,0:T(8,128)S(1)}, u32[]{:S(2)}, u32[]{:S(2)}) collective-permute-start(f32[64,128]{1,0:T(8,128)S(1)} %get-tuple-element.344.refs_0_.refs_5_), channel_id=1, source_target_pairs={{0,2},{1,3},{2,0},{3,1},{4,6},{5,7},{6,4},{7,5},{8,10},{9,11},{10,... | collective-permute-start | bytes 98312 | tf_op jit(solution)/shard_map/while/body/ppermute | solution.py:220
  6.3 6.4 %collective-permute-start.4 = (f32[64,128]{1,0:T(8,128)S(1)}, f32[64,128]{1,0:T(8,128)S(1)}, u32[]{:S(2)}, u32[]{:S(2)}) collective-permute-start(f32[64,128]{1,0:T(8,128)S(1)} %get-tuple-element.344.refs_0_.refs_5_), channel_id=1, source_target_pairs={{0,1},{1,0},{2,3},{3,2},{4,5},{5,4},{6,7},{7,6},{8,9},{9,8},{10,11... | collective-permute-start | bytes 98312 | tf_op jit(solution)/shard_map/while/body/ppermute | solution.py:220
  6.3 6.4 %collective-permute-start = (f32[64,128]{1,0:T(8,128)S(1)}, f32[64,128]{1,0:T(8,128)S(1)}, u32[]{:S(2)}, u32[]{:S(2)}) collective-permute-start(f32[64,128]{1,0:T(8,128)S(1)} %get-tuple-element.344.refs_0_.refs_5_), channel_id=1, source_target_pairs={{0,8},{8,16},{16,24},{24,32},{32,40},{40,48},{48,56},{56,64},{64,7... | collective-permute-start | bytes 98312 | tf_op jit(solution)/shard_map/while/body/ppermute | solution.py:225
  8.2 4.5 %collective-permute-start.7 = (f32[64,128]{1,0:T(8,128)S(1)}, f32[64,128]{1,0:T(8,128)S(1)}, u32[]{:S(2)}, u32[]{:S(2)}) collective-permute-start(f32[64,128]{1,0:T(8,128)S(1)} %collective-permute-done.3.refs_3_), channel_id=1, source_target_pairs={{0,1},{1,0},{2,3},{3,2},{4,5},{5,4},{6,7},{7,6},{8,9},{9,8},{10,11... | collective-permute-start | bytes 98312 | tf_op jit(solution)/shard_map/while/body/ppermute | solution.py:220
  10.6 2.1 %collective-permute-start.6 = (f32[64,128]{1,0:T(8,128)S(1)}, f32[64,128]{1,0:T(8,128)S(1)}, u32[]{:S(2)}, u32[]{:S(2)}) collective-permute-start(f32[64,128]{1,0:T(8,128)S(1)} %collective-permute-done.2.refs_2_), channel_id=1, source_target_pairs={{0,1},{1,0},{2,3},{3,2},{4,5},{5,4},{6,7},{7,6},{8,9},{9,8},{10,11... | collective-permute-start | bytes 98312 | tf_op jit(solution)/shard_map/while/body/ppermute | solution.py:220
  10.7 2.1 %collective-permute-start.5 = (f32[64,128]{1,0:T(8,128)S(1)}, f32[64,128]{1,0:T(8,128)S(1)}, u32[]{:S(2)}, u32[]{:S(2)}) collective-permute-start(f32[64,128]{1,0:T(8,128)S(1)} %collective-permute-done.1.refs_1_), channel_id=1, source_target_pairs={{0,1},{1,0},{2,3},{3,2},{4,5},{5,4},{6,7},{7,6},{8,9},{9,8},{10,11... | collective-permute-start | bytes 98312 | tf_op jit(solution)/shard_map/while/body/ppermute | solution.py:220
  11.2 26.9 %copy-start.1 = (bf16[1,1,48,128,128]{4,3,2,1,0:T(8,128)(2,1)S(1)}, bf16[1,1,48,128,128]{4,3,2,1,0:T(8,128)(2,1)}, u32[]{:S(2)}) copy-start(bf16[1,1,48,128,128]{4,3,2,1,0:T(8,128)(2,1)} %get-tuple-element.425.ex_ref) | copy-start | bytes 4718596 | tf_op jit(solution)/shard_map/while
  15.5 4.0 %collective-permute-start.8 = (f32[256,128]{1,0:T(8,128)S(1)}, f32[256,128]{1,0:T(8,128)S(1)}, u32[]{:S(2)}, u32[]{:S(2)}) collective-permute-start(f32[256,128]{1,0:T(8,128)S(1)} %get-tuple-element.347), channel_id=1, source_target_pairs={{0,1},{1,0},{2,3},{3,2},{4,5},{5,4},{6,7},{7,6},{8,9},{9,8},{10,11... | collective-permute-start | bytes 393224 | tf_op jit(solution)/shard_map/while/body/ppermute | solution.py:220
  15.6 8.7 %collective-permute-start.12 = (f32[64,128]{1,0:T(8,128)S(1)}, f32[64,128]{1,0:T(8,128)S(1)}, u32[]{:S(2)}, u32[]{:S(2)}) collective-permute-start(f32[64,128]{1,0:T(8,128)S(1)} %get-tuple-element.352), channel_id=1, source_target_pairs={{0,248},{8,0},{16,8},{24,16},{32,24},{40,32},{48,40},{56,48},{64,5... | collective-permute-start | bytes 98312 | tf_op jit(solution)/shard_map/while/body/ppermute | solution.py:225
  19.5 4.8 %collective-permute-start.9 = (f32[64,128]{1,0:T(8,128)S(1)}, f32[64,128]{1,0:T(8,128)S(1)}, u32[]{:S(2)}, u32[]{:S(2)}) collective-permute-start(f32[64,128]{1,0:T(8,128)S(1)} %get-tuple-element.349), channel_id=1, source_target_pairs={{0,2},{1,3},{2,0},{3,1},{4,6},{5,7},{6,4},{7,5},{8,10},{9,11},{10,... | collective-permute-start | bytes 98312 | tf_op jit(solution)/shard_map/while/body/ppermute | solution.py:220
  21.2 5.4 %collective-permute-start.10 = (f32[64,128]{1,0:T(8,128)S(1)}, f32[64,128]{1,0:T(8,128)S(1)}, u32[]{:S(2)}, u32[]{:S(2)}) collective-permute-start(f32[64,128]{1,0:T(8,128)S(1)} %get-tuple-element.350), channel_id=1, source_target_pairs={{0,4},{1,5},{2,6},{3,7},{4,0},{5,1},{6,2},{7,3},{8,12},{9,13},{10,... | collective-permute-start | bytes 98312 | tf_op jit(solution)/shard_map/while/body/ppermute | solution.py:220
  24.1 5.1 %collective-permute-start.11 = (f32[64,128]{1,0:T(8,128)S(1)}, f32[64,128]{1,0:T(8,128)S(1)}, u32[]{:S(2)}, u32[]{:S(2)}) collective-permute-start(f32[64,128]{1,0:T(8,128)S(1)} %get-tuple-element.351), channel_id=1, source_target_pairs={{0,6},{1,7},{2,4},{3,5},{4,2},{5,3},{6,0},{7,1},{8,14},{9,15},{10,... | collective-permute-start | bytes 98312 | tf_op jit(solution)/shard_map/while/body/ppermute | solution.py:220
  29.2 5.2 %collective-permute-start.16 = (f32[64,128]{1,0:T(8,128)S(1)}, f32[64,128]{1,0:T(8,128)S(1)}, u32[]{:S(2)}, u32[]{:S(2)}) collective-permute-start(f32[64,128]{1,0:T(8,128)S(1)} %body.46.refs_0_.refs_6_), channel_id=1, source_target_pairs={{0,6},{1,7},{2,4},{3,5},{4,2},{5,3},{6,0},{7,1},{8,14},{9,15},{10,... | collective-permute-start | bytes 98312 | tf_op jit(solution)/shard_map/while/body/ppermute | solution.py:220
  29.5 5.4 %collective-permute-start.15 = (f32[64,128]{1,0:T(8,128)S(1)}, f32[64,128]{1,0:T(8,128)S(1)}, u32[]{:S(2)}, u32[]{:S(2)}) collective-permute-start(f32[64,128]{1,0:T(8,128)S(1)} %body.46.refs_0_.refs_6_), channel_id=1, source_target_pairs={{0,4},{1,5},{2,6},{3,7},{4,0},{5,1},{6,2},{7,3},{8,12},{9,13},{10,... | collective-permute-start | bytes 98312 | tf_op jit(solution)/shard_map/while/body/ppermute | solution.py:220
  30.3 5.3 %collective-permute-start.14 = (f32[64,128]{1,0:T(8,128)S(1)}, f32[64,128]{1,0:T(8,128)S(1)}, u32[]{:S(2)}, u32[]{:S(2)}) collective-permute-start(f32[64,128]{1,0:T(8,128)S(1)} %body.46.refs_0_.refs_6_), channel_id=1, source_target_pairs={{0,2},{1,3},{2,0},{3,1},{4,6},{5,7},{6,4},{7,5},{8,10},{9,11},{10,... | collective-permute-start | bytes 98312 | tf_op jit(solution)/shard_map/while/body/ppermute | solution.py:220
  33.4 2.2 %collective-permute-start.17 = (f32[64,128]{1,0:T(8,128)S(1)}, f32[64,128]{1,0:T(8,128)S(1)}, u32[]{:S(2)}, u32[]{:S(2)}) collective-permute-start(f32[64,128]{1,0:T(8,128)S(1)} %body.46.refs_0_.refs_6_), channel_id=1, source_target_pairs={{0,1},{1,0},{2,3},{3,2},{4,5},{5,4},{6,7},{7,6},{8,9},{9,8},{10,11... | collective-permute-start | bytes 98312 | tf_op jit(solution)/shard_map/while/body/ppermute | solution.py:220
  33.4 4.6 %collective-permute-start.13 = (f32[64,128]{1,0:T(8,128)S(1)}, f32[64,128]{1,0:T(8,128)S(1)}, u32[]{:S(2)}, u32[]{:S(2)}) collective-permute-start(f32[64,128]{1,0:T(8,128)S(1)} %body.46.refs_0_.refs_6_), channel_id=1, source_target_pairs={{0,8},{8,16},{16,24},{24,32},{32,40},{40,48},{48,56},{56,64},{64,7... | collective-permute-start | bytes 98312 | tf_op jit(solution)/shard_map/while/body/ppermute | solution.py:225
  34.4 3.6 %collective-permute-start.20 = (f32[64,128]{1,0:T(8,128)S(1)}, f32[64,128]{1,0:T(8,128)S(1)}, u32[]{:S(2)}, u32[]{:S(2)}) collective-permute-start(f32[64,128]{1,0:T(8,128)S(1)} %collective-permute-done.16.refs_3_), channel_id=1, source_target_pairs={{0,1},{1,0},{2,3},{3,2},{4,5},{5,4},{6,7},{7,6},{8,9},{9,8},{10,11... | collective-permute-start | bytes 98312 | tf_op jit(solution)/shard_map/while/body/ppermute | solution.py:220
  35.0 3.1 %collective-permute-start.19 = (f32[64,128]{1,0:T(8,128)S(1)}, f32[64,128]{1,0:T(8,128)S(1)}, u32[]{:S(2)}, u32[]{:S(2)}) collective-permute-start(f32[64,128]{1,0:T(8,128)S(1)} %collective-permute-done.15.refs_2_), channel_id=1, source_target_pairs={{0,1},{1,0},{2,3},{3,2},{4,5},{5,4},{6,7},{7,6},{8,9},{9,8},{10,11... | collective-permute-start | bytes 98312 | tf_op jit(solution)/shard_map/while/body/ppermute | solution.py:220
  35.6 2.4 %collective-permute-start.18 = (f32[64,128]{1,0:T(8,128)S(1)}, f32[64,128]{1,0:T(8,128)S(1)}, u32[]{:S(2)}, u32[]{:S(2)}) collective-permute-start(f32[64,128]{1,0:T(8,128)S(1)} %collective-permute-done.14.refs_1_), channel_id=1, source_target_pairs={{0,1},{1,0},{2,3},{3,2},{4,5},{5,4},{6,7},{7,6},{8,9},{9,8},{10,11... | collective-permute-start | bytes 98312 | tf_op jit(solution)/shard_map/while/body/ppermute | solution.py:220
  39.4 5.4 %collective-permute-start.21 = (f32[256,128]{1,0:T(8,128)S(1)}, f32[256,128]{1,0:T(8,128)S(1)}, u32[]{:S(2)}, u32[]{:S(2)}) collective-permute-start(f32[256,128]{1,0:T(8,128)S(1)} %get-tuple-element.355), channel_id=1, source_target_pairs={{0,1},{1,0},{2,3},{3,2},{4,5},{5,4},{6,7},{7,6},{8,9},{9,8},{10,11... | collective-permute-start | bytes 393224 | tf_op jit(solution)/shard_map/while/body/ppermute | solution.py:220
  39.5 10.1 %collective-permute-start.25 = (f32[64,128]{1,0:T(8,128)S(1)}, f32[64,128]{1,0:T(8,128)S(1)}, u32[]{:S(2)}, u32[]{:S(2)}) collective-permute-start(f32[64,128]{1,0:T(8,128)S(1)} %get-tuple-element.360), channel_id=1, source_target_pairs={{0,248},{8,0},{16,8},{24,16},{32,24},{40,32},{48,40},{56,48},{64,5... | collective-permute-start | bytes 98312 | tf_op jit(solution)/shard_map/while/body/ppermute | solution.py:225
  44.8 4.8 %collective-permute-start.22 = (f32[64,128]{1,0:T(8,128)S(1)}, f32[64,128]{1,0:T(8,128)S(1)}, u32[]{:S(2)}, u32[]{:S(2)}) collective-permute-start(f32[64,128]{1,0:T(8,128)S(1)} %get-tuple-element.357), channel_id=1, source_target_pairs={{0,2},{1,3},{2,0},{3,1},{4,6},{5,7},{6,4},{7,5},{8,10},{9,11},{10,... | collective-permute-start | bytes 98312 | tf_op jit(solution)/shard_map/while/body/ppermute | solution.py:220
  44.9 5.7 %collective-permute-start.23 = (f32[64,128]{1,0:T(8,128)S(1)}, f32[64,128]{1,0:T(8,128)S(1)}, u32[]{:S(2)}, u32[]{:S(2)}) collective-permute-start(f32[64,128]{1,0:T(8,128)S(1)} %get-tuple-element.358), channel_id=1, source_target_pairs={{0,4},{1,5},{2,6},{3,7},{4,0},{5,1},{6,2},{7,3},{8,12},{9,13},{10,... | collective-permute-start | bytes 98312 | tf_op jit(solution)/shard_map/while/body/ppermute | solution.py:220
  48.4 5.1 %collective-permute-start.24 = (f32[64,128]{1,0:T(8,128)S(1)}, f32[64,128]{1,0:T(8,128)S(1)}, u32[]{:S(2)}, u32[]{:S(2)}) collective-permute-start(f32[64,128]{1,0:T(8,128)S(1)} %get-tuple-element.359), channel_id=1, source_target_pairs={{0,6},{1,7},{2,4},{3,5},{4,2},{5,3},{6,0},{7,1},{8,14},{9,15},{10,... | collective-permute-start | bytes 98312 | tf_op jit(solution)/shard_map/while/body/ppermute | solution.py:220
  53.5 5.2 %collective-permute-start.29 = (f32[64,128]{1,0:T(8,128)S(1)}, f32[64,128]{1,0:T(8,128)S(1)}, u32[]{:S(2)}, u32[]{:S(2)}) collective-permute-start(f32[64,128]{1,0:T(8,128)S(1)} %body.49.refs_0_.refs_7_), channel_id=1, source_target_pairs={{0,6},{1,7},{2,4},{3,5},{4,2},{5,3},{6,0},{7,1},{8,14},{9,15},{10,... | collective-permute-start | bytes 98312 | tf_op jit(solution)/shard_map/while/body/ppermute | solution.py:220
  54.8 5.4 %collective-permute-start.28 = (f32[64,128]{1,0:T(8,128)S(1)}, f32[64,128]{1,0:T(8,128)S(1)}, u32[]{:S(2)}, u32[]{:S(2)}) collective-permute-start(f32[64,128]{1,0:T(8,128)S(1)} %body.49.refs_0_.refs_7_), channel_id=1, source_target_pairs={{0,4},{1,5},{2,6},{3,7},{4,0},{5,1},{6,2},{7,3},{8,12},{9,13},{10,... | collective-permute-start | bytes 98312 | tf_op jit(solution)/shard_map/while/body/ppermute | solution.py:220
  54.8 5.4 %collective-permute-start.27 = (f32[64,128]{1,0:T(8,128)S(1)}, f32[64,128]{1,0:T(8,128)S(1)}, u32[]{:S(2)}, u32[]{:S(2)}) collective-permute-start(f32[64,128]{1,0:T(8,128)S(1)} %body.49.refs_0_.refs_7_), channel_id=1, source_target_pairs={{0,2},{1,3},{2,0},{3,1},{4,6},{5,7},{6,4},{7,5},{8,10},{9,11},{10,... | collective-permute-start | bytes 98312 | tf_op jit(solution)/shard_map/while/body/ppermute | solution.py:220
  57.7 3.1 %collective-permute-start.30 = (f32[64,128]{1,0:T(8,128)S(1)}, f32[64,128]{1,0:T(8,128)S(1)}, u32[]{:S(2)}, u32[]{:S(2)}) collective-permute-start(f32[64,128]{1,0:T(8,128)S(1)} %body.49.refs_0_.refs_7_), channel_id=1, source_target_pairs={{0,1},{1,0},{2,3},{3,2},{4,5},{5,4},{6,7},{7,6},{8,9},{9,8},{10,11... | collective-permute-start | bytes 98312 | tf_op jit(solution)/shard_map/while/body/ppermute | solution.py:220
  57.7 3.9 %collective-permute-start.26 = (f32[64,128]{1,0:T(8,128)S(1)}, f32[64,128]{1,0:T(8,128)S(1)}, u32[]{:S(2)}, u32[]{:S(2)}) collective-permute-start(f32[64,128]{1,0:T(8,128)S(1)} %body.49.refs_0_.refs_7_), channel_id=1, source_target_pairs={{0,8},{8,16},{16,24},{24,32},{32,40},{40,48},{48,56},{56,64},{64,7... | collective-permute-start | bytes 98312 | tf_op jit(solution)/shard_map/while/body/ppermute | solution.py:225
  58.7 2.9 %collective-permute-start.33 = (f32[64,128]{1,0:T(8,128)S(1)}, f32[64,128]{1,0:T(8,128)S(1)}, u32[]{:S(2)}, u32[]{:S(2)}) collective-permute-start(f32[64,128]{1,0:T(8,128)S(1)} %collective-permute-done.29.refs_3_), channel_id=1, source_target_pairs={{0,1},{1,0},{2,3},{3,2},{4,5},{5,4},{6,7},{7,6},{8,9},{9,8},{10,11... | collective-permute-start | bytes 98312 | tf_op jit(solution)/shard_map/while/body/ppermute | solution.py:220
  60.2 1.4 %collective-permute-start.32 = (f32[64,128]{1,0:T(8,128)S(1)}, f32[64,128]{1,0:T(8,128)S(1)}, u32[]{:S(2)}, u32[]{:S(2)}) collective-permute-start(f32[64,128]{1,0:T(8,128)S(1)} %collective-permute-done.28.refs_2_), channel_id=1, source_target_pairs={{0,1},{1,0},{2,3},{3,2},{4,5},{5,4},{6,7},{7,6},{8,9},{9,8},{10,11... | collective-permute-start | bytes 98312 | tf_op jit(solution)/shard_map/while/body/ppermute | solution.py:220
  60.2 1.4 %collective-permute-start.31 = (f32[64,128]{1,0:T(8,128)S(1)}, f32[64,128]{1,0:T(8,128)S(1)}, u32[]{:S(2)}, u32[]{:S(2)}) collective-permute-start(f32[64,128]{1,0:T(8,128)S(1)} %collective-permute-done.27.refs_1_), channel_id=1, source_target_pairs={{0,1},{1,0},{2,3},{3,2},{4,5},{5,4},{6,7},{7,6},{8,9},{9,8},{10,11... | collective-permute-start | bytes 98312 | tf_op jit(solution)/shard_map/while/body/ppermute | solution.py:220
  63.4 1.4 %collective-permute-start.34 = (f32[288,128]{1,0:T(8,128)S(1)}, f32[288,128]{1,0:T(8,128)S(1)}, u32[]{:S(2)}, u32[]{:S(2)}) collective-permute-start(f32[288,128]{1,0:T(8,128)S(1)} %get-tuple-element.362), channel_id=1, source_target_pairs={{0,1},{1,0},{2,3},{3,2},{4,5},{5,4},{6,7},{7,6},{8,9},{9,8},{10,11... | collective-permute-start | bytes 442376 | tf_op jit(solution)/shard_map/while/body/ppermute | solution.py:220
  64.8 4.8 %collective-permute-start.35 = (f32[72,128]{1,0:T(8,128)S(1)}, f32[72,128]{1,0:T(8,128)S(1)}, u32[]{:S(2)}, u32[]{:S(2)}) collective-permute-start(f32[72,128]{1,0:T(8,128)S(1)} %get-tuple-element.364), channel_id=1, source_target_pairs={{0,2},{1,3},{2,0},{3,1},{4,6},{5,7},{6,4},{7,5},{8,10},{9,11},{10,... | collective-permute-start | bytes 110600 | tf_op jit(solution)/shard_map/while/body/ppermute | solution.py:220
  66.1 5.5 %collective-permute-start.36 = (f32[72,128]{1,0:T(8,128)S(1)}, f32[72,128]{1,0:T(8,128)S(1)}, u32[]{:S(2)}, u32[]{:S(2)}) collective-permute-start(f32[72,128]{1,0:T(8,128)S(1)} %get-tuple-element.365), channel_id=1, source_target_pairs={{0,4},{1,5},{2,6},{3,7},{4,0},{5,1},{6,2},{7,3},{8,12},{9,13},{10,... | collective-permute-start | bytes 110600 | tf_op jit(solution)/shard_map/while/body/ppermute | solution.py:220
  68.4 5.2 %collective-permute-start.37 = (f32[72,128]{1,0:T(8,128)S(1)}, f32[72,128]{1,0:T(8,128)S(1)}, u32[]{:S(2)}, u32[]{:S(2)}) collective-permute-start(f32[72,128]{1,0:T(8,128)S(1)} %get-tuple-element.366), channel_id=1, source_target_pairs={{0,6},{1,7},{2,4},{3,5},{4,2},{5,3},{6,0},{7,1},{8,14},{9,15},{10,... | collective-permute-start | bytes 110600 | tf_op jit(solution)/shard_map/while/body/ppermute | solution.py:220
  74.2 17.0 %all-to-all-start = ((f32[32,8,128]{2,1,0:T(8,128)}), f32[32,8,128]{2,1,0:T(8,128)S(1)}, u32[]{:S(2)}, u32[]{:S(2)}) async-start(f32[32,8,128]{2,1,0:T(8,128)} %body.52), calls=%async_computation | async-start | bytes 262144 | tf_op jit(solution)/shard_map/while/body/all_to_all | solution.py:274
  81.5 5.8 %collective-permute-start.38 = (f32[64,128]{1,0:T(8,128)S(1)}, f32[64,128]{1,0:T(8,128)S(1)}, u32[]{:S(2)}, u32[]{:S(2)}) collective-permute-start(f32[64,128]{1,0:T(8,128)S(1)} %get-tuple-element.367), channel_id=1, source_target_pairs={{8,0},{16,8},{24,16},{32,24},{40,32},{48,40},{56,48},{64,56},{72,6... | collective-permute-start | bytes 98312 | tf_op jit(solution)/shard_map/while/body/ppermute | solution.py:225
